TPU v7x, 32 devices: a whole 2x2x4 slice. The times are simulated.
32 devices in a mesh: tile: 16 (over z, x, core), mp: 2 (over y).
Axes of the slice: x: 2, y: 2, z: 4, core: 2. Of those that a mesh axis runs over, the one named last changes fastest.
Arguments:
- lo_in: bfloat16 [2, 384, 24, 1024], P(None, 'tile', None, 'mp'), may hold values from -6 to 6
- hi_in: bfloat16 [2, 768, 2, 36864], P(None, 'tile', 'mp'), may hold values from -6 to 6
- image_ids: int32 [2, 384], replicated, may hold values from 0 to 31, never falling along the last dimension, each value on 1 to 24 neighbouring positions
- cn_kernel: bfloat16 [49, 1536], P(None, 'mp'), may hold values from -0.875 to 0.875
- cn_gain: bfloat16 [1536], replicated, may hold values from 0.5 to 1.5
- cn_w1: bfloat16 [1536, 6144], P('tile', 'mp'), may hold values from -0.15625 to 0.15625
- cn_w2: bfloat16 [6144, 1536], P('mp', 'tile'), may hold values from -0.078125 to 0.078125
- cn_scale: bfloat16 [1536], P('mp'), may hold values from 0.29882812 to 1.5
- ad_proj: bfloat16 [1536, 1024], P('tile', 'mp'), may hold values from -0.15625 to 0.15625
- ad_kernel: bfloat16 [9, 1024], P(None, 'mp'), may hold values from -2 to 2
- gate_w1: bfloat16 [1536, 768], P('tile', 'mp'), may hold values from -0.15625 to 0.15625
- gate_w2: bfloat16 [768, 1024], P('mp', 'tile'), may hold values from -0.21875 to 0.21875
- ln1_gain: bfloat16 [1024], replicated, may hold values from 0.5 to 1.5
- qkv: bfloat16 [3, 1024, 1024], P(None, 'tile', 'mp'), may hold values from -0.1875 to 0.1875
- out_proj: bfloat16 [1024, 1024], P('mp', 'tile'), may hold values from -0.75 to 0.75
- ln2_gain: bfloat16 [1024], replicated, may hold values from 0.5 to 1.5
- fc1: bfloat16 [1024, 4096], P('tile', 'mp'), may hold values from -0.1875 to 0.1875
- fc2: bfloat16 [4096, 1024], P('mp', 'tile'), may hold values from -0.09375 to 0.09375
- d_lo_out: bfloat16 [2, 384, 24, 1024], P(None, 'tile', None, 'mp'), may hold values from -6 to 6
- d_hi_out: bfloat16 [2, 768, 2, 36864], P(None, 'tile', 'mp'), may hold values from -6 to 6
Outputs:
- lo_out: bfloat16 [2, 384, 24, 1024], P(None, 'tile', None, 'mp')
- hi_out: bfloat16 [2, 768, 2, 36864], P(None, 'tile', 'mp')
- grad_lo: float32 [2, 384, 24, 1024], P(None, 'tile', None, 'mp')
- grad_hi: float32 [2, 768, 2, 36864], P(None, 'tile', 'mp')
- g_cn_kernel: float32 [49, 1536], P(None, 'mp')
- g_cn_gain: float32 [1536], replicated
- g_cn_w1: float32 [1536, 6144], P('tile', 'mp')
- g_cn_w2: float32 [6144, 1536], P('mp', 'tile')
- g_cn_scale: float32 [1536], P('mp')
- g_ad_proj: float32 [1536, 1024], P('tile', 'mp')
- g_ad_kernel: float32 [9, 1024], P(None, 'mp')
- g_gate_w1: float32 [1536, 768], P('tile', 'mp')
- g_gate_w2: float32 [768, 1024], P('mp', 'tile')
- g_ln1_gain: float32 [1024], replicated
- g_qkv: float32 [3, 1024, 1024], P(None, 'tile', 'mp')
- g_out_proj: float32 [1024, 1024], P('mp', 'tile')
- g_ln2_gain: float32 [1024], replicated
- g_fc1: float32 [1024, 4096], P('tile', 'mp')
- g_fc2: float32 [4096, 1024], P('mp', 'tile')
Inputs may be any that keep to these rules, and one draw needn't show every extreme that they name: `image_ids`: image numbers never fall along a canvas; each image covers 1 to 24 whole consecutive rows, and some image covers exactly 24.
All inputs are finite; a program needn't handle non-finite values.
Results may differ from a plain program's by a relative error of at most 0.03.
Values may be sent and summed in bfloat16 or wider, within the bound.
No kernel may reach another device: no remote copies, remote signals or barrier semaphores. Data moves between devices by JAX's collectives and lax.ppermute only.
A program may use at most 832 MiB of HBM per device.

v0:
```python
from functools import reduce

import jax
import jax.numpy as jnp
from jax import lax
from jax.sharding import PartitionSpec as P

HDIM = 64
IMG_ROWS = 24
HCOLS = 48


EPS = 1e-06
NEG = -1e30


def padded_2(value, sides, width):
    for axis, dim in sides:
        devices, length = (lax.axis_size(axis), value.shape[dim])
        up = [(i, (i + 1) % devices) for i in range(devices - 1)]
        down = [(j, i) for i, j in up]
        last = lax.slice_in_dim(value, length - width, length, axis=dim)
        initial = lax.slice_in_dim(value, 0, width, axis=dim)
        before = lax.ppermute(last, axis, up)
        after = lax.ppermute(initial, axis, down)
        value = jnp.concatenate([before, value, after], axis=dim)
    return value


def matmul(left, right):
    return jnp.dot(left, right, preferred_element_type=jnp.float32)


def matmul_tn(left, right):
    return lax.dot_general(
        left, right, (((0,), (0,)), ((), ())), preferred_element_type=jnp.float32
    )


def matmul_nt(left, right):
    return lax.dot_general(
        left, right, (((1,), (1,)), ((), ())), preferred_element_type=jnp.float32
    )


def layer_norm(values, gain_vec):
    average = jnp.mean(values, axis=-1, keepdims=True)
    centered = values - average
    variance = jnp.mean(centered * centered, axis=-1, keepdims=True)
    return centered * lax.rsqrt(variance + EPS) * gain_vec


def gelu_exact(values):
    return jax.nn.gelu(values, approximate=False)


def gelu_grad(pre_act, grad_in):
    result, pull_back = jax.vjp(gelu_exact, pre_act)
    return pull_back(grad_in)[0]


def features(values):
    return lax.all_gather(values, "mp", axis=1, tiled=True)


def partial_sums(values):
    return lax.psum_scatter(values, "mp", scatter_dimension=1, tiled=True)


def rim_rows(values, margin):
    return padded_2(values, (("tile", 0),), margin)


def rim_stats(values, margin):
    return padded_2(values, (("tile", 0),), margin)


def row_labels(labels, first_row, count_rows, margin):
    padded = jnp.pad(labels, (margin, margin), constant_values=-1)
    return lax.dynamic_slice_in_dim(padded, first_row, count_rows + 2 * margin, 0)


def depthwise(padded, kernel, ids_pad, ids_mid, tap_size, flipped):
    margin = tap_size // 2
    row_count = ids_mid.shape[0]
    col_count = padded.shape[1]
    widened = jnp.pad(padded, ((0, 0), (margin, margin), (0, 0)))
    summed = jnp.zeros((row_count, col_count, padded.shape[2]), jnp.float32)
    for a in range(tap_size):
        same_img = (ids_pad[a : a + row_count] == ids_mid)[:, None, None]
        shifted = jnp.where(same_img, widened[a : a + row_count].astype(jnp.float32), 0.0)
        for b in range(tap_size):
            tap_index = (
                (tap_size - 1 - a) * tap_size + (tap_size - 1 - b) if flipped else a * tap_size + b
            )
            summed = summed + kernel[tap_index].astype(jnp.float32) * shifted[:, b : b + col_count]
    return summed


def tap_grads(padded, grad_low, ids_pad, ids_mid, tap_size):
    margin = tap_size // 2
    row_count = ids_mid.shape[0]
    col_count = padded.shape[1]
    widened = jnp.pad(padded, ((0, 0), (margin, margin), (0, 0)))
    grad_vals = grad_low.astype(jnp.float32)
    results = []
    for a in range(tap_size):
        same_img = (ids_pad[a : a + row_count] == ids_mid)[:, None, None]
        shifted = jnp.where(same_img, widened[a : a + row_count].astype(jnp.float32), 0.0)
        for b in range(tap_size):
            results.append(jnp.sum(shifted[:, b : b + col_count] * grad_vals, axis=(0, 1)))
    return jnp.stack(results)


def reduce_grads(terms):
    return (
        lax.psum_scatter(
            terms[0].astype(jnp.bfloat16), "tile", scatter_dimension=0, tiled=True
        ).astype(jnp.float32),
        lax.psum_scatter(
            terms[1].astype(jnp.bfloat16), "tile", scatter_dimension=1, tiled=True
        ).astype(jnp.float32),
        lax.psum_scatter(
            terms[2].astype(jnp.bfloat16), "tile", scatter_dimension=0, tiled=True
        ).astype(jnp.float32),
        lax.psum_scatter(
            terms[3].astype(jnp.bfloat16), "tile", scatter_dimension=0, tiled=True
        ).astype(jnp.float32),
        lax.psum_scatter(
            terms[4].astype(jnp.bfloat16), "tile", scatter_dimension=1, tiled=True
        ).astype(jnp.float32),
        lax.psum_scatter(
            terms[5].astype(jnp.bfloat16), "tile", scatter_dimension=1, tiled=True
        ).astype(jnp.float32),
        lax.psum_scatter(
            terms[6].astype(jnp.bfloat16), "tile", scatter_dimension=1, tiled=True
        ).astype(jnp.float32),
        lax.psum_scatter(
            terms[7].astype(jnp.bfloat16), "tile", scatter_dimension=0, tiled=True
        ).astype(jnp.float32),
        lax.psum_scatter(
            terms[8].astype(jnp.bfloat16), "tile", scatter_dimension=1, tiled=True
        ).astype(jnp.float32),
    )


def add_trees(first_tree, second_tree):
    return jax.tree.map(lambda left, right: left + right, first_tree, second_tree)


def on_device(
    lo_in,
    hi_in,
    image_ids,
    cn_kernel,
    cn_gain,
    cn_w1,
    cn_w2,
    cn_scale,
    ad_proj,
    ad_kernel,
    gate_w1,
    gate_w2,
    ln1_gain,
    qkv,
    out_proj,
    ln2_gain,
    fc1,
    fc2,
    d_lo_out,
    d_hi_out,
):
    micro_count, row_count, col_count, d_shard = lo_in.shape
    hi_rows = hi_in.shape[1]
    hi_cols = HCOLS
    c_shard = hi_in.shape[3] // hi_cols
    margin = IMG_ROWS - 1
    tok_count = row_count * col_count
    pix_count = hi_rows * hi_cols
    row_start = lax.axis_index("tile") * row_count
    mp_index = lax.axis_index("mp")
    head_count = d_shard // HDIM
    attn_scale = HDIM ** (-0.5)

    def own_slice(full_vals, shard_width):
        return lax.dynamic_slice_in_dim(full_vals, mp_index * shard_width, shard_width, 1)

    def attend_scores(query_set, key_set):
        return (
            jnp.einsum("qhd,khd->hqk", query_set, key_set, preferred_element_type=jnp.float32)
            * attn_scale
        )

    big_list, small_list, shown_list = ([], [], [])
    for micro_idx in range(micro_count):
        mlp_in = lax.all_gather(cn_w1, "tile", axis=0, tiled=True)
        mlp_out = lax.all_gather(cn_w2, "tile", axis=1, tiled=True)
        ad_matrix = lax.all_gather(ad_proj, "tile", axis=0, tiled=True)
        gate_in = lax.all_gather(gate_w1, "tile", axis=0, tiled=True)
        gate_out = lax.all_gather(gate_w2, "tile", axis=1, tiled=True)
        qkv_full = lax.all_gather(qkv, "tile", axis=1, tiled=True)
        out_full = lax.all_gather(out_proj, "tile", axis=1, tiled=True)
        ff_in = lax.all_gather(fc1, "tile", axis=0, tiled=True)
        ff_out = lax.all_gather(fc2, "tile", axis=1, tiled=True)
        canvas_ids = image_ids[micro_idx]
        lo_ids = row_labels(canvas_ids, row_start, row_count, margin)
        lo_mid = lo_ids[margin : margin + row_count]
        small_ids = lo_ids[margin - 1 : margin + row_count + 1]
        hi_ids = row_labels(jnp.repeat(canvas_ids, 2), 2 * row_start, hi_rows, 3)
        hi_mid = hi_ids[3 : 3 + hi_rows]
        hi_field = hi_in[micro_idx].reshape(hi_rows, hi_cols, c_shard)
        lo_field = lo_in[micro_idx].astype(jnp.float32).reshape(tok_count, d_shard)
        hi_pad = rim_rows(hi_field, 3)
        conv_low = depthwise(hi_pad, cn_kernel, hi_ids, hi_mid, 7, False).astype(jnp.bfloat16)
        conv_flat = conv_low.reshape(pix_count, c_shard)
        conv_full = features(conv_flat)
        normed, norm_pull = jax.vjp(
            layer_norm, conv_full.astype(jnp.float32), cn_gain.astype(jnp.float32)
        )
        normed_low = normed.astype(jnp.bfloat16)
        inner_pre = matmul(normed_low, mlp_in)
        inner_act = gelu_exact(inner_pre).astype(jnp.bfloat16)
        branch_terms = matmul(inner_act, mlp_out)
        branch = partial_sums(branch_terms)
        hi_scale = cn_scale.astype(jnp.float32)
        hi_sum = hi_field.astype(jnp.float32).reshape(pix_count, c_shard) + hi_scale * branch
        pooled = jnp.mean(hi_sum.reshape(row_count, 2, col_count, 2, c_shard), axis=(1, 3))
        pooled_full = features(pooled.reshape(tok_count, c_shard).astype(jnp.bfloat16))
        proj_low = matmul(pooled_full, ad_matrix).astype(jnp.bfloat16)
        proj_pad = rim_rows(proj_low.reshape(row_count, col_count, d_shard), 1)
        local_conv = depthwise(proj_pad, ad_kernel, small_ids, lo_mid, 3, False).reshape(
            tok_count, d_shard
        )
        gate_pre = matmul(pooled_full, gate_in)
        gate_hidden = gelu_exact(gate_pre).astype(jnp.bfloat16)
        gate_val = jnp.tanh(partial_sums(matmul(gate_hidden, gate_out)))
        mixed_one = lo_field + gate_val * local_conv
        mixed_full = features(mixed_one.astype(jnp.bfloat16))
        norm_one, first_pull = jax.vjp(
            layer_norm, mixed_full.astype(jnp.float32), ln1_gain.astype(jnp.float32)
        )
        norm_low = norm_one.astype(jnp.bfloat16)
        queries = matmul(norm_low, qkv_full[0]).astype(jnp.bfloat16)
        key_rows = matmul(norm_low, qkv_full[1]).astype(jnp.bfloat16)
        value_rows = matmul(norm_low, qkv_full[2]).astype(jnp.bfloat16)
        kv_pad = rim_rows(
            jnp.concatenate([key_rows, value_rows], axis=1).reshape(
                row_count, col_count, 2 * d_shard
            ),
            margin,
        ).reshape(-1, 2 * d_shard)
        key_all = kv_pad[:, :d_shard].reshape(-1, head_count, HDIM)
        value_all = kv_pad[:, d_shard:].reshape(-1, head_count, HDIM)
        query_tok = jnp.repeat(lo_mid, col_count)
        key_tok = jnp.repeat(lo_ids, col_count)
        query3 = queries.reshape(tok_count, head_count, HDIM)
        allowed = (query_tok[:, None] == key_tok[None, :])[None]
        scores = attend_scores(query3, key_all)
        row_max = jnp.max(jnp.where(allowed, scores, NEG), axis=-1, keepdims=True)
        exp_terms = jnp.exp(jnp.where(allowed, scores - row_max, NEG))
        row_total = jnp.sum(exp_terms, axis=-1, keepdims=True)
        log_total = row_max + jnp.log(row_total)
        prob_low = (exp_terms / row_total).astype(jnp.bfloat16)
        attended = (
            jnp.einsum("hqk,khd->qhd", prob_low, value_all, preferred_element_type=jnp.float32)
            .reshape(tok_count, d_shard)
            .astype(jnp.bfloat16)
        )
        mixed_two = mixed_one + partial_sums(matmul(attended, out_full))
        mixed2_full = features(mixed_two.astype(jnp.bfloat16))
        norm_two, second_pull = jax.vjp(
            layer_norm, mixed2_full.astype(jnp.float32), ln2_gain.astype(jnp.float32)
        )
        norm2_low = norm_two.astype(jnp.bfloat16)
        ff_pre = matmul(norm2_low, ff_in)
        ff_hidden = gelu_exact(ff_pre).astype(jnp.bfloat16)
        lo_result = mixed_two + partial_sums(matmul(ff_hidden, ff_out))
        grad_out = d_lo_out[micro_idx].astype(jnp.float32).reshape(tok_count, d_shard)
        ff_grad_full = features(grad_out.astype(jnp.bfloat16))
        grad_ff_out = matmul_tn(ff_hidden, ff_grad_full)
        ff_pre_grad = gelu_grad(ff_pre, matmul_nt(ff_grad_full, ff_out)).astype(jnp.bfloat16)
        grad_ff_in = matmul_tn(norm2_low, ff_pre_grad)
        second_grad = partial_sums(matmul_nt(ff_pre_grad, ff_in)).astype(jnp.bfloat16)
        back_two, grad_ln2 = second_pull(features(second_grad).astype(jnp.float32))
        grad_two = grad_out + own_slice(back_two, d_shard)
        att_grad_full = features(grad_two.astype(jnp.bfloat16))
        grad_out_full = matmul_tn(attended, att_grad_full)
        att_grad = matmul_nt(att_grad_full, out_full).astype(jnp.bfloat16)
        grad3 = att_grad.reshape(tok_count, head_count, HDIM)
        scores_again = attend_scores(query3, key_all)
        chance = jnp.exp(jnp.where(allowed, scores_again - log_total, NEG))
        chance_grad = jnp.einsum(
            "qhd,khd->hqk", grad3, value_all, preferred_element_type=jnp.float32
        )
        delta = jnp.sum(chance * chance_grad, axis=-1, keepdims=True)
        score_grad = (chance * (chance_grad - delta)).astype(jnp.bfloat16)
        query_grad = (
            (
                jnp.einsum("hqk,khd->qhd", score_grad, key_all, preferred_element_type=jnp.float32)
                * attn_scale
            )
            .reshape(tok_count, d_shard)
            .astype(jnp.bfloat16)
        )
        sent_pad = rim_rows(
            jnp.concatenate([queries, att_grad], axis=1).reshape(row_count, col_count, 2 * d_shard),
            margin,
        ).reshape(-1, 2 * d_shard)
        stats_local = jnp.concatenate([log_total[:, :, 0], delta[:, :, 0]], axis=0)
        stats_pad = (
            rim_stats(stats_local.T.reshape(row_count, col_count, 2 * head_count), margin)
            .reshape(-1, 2 * head_count)
            .T
        )
        query_pad = sent_pad[:, :d_shard].reshape(-1, head_count, HDIM)
        grad_pad = sent_pad[:, d_shard:].reshape(-1, head_count, HDIM)
        total_pad = stats_pad[:head_count][:, :, None]
        delta_pad = stats_pad[head_count:][:, :, None]
        key3 = key_rows.reshape(tok_count, head_count, HDIM)
        value3 = value_rows.reshape(tok_count, head_count, HDIM)
        allowed_back = (key_tok[:, None] == query_tok[None, :])[None]
        scores_back = attend_scores(query_pad, key3)
        chance_back = jnp.exp(jnp.where(allowed_back, scores_back - total_pad, NEG))
        chance_grad_back = jnp.einsum(
            "qhd,khd->hqk", grad_pad, value3, preferred_element_type=jnp.float32
        )
        score_grad_back = (chance_back * (chance_grad_back - delta_pad)).astype(jnp.bfloat16)
        key_grad = (
            (
                jnp.einsum(
                    "hqk,qhd->khd", score_grad_back, query_pad, preferred_element_type=jnp.float32
                )
                * attn_scale
            )
            .reshape(tok_count, d_shard)
            .astype(jnp.bfloat16)
        )
        value_grad = (
            jnp.einsum(
                "hqk,qhd->khd",
                chance_back.astype(jnp.bfloat16),
                grad_pad,
                preferred_element_type=jnp.float32,
            )
            .reshape(tok_count, d_shard)
            .astype(jnp.bfloat16)
        )
        grad_qkv = jnp.stack(
            [
                matmul_tn(norm_low, query_grad),
                matmul_tn(norm_low, key_grad),
                matmul_tn(norm_low, value_grad),
            ]
        )
        first_grad = partial_sums(
            matmul_nt(query_grad, qkv_full[0])
            + matmul_nt(key_grad, qkv_full[1])
            + matmul_nt(value_grad, qkv_full[2])
        ).astype(jnp.bfloat16)
        back_one, grad_ln1 = first_pull(features(first_grad).astype(jnp.float32))
        grad_one = grad_two + own_slice(back_one, d_shard)
        gate_pre_grad = (grad_one * local_conv * (1.0 - gate_val * gate_val)).astype(jnp.bfloat16)
        gate_grad_full = features(gate_pre_grad)
        grad_gate_out = matmul_tn(gate_hidden, gate_grad_full)
        hidden_grad = gelu_grad(gate_pre, matmul_nt(gate_grad_full, gate_out)).astype(jnp.bfloat16)
        grad_gate_in = matmul_tn(pooled_full, hidden_grad)
        local_grad = (
            (grad_one * gate_val).astype(jnp.bfloat16).reshape(row_count, col_count, d_shard)
        )
        local_pad = rim_rows(local_grad, 1)
        proj_grad = (
            depthwise(local_pad, ad_kernel, small_ids, lo_mid, 3, True)
            .reshape(tok_count, d_shard)
            .astype(jnp.bfloat16)
        )
        grad_ad_kernel = tap_grads(proj_pad, local_grad, small_ids, lo_mid, 3)
        grad_ad_matrix = matmul_tn(pooled_full, proj_grad)
        pooled_grad = partial_sums(
            matmul_nt(hidden_grad, gate_in) + matmul_nt(proj_grad, ad_matrix)
        )
        spread_grad = jnp.broadcast_to(
            pooled_grad.reshape(row_count, 1, col_count, 1, c_shard) * 0.25,
            (row_count, 2, col_count, 2, c_shard),
        ).reshape(pix_count, c_shard)
        hi_grad = d_hi_out[micro_idx].astype(jnp.float32).reshape(pix_count, c_shard) + spread_grad
        grad_scale = jnp.sum(hi_grad * branch, axis=0)
        scaled_grad = (hi_grad * hi_scale).astype(jnp.bfloat16)
        branch_full = features(scaled_grad)
        grad_mlp_out = matmul_tn(inner_act, branch_full)
        inner_grad = gelu_grad(inner_pre, matmul_nt(branch_full, mlp_out)).astype(jnp.bfloat16)
        grad_mlp_in = matmul_tn(normed_low, inner_grad)
        normed_terms = matmul_nt(inner_grad, mlp_in)
        normed_grad = partial_sums(normed_terms).astype(jnp.bfloat16)
        back_conv, grad_cn_gain = norm_pull(features(normed_grad).astype(jnp.float32))
        conv_grad = own_slice(back_conv, c_shard).astype(jnp.bfloat16)
        conv_grad = conv_grad.reshape(hi_rows, hi_cols, c_shard)
        conv_pad = rim_rows(conv_grad, 3)
        hi_back = hi_grad.reshape(hi_rows, hi_cols, c_shard) + depthwise(
            conv_pad, cn_kernel, hi_ids, hi_mid, 7, True
        )
        grad_cn_kernel = tap_grads(hi_pad, conv_grad, hi_ids, hi_mid, 7)
        big_terms = (
            grad_mlp_in,
            grad_mlp_out,
            grad_ad_matrix,
            grad_gate_in,
            grad_gate_out,
            grad_qkv,
            grad_out_full,
            grad_ff_in,
            grad_ff_out,
        )
        small_terms = (grad_cn_kernel, grad_cn_gain, grad_scale, grad_ad_kernel, grad_ln1, grad_ln2)
        shown = (
            lo_result.reshape(row_count, col_count, d_shard).astype(jnp.bfloat16),
            hi_sum.reshape(hi_rows, 1, hi_cols * c_shard).astype(jnp.bfloat16),
            grad_one.reshape(row_count, col_count, d_shard),
            hi_back.reshape(hi_rows, 1, hi_cols * c_shard),
        )
        big_terms, small_terms, shown = (big_terms, small_terms, shown)
        big_list.append(big_terms)
        small_list.append(small_terms)
        shown_list.append(shown)
    big_final = reduce(add_trees, [reduce_grads(terms) for terms in big_list])
    small_local = reduce(add_trees, small_list)
    small_final = (
        lax.psum(small_local[0].astype(jnp.bfloat16), "tile").astype(jnp.float32),
        lax.psum(small_local[1].astype(jnp.bfloat16), "tile").astype(jnp.float32),
        lax.psum(small_local[2].astype(jnp.bfloat16), "tile").astype(jnp.float32),
        lax.psum(small_local[3].astype(jnp.bfloat16), "tile").astype(jnp.float32),
        lax.psum(small_local[4].astype(jnp.bfloat16), "tile").astype(jnp.float32),
        lax.psum(small_local[5].astype(jnp.bfloat16), "tile").astype(jnp.float32),
    )
    lo_stack = jnp.stack([item[0] for item in shown_list])
    hi_stack = jnp.stack([item[1] for item in shown_list])
    glo_stack = jnp.stack([item[2] for item in shown_list])
    ghi_stack = jnp.stack([item[3] for item in shown_list])
    return (
        lo_stack,
        hi_stack,
        glo_stack,
        ghi_stack,
        small_final[0],
        small_final[1],
        big_final[0],
        big_final[1],
        small_final[2],
        big_final[2],
        small_final[3],
        big_final[3],
        big_final[4],
        small_final[4],
        big_final[5],
        big_final[6],
        small_final[5],
        big_final[7],
        big_final[8],
    )


def solution(mesh):
    in_specs = (
        P(None, "tile", None, "mp"),
        P(None, "tile", "mp", None),
        P(),
        P(None, "mp"),
        P(),
        P("tile", "mp"),
        P("mp", "tile"),
        P("mp"),
        P("tile", "mp"),
        P(None, "mp"),
        P("tile", "mp"),
        P("mp", "tile"),
        P(),
        P(None, "tile", "mp"),
        P("mp", "tile"),
        P(),
        P("tile", "mp"),
        P("mp", "tile"),
        P(None, "tile", None, "mp"),
        P(None, "tile", "mp", None),
    )
    out_specs = (
        P(None, "tile", None, "mp"),
        P(None, "tile", "mp", None),
        P(None, "tile", None, "mp"),
        P(None, "tile", "mp", None),
        P(None, "mp"),
        P(),
        P("tile", "mp"),
        P("mp", "tile"),
        P("mp"),
        P("tile", "mp"),
        P(None, "mp"),
        P("tile", "mp"),
        P("mp", "tile"),
        P(),
        P(None, "tile", "mp"),
        P("mp", "tile"),
        P(),
        P("tile", "mp"),
        P("mp", "tile"),
    )
    return jax.shard_map(
        on_device, mesh=mesh, in_specs=in_specs, out_specs=out_specs, check_vma=False
    )
```

profile of v0, /device:TPU:0, one launch (start us, length us, event | category | flops | bytes accessed | tf_op | source)
XLA Modules:
  0.0 5696.5 jit_solution(18362882258985663035)
XLA Ops:
  66.9 132.4 %add_convert_fusion.3 = bf16[48,48,768]{2,1,0:T(8,128)(2,1)} fusion(f32[48,54,768]{2,1,0:T(8,128)} %get-tuple-element.324, f32[48,54,768]{2,1,0:T(8,128)} %get-tuple-element.320, f32[48,54,768]{2,1,0:T(8,128)} %get-tuple-element.321, f32[48,54,768]{2,1,0:T(8,128)} %slice_convert_fusion.3, f32[48,54,768]{2,1,0:T(8,128)} %get-tuple-element.322, ...), kind=kLoop, calls=%fused_computation.532 | loop fusion | flops 173408256 | bytes 350505984 | tf_op jit(solution)/shard_map/convert_element_type | solution.py:214
  213.1 78.4 %all-gather.31.cloned.1.call-done = bf16[2304,1536]{1,0:T(8,128)(2,1)} async-done(((bf16[2304,768]{1,0:T(8,128)(2,1)}), bf16[2304,1536]{1,0:T(8,128)(2,1)}) %all-gather.31.cloned.1.call-update) | async-done | bytes 7077904 | tf_op jit(solution)/shard_map/all_gather | solution.py:63
  299.1 76.1 %all-gather.33.cloned.1.call-done = bf16[1536,3072]{1,0:T(8,128)(2,1)} async-done(((bf16[96,3072]{1,0:T(8,128)(2,1)}), bf16[1536,3072]{1,0:T(8,128)(2,1)}) %all-gather.33.cloned.1.call-update) | async-done | bytes 9437200 | tf_op jit(solution)/shard_map/all_gather | solution.py:196
  375.2 89.9 %multiply_convert_fusion.5 = (bf16[2304,3072]{1,0:T(8,128)(2,1)}, f32[2304,3072]{1,0:T(8,128)}, f32[2304,3072]{1,0:T(8,128)}) fusion(bf16[1536,3072]{1,0:T(8,128)(2,1)} %all-gather.33.cloned.1.call-done, bf16[2304,1536]{1,0:T(8,128)(2,1)} %all-gather.31.cloned.1.call-done, f32[1536]{0:T(1024)S(1)} %convert_element_type.1630, f32[2304]{0:T(1024)S(1)} %fusion.394, ...), kind=kOutput, calls=%fused_computation.133 | convolution fusion | flops 22221029376 | bytes 87318528 | tf_op jit(solution)/shard_map/dot_general | solution.py:31
  502.8 151.6 %reduce-scatter.35.cloned.1.call-done = f32[2304,768]{1,0:T(8,128)} async-done(((f32[2304,1536]{1,0:T(8,128)}), f32[2304,768]{1,0:T(8,128)}) %reduce-scatter.35.cloned.1.call-update) | async-done | bytes 7077904 | tf_op jit(solution)/shard_map/reduce_scatter | solution.py:67
  1430.9 131.1 %add_convert_fusion.2 = bf16[48,48,768]{2,1,0:T(8,128)(2,1)} fusion(f32[48,54,768]{2,1,0:T(8,128)} %get-tuple-element.330, f32[48,54,768]{2,1,0:T(8,128)} %get-tuple-element.326, f32[48,54,768]{2,1,0:T(8,128)} %get-tuple-element.327, f32[48,54,768]{2,1,0:T(8,128)} %slice_convert_fusion.2, f32[48,54,768]{2,1,0:T(8,128)} %get-tuple-element.328, ...), kind=kLoop, calls=%fused_computation.530 | loop fusion | flops 173408256 | bytes 350505984 | tf_op jit(solution)/shard_map/convert_element_type | solution.py:214
  1564.5 88.1 %all-gather.55.cloned.1.call-done = bf16[2304,1536]{1,0:T(8,128)(2,1)} async-done(((bf16[2304,768]{1,0:T(8,128)(2,1)}), bf16[2304,1536]{1,0:T(8,128)(2,1)}) %all-gather.55.cloned.1.call-update) | async-done | bytes 7077904 | tf_op jit(solution)/shard_map/all_gather | solution.py:63
  1720.5 90.2 %multiply_convert_fusion.4 = (bf16[2304,3072]{1,0:T(8,128)(2,1)}, f32[2304,3072]{1,0:T(8,128)}, f32[2304,3072]{1,0:T(8,128)}) fusion(bf16[1536,3072]{1,0:T(8,128)(2,1)} %all-gather.33.cloned.1.call-done, bf16[2304,1536]{1,0:T(8,128)(2,1)} %all-gather.55.cloned.1.call-done, f32[2304]{0:T(1024)S(1)} %fusion.395, f32[2304]{0:T(1024)S(1)} %broadcast_multiply_fusion.2, ...), kind=kOutput, calls=%fused_computation.120 | convolution fusion | flops 22221029376 | bytes 87318528 | tf_op jit(solution)/shard_map/dot_general | solution.py:31
  1880.2 118.6 %reduce-scatter.43.cloned.1.call-done = f32[2304,768]{1,0:T(8,128)} async-done(((f32[2304,1536]{1,0:T(8,128)}), f32[2304,768]{1,0:T(8,128)}) %reduce-scatter.43.cloned.1.call-update) | async-done | bytes 7077904 | tf_op jit(solution)/shard_map/reduce_scatter | solution.py:67
  3307.7 71.5 %reduce-scatter.99.cloned.1.call-done = bf16[2048,64]{0,1:T(8,128)(2,1)} async-done(((bf16[2048,1024]{0,1:T(8,128)(2,1)}), bf16[2048,64]{0,1:T(8,128)(2,1)}) %reduce-scatter.99.cloned.1.call-update) | async-done | bytes 262160 | tf_op jit(solution)/shard_map/reduce_scatter | solution.py:141
  3379.2 76.1 %reduce-scatter.101.cloned.1.call-done = bf16[2048,64]{0,1:T(8,128)(2,1)} async-done(((bf16[2048,1024]{0,1:T(8,128)(2,1)}), bf16[2048,64]{0,1:T(8,128)(2,1)}) %reduce-scatter.101.cloned.1.call-update) | async-done | bytes 262160 | tf_op jit(solution)/shard_map/reduce_scatter | solution.py:141
  3457.2 73.3 %reduce-scatter.95.cloned.1.call-done = bf16[64,2048]{1,0:T(8,128)(2,1)} async-done(((bf16[1024,2048]{1,0:T(8,128)(2,1)}), bf16[64,2048]{1,0:T(8,128)(2,1)}) %reduce-scatter.95.cloned.1.call-update) | async-done | bytes 262160 | tf_op jit(solution)/shard_map/reduce_scatter | solution.py:138
  3530.4 76.0 %reduce-scatter.97.cloned.1.call-done = bf16[64,2048]{1,0:T(8,128)(2,1)} async-done(((bf16[1024,2048]{1,0:T(8,128)(2,1)}), bf16[64,2048]{1,0:T(8,128)(2,1)}) %reduce-scatter.97.cloned.1.call-update) | async-done | bytes 262160 | tf_op jit(solution)/shard_map/reduce_scatter | solution.py:138
  3728.3 67.3 %reduce-scatter.87.cloned.1.call-done = bf16[3,64,512]{2,1,0:T(8,128)(2,1)} async-done(((bf16[3,1024,512]{2,1,0:T(8,128)(2,1)}), bf16[3,64,512]{2,1,0:T(8,128)(2,1)}) %reduce-scatter.87.cloned.1.call-update) | async-done | bytes 196624 | tf_op jit(solution)/shard_map/reduce_scatter | solution.py:132
  3795.6 68.9 %reduce-scatter.89.cloned.1.call-done = bf16[3,64,512]{2,1,0:T(8,128)(2,1)} async-done(((bf16[3,1024,512]{2,1,0:T(8,128)(2,1)}), bf16[3,64,512]{2,1,0:T(8,128)(2,1)}) %reduce-scatter.89.cloned.1.call-update) | async-done | bytes 196624 | tf_op jit(solution)/shard_map/reduce_scatter | solution.py:132
  4045.1 62.7 %reduce-scatter.77.cloned.1.call-done = bf16[96,512]{1,0:T(8,128)(2,1)} async-done(((bf16[1536,512]{1,0:T(8,128)(2,1)}), bf16[96,512]{1,0:T(8,128)(2,1)}) %reduce-scatter.77.cloned.1.call-update) | async-done | bytes 98320 | tf_op jit(solution)/shard_map/reduce_scatter | solution.py:123
  4240.9 102.5 %reduce-scatter.71.cloned.1.call-done = bf16[3072,96]{0,1:T(8,128)(2,1)} async-done(((bf16[3072,1536]{0,1:T(8,128)(2,1)}), bf16[3072,96]{0,1:T(8,128)(2,1)}) %reduce-scatter.71.cloned.1.call-update) | async-done | bytes 589840 | tf_op jit(solution)/shard_map/reduce_scatter | solution.py:120
  4343.4 115.8 %reduce-scatter.73.cloned.1.call-done = bf16[3072,96]{0,1:T(8,128)(2,1)} async-done(((bf16[3072,1536]{0,1:T(8,128)(2,1)}), bf16[3072,96]{0,1:T(8,128)(2,1)}) %reduce-scatter.73.cloned.1.call-update) | async-done | bytes 589840 | tf_op jit(solution)/shard_map/reduce_scatter | solution.py:120
  4461.6 112.8 %reduce-scatter.67.cloned.1.call-done = bf16[96,3072]{1,0:T(8,128)(2,1)} async-done(((bf16[1536,3072]{1,0:T(8,128)(2,1)}), bf16[96,3072]{1,0:T(8,128)(2,1)}) %reduce-scatter.67.cloned.1.call-update) | async-done | bytes 589840 | tf_op jit(solution)/shard_map/reduce_scatter | solution.py:117
  4574.5 116.4 %reduce-scatter.69.cloned.1.call-done = bf16[96,3072]{1,0:T(8,128)(2,1)} async-done(((bf16[1536,3072]{1,0:T(8,128)(2,1)}), bf16[96,3072]{1,0:T(8,128)(2,1)}) %reduce-scatter.69.cloned.1.call-update) | async-done | bytes 589840 | tf_op jit(solution)/shard_map/reduce_scatter | solution.py:117
  4693.2 88.0 %all-gather.83.cloned.1.call-done = bf16[2304,1536]{1,0:T(8,128)(2,1)} async-done(((bf16[2304,768]{1,0:T(8,128)(2,1)}), bf16[2304,1536]{1,0:T(8,128)(2,1)}) %all-gather.83.cloned.1.call-update) | async-done | bytes 7077904 | tf_op jit(solution)/shard_map/all_gather | solution.py:63
  4781.3 90.7 %all-gather.89.cloned.1.call-done = bf16[2304,1536]{1,0:T(8,128)(2,1)} async-done(((bf16[2304,768]{1,0:T(8,128)(2,1)}), bf16[2304,1536]{1,0:T(8,128)(2,1)}) %all-gather.89.cloned.1.call-update) | async-done | bytes 7077904 | tf_op jit(solution)/shard_map/all_gather | solution.py:63
  5380.7 134.1 %fusion.148 = f32[48,48,768]{2,1,0:T(8,128)} fusion(f32[48,48,768]{2,1,0:T(8,128)} %reshape.1143, f32[6,8,48,768]{3,2,1,0:T(8,128)} %copy.145, f32[48,54,768]{2,1,0:T(8,128)} %get-tuple-element.312, f32[48,54,768]{2,1,0:T(8,128)} %get-tuple-element.308, f32[48,54,768]{2,1,0:T(8,128)} %get-tuple-element.309, f32[48,54,768]{2,1,0:T(8,128)} %slice_convert_fusion.1, ...), kind=kLoop, calls=%fused_computation.325 | loop fusion | flops 175177728 | bytes 368200704 | tf_op jit(solution)/shard_map/add | solution.py:398
  5526.1 135.4 %fusion.147 = f32[48,48,768]{2,1,0:T(8,128)} fusion(f32[48,48,768]{2,1,0:T(8,128)} %reshape.1147, f32[6,8,48,768]{3,2,1,0:T(8,128)} %copy.146, f32[48,54,768]{2,1,0:T(8,128)} %get-tuple-element.318, f32[48,54,768]{2,1,0:T(8,128)} %get-tuple-element.314, f32[48,54,768]{2,1,0:T(8,128)} %get-tuple-element.315, f32[48,54,768]{2,1,0:T(8,128)} %slice_convert_fusion, ...), kind=kLoop, calls=%fused_computation.323 | loop fusion | flops 175177728 | bytes 368200704 | tf_op jit(solution)/shard_map/add | solution.py:398
  (1502 shorter events, 3327.2 us)
Async XLA Ops:
  200.9 453.5 %reduce-scatter.35.cloned.1.call-start = ((), (), s32[]{:S(2)}) async-start(), calls=%async_computation.37 | async-start | bytes 21233664 | tf_op jit(solution)/shard_map/reduce_scatter | solution.py:67
  2748.7 428.2 %reduce-scatter.61.cloned.1.call-start = ((), (), s32[]{:S(2)}) async-start(), calls=%async_computation.73 | async-start | bytes 21233664 | tf_op jit(solution)/shard_map/reduce_scatter | solution.py:67
  2893.2 372.2 %reduce-scatter.65.cloned.1.call-start = ((), (), s32[]{:S(2)}) async-start(), calls=%async_computation.78 | async-start | bytes 21233664 | tf_op jit(solution)/shard_map/reduce_scatter | solution.py:67
  2984.8 394.4 %reduce-scatter.99.cloned.1.call-start = ((), (), s32[]{:S(2)}) async-start(), calls=%async_computation.97 | async-start | bytes 4456448 | tf_op jit(solution)/shard_map/reduce_scatter | solution.py:141
  2990.0 465.3 %reduce-scatter.101.cloned.1.call-start = ((), (), s32[]{:S(2)}) async-start(), calls=%async_computation.98 | async-start | bytes 4456448 | tf_op jit(solution)/shard_map/reduce_scatter | solution.py:141
  2998.0 532.4 %reduce-scatter.95.cloned.1.call-start = ((), (), s32[]{:S(2)}) async-start(), calls=%async_computation.95 | async-start | bytes 4456448 | tf_op jit(solution)/shard_map/reduce_scatter | solution.py:138
  3005.4 601.1 %reduce-scatter.97.cloned.1.call-start = ((), (), s32[]{:S(2)}) async-start(), calls=%async_computation.96 | async-start | bytes 4456448 | tf_op jit(solution)/shard_map/reduce_scatter | solution.py:138
  3012.5 653.8 %reduce-scatter.91.cloned.1.call-start = ((), (), s32[]{:S(2)}) async-start(), calls=%async_computation.93 | async-start | bytes 1114112 | tf_op jit(solution)/shard_map/reduce_scatter | solution.py:135
  3016.0 710.8 %reduce-scatter.93.cloned.1.call-start = ((), (), s32[]{:S(2)}) async-start(), calls=%async_computation.94 | async-start | bytes 1114112 | tf_op jit(solution)/shard_map/reduce_scatter | solution.py:135
  3019.7 775.9 %reduce-scatter.87.cloned.1.call-start = ((), (), s32[]{:S(2)}) async-start(), calls=%async_computation.91 | async-start | bytes 3342336 | tf_op jit(solution)/shard_map/reduce_scatter | solution.py:132
  3028.1 836.4 %reduce-scatter.89.cloned.1.call-start = ((), (), s32[]{:S(2)}) async-start(), calls=%async_computation.92 | async-start | bytes 3342336 | tf_op jit(solution)/shard_map/reduce_scatter | solution.py:132
  3035.1 888.2 %reduce-scatter.83.cloned.1.call-start = ((), (), s32[]{:S(2)}) async-start(), calls=%async_computation.89 | async-start | bytes 835584 | tf_op jit(solution)/shard_map/reduce_scatter | solution.py:129
  3038.4 944.5 %reduce-scatter.85.cloned.1.call-start = ((), (), s32[]{:S(2)}) async-start(), calls=%async_computation.90 | async-start | bytes 835584 | tf_op jit(solution)/shard_map/reduce_scatter | solution.py:129
  3041.7 1003.4 %reduce-scatter.75.cloned.1.call-start = ((), (), s32[]{:S(2)}) async-start(), calls=%async_computation.85 | async-start | bytes 1671168 | tf_op jit(solution)/shard_map/reduce_scatter | solution.py:123
  3044.4 1063.4 %reduce-scatter.77.cloned.1.call-start = ((), (), s32[]{:S(2)}) async-start(), calls=%async_computation.86 | async-start | bytes 1671168 | tf_op jit(solution)/shard_map/reduce_scatter | solution.py:123
  3048.7 1119.8 %reduce-scatter.79.cloned.1.call-start = ((), (), s32[]{:S(2)}) async-start(), calls=%async_computation.87 | async-start | bytes 1253376 | tf_op jit(solution)/shard_map/reduce_scatter | solution.py:126
  3051.4 1177.7 %reduce-scatter.81.cloned.1.call-start = ((), (), s32[]{:S(2)}) async-start(), calls=%async_computation.88 | async-start | bytes 1253376 | tf_op jit(solution)/shard_map/reduce_scatter | solution.py:126
  3055.3 1288.1 %reduce-scatter.71.cloned.1.call-start = ((), (), s32[]{:S(2)}) async-start(), calls=%async_computation.83 | async-start | bytes 10027008 | tf_op jit(solution)/shard_map/reduce_scatter | solution.py:120
  3084.1 1375.1 %reduce-scatter.73.cloned.1.call-start = ((), (), s32[]{:S(2)}) async-start(), calls=%async_computation.84 | async-start | bytes 10027008 | tf_op jit(solution)/shard_map/reduce_scatter | solution.py:120
  3113.3 1461.2 %reduce-scatter.67.cloned.1.call-start = ((), (), s32[]{:S(2)}) async-start(), calls=%async_computation.81 | async-start | bytes 10027008 | tf_op jit(solution)/shard_map/reduce_scatter | solution.py:117
  3145.1 1545.8 %reduce-scatter.69.cloned.1.call-start = ((), (), s32[]{:S(2)}) async-start(), calls=%async_computation.82 | async-start | bytes 10027008 | tf_op jit(solution)/shard_map/reduce_scatter | solution.py:117
  3176.8 1604.5 %all-gather.83.cloned.1.call-start = ((), (), s32[]{:S(2)}) async-start(), calls=%async_computation.74 | async-start | bytes 10616832 | tf_op jit(solution)/shard_map/all_gather | solution.py:63
  3182.0 1689.9 %all-gather.89.cloned.1.call-start = ((), (), s32[]{:S(2)}) async-start(), calls=%async_computation.79 | async-start | bytes 10616832 | tf_op jit(solution)/shard_map/all_gather | solution.py:63
  3270.6 2060.2 %all-reduce.15.cloned.1.call-start = ((), (), s32[]{:S(2)}) async-start(), calls=%async_computation.80 | async-start | bytes 172032 | tf_op jit(solution)/shard_map/psum | solution.py:427
  (481 other events, 21645.1 us)
Sparse Core Ops, SparseCore 0:
  199.5 91.9 all-gather.30
  293.8 81.4 all-gather.32
  377.5 79.5 all-gather.34
  494.6 159.7 reduce-scatter.34
  1562.1 90.4 all-gather.54
  1837.3 161.3 reduce-scatter.42
  2720.8 89.2 all-gather.80
  2811.7 89.2 all-gather.86
  2903.2 161.4 reduce-scatter.60
  3104.0 161.4 reduce-scatter.64
  3306.8 72.3 reduce-scatter.98
  3383.4 71.8 reduce-scatter.100
  3459.0 71.4 reduce-scatter.94
  3534.6 71.7 reduce-scatter.96
  3730.5 65.1 reduce-scatter.86
  3799.4 65.0 reduce-scatter.88
  4049.2 58.5 reduce-scatter.76
  4233.0 110.3 reduce-scatter.70
  4348.1 111.1 reduce-scatter.72
  4463.3 111.0 reduce-scatter.66
  4579.7 111.0 reduce-scatter.68
  4692.2 88.9 all-gather.82
  4782.6 89.2 all-gather.88
  5244.4 86.3 all-reduce.14
  (41 shorter events, 1517.5 us)
where the time goes:
time: 5720 us; the launch traced here: 5700 us
  waiting for transfers between devices  2960 us (52%)
  other arithmetic  1290 us (23%)
  matrix products  976 us (17%)
  local copies, waits for them, and re-layouts  290 us (5%)
  blocking collectives  84.5 us (1%)
  starting transfers between devices  79.5 us (1%)
    all_gather x22, waiting for transfers between devices, features(): return lax.all_gather(values, 'mp', axis=1, tiled=True)  699 us
    reduce_scatter x16, waiting for transfers between devices, partial_sums(): return lax.psum_scatter(values, 'mp', scatter_dimension=1, tiled=True)  623 us
    dot_general x22, matrix products, matmul(): return jnp.dot(left, right, preferred_element_type=jnp.float32)  302 us
    reduce_sum x10, other arithmetic, tap_grads(): jnp.sum(shifted[:, b:b + col_count] * grad_vals, axis=(0, 1))  302 us
    add x2, other arithmetic, on_device(): hi_grad.reshape(hi_rows, hi_cols, c_shard)  270 us
    convert_element_type x2, other arithmetic, on_device(): depthwise(hi_pad, cn_kernel, hi_ids, hi_mid, 7, False).astype(jnp.bfloat16)  263 us
    reduce_scatter x2, waiting for transfers between devices, reduce_grads(): lax.psum_scatter(terms[0].astype(jnp.bfloat16), 'tile', scatter_dimension...  229 us
    dot_general x22, matrix products, matmul_nt(): lax.dot_general(left, right, (((1,), (1,)), ((), ())), preferred_element_...  228 us
  transfers between devices with their start and end apart: 93, of which 61 were waited for; matrix products, arithmetic and copies ran while one was open for 22% of the time, Pallas kernels for 0%

commit v1 on v0

v1 whole, which is shorter than its diff:
```python
import jax
import jax.numpy as jnp
import numpy as np
from jax import lax
from jax.experimental import pallas as pl
from jax.experimental.pallas import tpu as pltpu
from jax.sharding import Mesh
from jax.sharding import PartitionSpec as P

HDIM = 64
IMG_ROWS = 24
HCOLS = 48

EPS = 1e-06
NEG = -1e30
BF = jnp.bfloat16
F32 = jnp.float32
ALL = ("mb", "tile")


def rim_pair(value, width, axis):
    devices, length = lax.axis_size("tile"), value.shape[axis]
    up = [(i, (i + 1) % devices) for i in range(devices - 1)]
    down = [(j, i) for i, j in up]
    before = lax.ppermute(lax.slice_in_dim(value, length - width, length, axis=axis), "tile", up)
    after = lax.ppermute(lax.slice_in_dim(value, 0, width, axis=axis), "tile", down)
    return before, after


def rim_rows(value, width):
    devices, length = lax.axis_size("tile"), value.shape[0]
    up = [(i, (i + 1) % devices) for i in range(devices - 1)]
    down = [(j, i) for i, j in up]
    before = lax.ppermute(value[length - width :], "tile", up)
    after = lax.ppermute(value[:width], "tile", down)
    return jnp.concatenate([before, value, after], axis=0)


def matmul(left, right):
    return jnp.dot(left, right, preferred_element_type=F32)


def matmul_tn(left, right):
    return lax.dot_general(left, right, (((0,), (0,)), ((), ())), preferred_element_type=F32)


def matmul_nt(left, right):
    return lax.dot_general(left, right, (((1,), (1,)), ((), ())), preferred_element_type=F32)


def layer_norm(values, gain_vec):
    average = jnp.mean(values, axis=-1, keepdims=True)
    centered = values - average
    variance = jnp.mean(centered * centered, axis=-1, keepdims=True)
    return centered * lax.rsqrt(variance + EPS) * gain_vec


def gelu_pair(values):
    cdf = 0.5 + 0.5 * lax.erf(values * 0.7071067811865476)
    slope = cdf + values * (0.3989422804014327 * jnp.exp(-0.5 * values * values))
    return (values * cdf).astype(BF), slope.astype(BF)


def features(values):
    parts = lax.axis_size("tp")
    if parts == 1:
        return values
    rows, width = values.shape
    full = lax.all_gather(values.reshape(rows, 2, width // 2), "tp", axis=2)
    return full.reshape(rows, parts * width)


def partial_sums(values):
    parts = lax.axis_size("tp")
    if parts == 1:
        return values
    rows, width = values.shape
    split = values.reshape(rows, 2, parts, width // (2 * parts))
    return lax.psum_scatter(split, "tp", scatter_dimension=2).reshape(rows, width // parts)


def own_slice(values):
    parts = lax.axis_size("tp")
    if parts == 1:
        return values
    rows, width = values.shape
    split = values.reshape(rows, 2, parts, width // (2 * parts))
    own = lax.dynamic_index_in_dim(split, lax.axis_index("tp"), 2, keepdims=False)
    return own.reshape(rows, width // parts)


SWAP = [(0, 1), (1, 0)]


def swap_micro(values):
    mine = lax.axis_index("mb")
    own = lax.dynamic_index_in_dim(values, mine, 0, keepdims=False)
    sent = lax.dynamic_index_in_dim(values, 1 - mine, 0, keepdims=False)
    return own, lax.ppermute(sent, "mb", SWAP)


def in_order(own, other, axis):
    first = lax.axis_index("mb") == 0
    return jnp.concatenate(
        [jnp.where(first, own, other), jnp.where(first, other, own)], axis=axis
    )


def both_micro(own, other):
    first = lax.axis_index("mb") == 0
    return jnp.stack([jnp.where(first, own, other), jnp.where(first, other, own)])


def halves(values):
    width = values.shape[-1] // 2
    mine = lax.axis_index("mb")
    own = lax.dynamic_slice_in_dim(values, mine * width, width, values.ndim - 1)
    sent = lax.dynamic_slice_in_dim(values, (1 - mine) * width, width, values.ndim - 1)
    return own, sent


def row_labels(labels, first_row, count_rows, margin):
    padded = jnp.pad(labels, (margin, margin), constant_values=-1)
    return lax.dynamic_slice_in_dim(padded, first_row, count_rows + 2 * margin, 0)


def depthwise(padded, kernel, ids_pad, ids_mid, tap_size, flipped):
    margin = tap_size // 2
    row_count = ids_mid.shape[0]
    col_count = padded.shape[1]
    widened = jnp.pad(padded, ((0, 0), (margin, margin), (0, 0)))
    summed = jnp.zeros((row_count, col_count, padded.shape[2]), F32)
    for a in range(tap_size):
        same_img = (ids_pad[a : a + row_count] == ids_mid)[:, None, None]
        shifted = jnp.where(same_img, widened[a : a + row_count].astype(F32), 0.0)
        for b in range(tap_size):
            tap_index = (
                (tap_size - 1 - a) * tap_size + (tap_size - 1 - b) if flipped else a * tap_size + b
            )
            summed = summed + kernel[tap_index].astype(F32) * shifted[:, b : b + col_count]
    return summed


def tap_grads(padded, grad_low, ids_pad, ids_mid, tap_size):
    margin = tap_size // 2
    row_count = ids_mid.shape[0]
    col_count = padded.shape[1]
    widened = jnp.pad(padded, ((0, 0), (margin, margin), (0, 0)))
    grad_vals = grad_low.astype(F32)
    results = []
    for a in range(tap_size):
        same_img = (ids_pad[a : a + row_count] == ids_mid)[:, None, None]
        shifted = jnp.where(same_img, widened[a : a + row_count].astype(F32), 0.0)
        for b in range(tap_size):
            results.append(jnp.sum(shifted[:, b : b + col_count] * grad_vals, axis=(0, 1)))
    return jnp.stack(results)


def gather_all(shard):
    full = lax.all_gather(shard, ALL, axis=0)
    return full.reshape(2, -1, shard.shape[1])


def reduce_all(first, second):
    both = jnp.concatenate([first.astype(BF), second.astype(BF)], axis=0)
    return lax.psum_scatter(both, ALL, scatter_dimension=0, tiled=True).astype(F32)


LANES = 128
RIM = 16
VMEM_LIMIT = 60 * 1024 * 1024


def conv_params(flops=0, moved=0):
    return dict(
        compiler_params=pltpu.CompilerParams(vmem_limit_bytes=VMEM_LIMIT),
        cost_estimate=pl.CostEstimate(flops=flops, bytes_accessed=moved, transcendentals=0),
    )


def masked_taps(taps_ref, mask_ref, km_ref, sub, flip):
    for a in range(7):
        seen = mask_ref[a, pl.ds(sub * 8, 8), :]
        for b in range(7):
            tap = 48 - (a * 7 + b) if flip else a * 7 + b
            km_ref[a * 7 + b] = taps_ref[tap : tap + 1, :] * seen


def conv_kernel(place_ref, x_ref, top_ref, bot_ref, taps_ref, mask_ref, out_ref, xs_ref, km_ref):
    rows, width = 48, x_ref.shape[1] // 48
    cb = pl.program_id(0)

    @pl.when(cb == 0)
    def _():
        for w in (0, 1, 2, 51, 52, 53):
            xs_ref[w] = jnp.zeros_like(xs_ref[w])

    def fill(w, carry):
        at = pl.ds(pl.multiple_of(w * width + cb * LANES, LANES), LANES)
        xs_ref[w + 3, 0:RIM, :] = top_ref[:, at].astype(F32)
        xs_ref[w + 3, RIM : RIM + rows, :] = x_ref[:, at].astype(F32)
        xs_ref[w + 3, RIM + rows :, :] = bot_ref[:, at].astype(F32)
        return carry

    lax.fori_loop(0, 48, fill, 0)

    def band(t, carry):
        for s in range(2):
            masked_taps(taps_ref, mask_ref, km_ref.at[s], t * 2 + s, False)

        def block(i, carry):
            w0 = i * 8
            accs = []
            for s in range(2):
                acc = [jnp.zeros((8, LANES), F32) for _ in range(8)]
                for a in range(7):
                    start = t * 16 + (s * 8 + RIM - 3 + a)
                    x = [xs_ref[w0 + j, pl.ds(start, 8), :] for j in range(14)]
                    for b in range(7):
                        k = km_ref[s, a * 7 + b]
                        for j in range(8):
                            acc[j] = acc[j] + k * x[j + b]
                accs.append(acc)
            for j in range(8):
                both = jnp.concatenate([accs[0][j], accs[1][j]], axis=0).astype(BF)
                out_ref[pl.ds(pl.multiple_of((w0 + j) * rows + t * 16, 16), 16), :] = both
            return carry

        lax.fori_loop(0, 6, block, 0)
        return carry

    lax.fori_loop(0, 3, band, 0)


def conv_forward(x, top, bot, taps, mask, place, into=None):
    width = x.shape[1] // 48
    blocks = width // LANES
    whole = lambda cb, place: (0, 0)
    half = lambda cb, place: (0, place[0] * blocks + cb)
    extra = [] if into is None else [into]
    kernel = conv_kernel if into is None else conv_kernel_into
    return pl.pallas_call(
        kernel,
        out_shape=jax.ShapeDtypeStruct((48 * 48, 2 * width), BF),
        grid_spec=pltpu.PrefetchScalarGridSpec(
            num_scalar_prefetch=1,
            grid=(blocks,),
            in_specs=[
                pl.BlockSpec(x.shape, whole),
                pl.BlockSpec(top.shape, whole),
                pl.BlockSpec(bot.shape, whole),
                pl.BlockSpec((49, LANES), half),
                pl.BlockSpec(mask.shape, lambda cb, place: (0, 0, 0)),
            ]
            + [pl.BlockSpec(memory_space=pl.ANY)] * len(extra),
            out_specs=pl.BlockSpec((48 * 48, LANES), half),
            scratch_shapes=[
                pltpu.VMEM((54, 80, LANES), F32),
                pltpu.VMEM((2, 49, 8, LANES), F32),
            ],
        ),
        input_output_aliases={} if into is None else {6: 0},
        **conv_params(2 * 49 * 48 * 48 * width * 8, 12_000_000),
    )(place, x, top, bot, taps, mask, *extra)


def conv_kernel_into(place_ref, x_ref, top_ref, bot_ref, taps_ref, mask_ref, into_ref, *rest):
    conv_kernel(place_ref, x_ref, top_ref, bot_ref, taps_ref, mask_ref, *rest)


def back_kernel(place_ref, g_ref, top_ref, bot_ref, x_ref, cot_ref, pool_ref, taps_ref, mask_ref,
                out_ref, tap_out_ref, gs_ref, km_ref, tacc_ref, sp_ref):
    rows, width = 48, x_ref.shape[1] // 48
    cb = pl.program_id(0)

    @pl.when(cb == 0)
    def _():
        for w in (0, 1, 2, 51, 52, 53):
            gs_ref[w] = jnp.zeros_like(gs_ref[w])

    tacc_ref[...] = jnp.zeros_like(tacc_ref)

    def fill(w, carry):
        gs_ref[w + 3, 0:RIM, :] = top_ref[pl.ds(pl.multiple_of(w * RIM, RIM), RIM), :].astype(F32)
        own = pl.ds(pl.multiple_of(w * rows, rows), rows)
        gs_ref[w + 3, RIM : RIM + rows, :] = g_ref[own, :].astype(F32)
        gs_ref[w + 3, RIM + rows :, :] = bot_ref[pl.ds(pl.multiple_of(w * RIM, RIM), RIM), :].astype(F32)
        return carry

    lax.fori_loop(0, 48, fill, 0)

    def spread(q, carry):
        quarter = pool_ref[q] * 0.25
        sp_ref[q, pl.ds(0, 24, stride=2), :] = quarter
        sp_ref[q, pl.ds(1, 24, stride=2), :] = quarter
        return carry

    lax.fori_loop(0, 24, spread, 0)

    def band(t, carry):
        for s in range(2):
            masked_taps(taps_ref, mask_ref, km_ref.at[s], t * 2 + s, True)

        def block(i, carry):
            w0 = i * 8
            ats = [
                pl.ds(pl.multiple_of((w0 + j) * width + cb * LANES, LANES), LANES) for j in range(8)
            ]
            band_rows = pl.ds(pl.multiple_of(t * 16, 16), 16)
            vals = [x_ref[band_rows, at].astype(F32) for at in ats]
            accs = []
            for s in range(2):
                acc = [jnp.zeros((8, LANES), F32) for _ in range(8)]
                v = [val[s * 8 : s * 8 + 8] for val in vals]
                for a in range(7):
                    start = t * 16 + (s * 8 + RIM - 3 + a)
                    g = [gs_ref[w0 + j, pl.ds(start, 8), :] for j in range(14)]
                    seen = mask_ref[a, pl.ds(t * 16 + s * 8, 8), :]
                    vm = [item * seen for item in v]
                    for b in range(7):
                        k = km_ref[s, a * 7 + b]
                        tap = None
                        for j in range(8):
                            acc[j] = acc[j] + k * g[j + b]
                            term = vm[j] * g[j + b]
                            tap = term if tap is None else tap + term
                        tacc_ref[48 - (a * 7 + b)] += tap
                accs.append(acc)
            for j in range(8):
                both = jnp.concatenate([accs[0][j], accs[1][j]], axis=0)
                total = both + cot_ref[band_rows, ats[j]].astype(F32)
                total = total + sp_ref[i * 4 + j // 2, band_rows, :]
                out_ref[0, band_rows, ats[j]] = total.astype(out_ref.dtype)
            return carry

        lax.fori_loop(0, 6, block, 0)
        return carry

    lax.fori_loop(0, 3, band, 0)
    tap_out_ref[0:49, :] = jnp.sum(tacc_ref[...], axis=1)


def conv_backward(grad, top, bot, x, cot, pool, taps, mask, place, slots, kind):
    width = x.shape[1] // 48
    blocks = width // LANES
    whole = lambda cb, place: (0, 0)
    half = lambda cb, place: (0, place[0] * blocks + cb)
    return pl.pallas_call(
        back_kernel,
        out_shape=(
            jax.ShapeDtypeStruct((slots, *x.shape), kind),
            jax.ShapeDtypeStruct((56, width), F32),
        ),
        grid_spec=pltpu.PrefetchScalarGridSpec(
            num_scalar_prefetch=1,
            grid=(blocks,),
            in_specs=[
                pl.BlockSpec((48 * 48, LANES), half),
                pl.BlockSpec((48 * RIM, LANES), half),
                pl.BlockSpec((48 * RIM, LANES), half),
                pl.BlockSpec(x.shape, whole),
                pl.BlockSpec(cot.shape, whole),
                pl.BlockSpec((24, 24, LANES), lambda cb, place: (0, 0, place[0] * blocks + cb)),
                pl.BlockSpec((49, LANES), half),
                pl.BlockSpec(mask.shape, lambda cb, place: (0, 0, 0)),
            ],
            out_specs=(
                pl.BlockSpec((1, *x.shape), lambda cb, place: (place[0] if slots == 2 else 0, 0, 0)),
                pl.BlockSpec((56, LANES), lambda cb, place: (0, cb)),
            ),
            scratch_shapes=[
                pltpu.VMEM((54, 80, LANES), F32),
                pltpu.VMEM((2, 49, 8, LANES), F32),
                pltpu.VMEM((49, 8, LANES), F32),
                pltpu.VMEM((24, 48, LANES), F32),
            ],
        ),
        **conv_params(4 * 49 * 48 * 48 * width * 8, 25_000_000),
    )(place, grad, top, bot, x, cot, pool, taps, mask)


def join_kernel(place_ref, branch_ref, scale_ref, own_ref, other_ref, own_out, other_out, pool_out, pair_ref):
    rows, width = 48, own_ref.shape[1] // 4
    for g, (src, dst) in enumerate(((own_ref, own_out), (other_ref, other_out))):
        side = place_ref[0] if g == 0 else 1 - place_ref[0]
        at = pl.ds(pl.multiple_of(side * width, LANES), width)
        scale = scale_ref[:, at]
        for q in range(2):
            total = None
            for w in (2 * q, 2 * q + 1):
                field = src[:, w * width : (w + 1) * width].astype(F32)
                field = field + scale * branch_ref[w * rows : (w + 1) * rows, at]
                dst[0, :, w * width : (w + 1) * width] = field.astype(BF)
                total = field if total is None else total + field
            for n in range(width // LANES):
                pair_ref[q, n] = total[:, n * LANES : (n + 1) * LANES]
                even = pair_ref[q, n, pl.ds(0, 24, stride=2), :]
                odd = pair_ref[q, n, pl.ds(1, 24, stride=2), :]
                lane = pl.ds(pl.multiple_of(side * width + n * LANES, LANES), LANES)
                pool_out[q, :, lane] = (even + odd) * 0.25


def join_branch(branch, scale, own, other, place):
    width = own.shape[1] // 48
    raw = pl.BlockSpec((48, 4 * width), lambda i, place: (0, i))
    return pl.pallas_call(
        join_kernel,
        out_shape=(
            jax.ShapeDtypeStruct((2, *own.shape), BF),
            jax.ShapeDtypeStruct((1, *own.shape), BF),
            jax.ShapeDtypeStruct((24, 24, 2 * width), F32),
        ),
        grid_spec=pltpu.PrefetchScalarGridSpec(
            num_scalar_prefetch=1,
            grid=(12,),
            in_specs=[
                pl.BlockSpec((4 * 48, 2 * width), lambda i, place: (i, 0)),
                pl.BlockSpec((1, 2 * width), lambda i, place: (0, 0)),
                raw,
                raw,
            ],
            out_specs=(
                pl.BlockSpec((1, 48, 4 * width), lambda i, place: (place[0], 0, i)),
                pl.BlockSpec((1, 48, 4 * width), lambda i, place: (0, 0, i)),
                pl.BlockSpec((2, 24, 2 * width), lambda i, place: (i, 0, 0)),
            ),
            scratch_shapes=[pltpu.VMEM((2, width // LANES, 48, LANES), F32)],
        ),
        **conv_params(10_000_000, 40_000_000),
    )(place, branch, scale, own, other)


def scaled_kernel(place_ref, pool_ref, branch_ref, scale_ref, own_ref, other_ref, out_ref, sum_ref, pair_ref):
    rows, width = 48, own_ref.shape[1] // 4

    @pl.when(pl.program_id(0) == 0)
    def _():
        sum_ref[...] = jnp.zeros_like(sum_ref)

    for g, src in enumerate((own_ref, other_ref)):
        side = place_ref[0] if g == 0 else 1 - place_ref[0]
        at = pl.ds(pl.multiple_of(side * width, LANES), width)
        scale = scale_ref[:, at]
        for q in range(2):
            quarter = pool_ref[q, :, at] * 0.25
            for n in range(width // LANES):
                part = quarter[:, n * LANES : (n + 1) * LANES]
                pair_ref[q, n, pl.ds(0, 24, stride=2), :] = part
                pair_ref[q, n, pl.ds(1, 24, stride=2), :] = part
            spread = jnp.concatenate([pair_ref[q, n] for n in range(width // LANES)], axis=1)
            for w in (2 * q, 2 * q + 1):
                here = slice(w * rows, (w + 1) * rows)
                grad = src[:, w * width : (w + 1) * width].astype(F32) + spread
                part = grad * branch_ref[here, at]
                sum_ref[:, at] += jnp.sum(part.reshape(6, 8, width), axis=0)
                out_ref[here, at] = (grad * scale).astype(BF)


def scaled_grads(pool, branch, scale, own, other, place):
    width = own.shape[1] // 48
    raw = pl.BlockSpec((48, 4 * width), lambda i, place: (0, i))
    return pl.pallas_call(
        scaled_kernel,
        out_shape=(
            jax.ShapeDtypeStruct(branch.shape, BF),
            jax.ShapeDtypeStruct((8, 2 * width), F32),
        ),
        grid_spec=pltpu.PrefetchScalarGridSpec(
            num_scalar_prefetch=1,
            grid=(12,),
            in_specs=[
                pl.BlockSpec((2, 24, 2 * width), lambda i, place: (i, 0, 0)),
                pl.BlockSpec((4 * 48, 2 * width), lambda i, place: (i, 0)),
                pl.BlockSpec((1, 2 * width), lambda i, place: (0, 0)),
                raw,
                raw,
            ],
            out_specs=(
                pl.BlockSpec((4 * 48, 2 * width), lambda i, place: (i, 0)),
                pl.BlockSpec((8, 2 * width), lambda i, place: (0, 0)),
            ),
            scratch_shapes=[pltpu.VMEM((2, width // LANES, 48, LANES), F32)],
        ),
        **conv_params(10_000_000, 40_000_000),
    )(place, pool, branch, scale, own, other)


CHUNK = 256
NT = (((1,), (1,)), ((), ()))
TN = (((0,), (0,)), ((), ()))


def dot(left, right, dims):
    return lax.dot_general(left, right, dims, preferred_element_type=F32)


NN = (((1,), (0,)), ((), ()))


def lane_half(shape, side):
    lanes = lax.broadcasted_iota(jnp.int32, shape, len(shape) - 1)
    return (lanes < 64) if side == 0 else (lanes >= 64)


def fill_window(win_ref, before, own, after):
    count = own.shape[0]
    win_ref[0:count] = before[...]
    win_ref[count : 2 * count] = own[...]
    win_ref[2 * count : 3 * count] = after[...]
    win_ref[3 * count :] = jnp.zeros_like(win_ref[3 * count :])


def attend_kernel(first_ref, last_ref, q_ref, kb_ref, k_ref, ka_ref, vb_ref, v_ref, va_ref,
                  klab_ref, qlab_ref, out_ref, total_ref, kw_ref, vw_ref):
    fill_window(kw_ref, kb_ref, k_ref, ka_ref)
    fill_window(vw_ref, vb_ref, v_ref, va_ref)
    for n in range(3):
        rows = slice(n * 192, (n + 1) * 192)
        q = q_ref[rows, :] * jnp.asarray(0.125, BF)
        q_half = [jnp.where(lane_half(q.shape, side), q, jnp.zeros_like(q)) for side in range(2)]
        q_lab = qlab_ref[n, 0:1, :]

        def chunk(c, carry):
            at = pl.ds(pl.multiple_of(c * CHUNK, CHUNK), CHUNK)
            kc, vc = kw_ref[at, :], vw_ref[at, :]
            same = klab_ref[at, 0:1] == q_lab
            new = []
            for side in range(2):
                top, total, acc = carry[side]
                s = jnp.where(same, dot(kc, q_half[side], NT), NEG)
                best = jnp.maximum(top, jnp.max(s, axis=0, keepdims=True))
                p = jnp.exp(s - best)
                shrink = jnp.exp(top - best)
                total = total * shrink + jnp.sum(p, axis=0, keepdims=True)
                new.append((best, total, acc * shrink + dot(vc, p.astype(BF), TN)))
            return tuple(new)

        start = (jnp.full((1, 192), NEG, F32), jnp.zeros((1, 192), F32), jnp.zeros((LANES, 192), F32))
        done = lax.fori_loop(first_ref[n], last_ref[n], chunk, (start, start))
        outs = []
        for side in range(2):
            top, total, acc = done[side]
            outs.append(acc * (1.0 / total))
            total_ref[0, n, side : side + 1, :] = top + jnp.log(total)
        both = jnp.concatenate([outs[0][:64], outs[1][64:]], axis=0)
        out_ref[rows, :] = both.T.astype(BF)


def attend(q, k, v, around, qlab, klab, first, last):
    count, width = q.shape
    window = -(-3 * count // CHUNK) * CHUNK
    block = pl.BlockSpec((count, LANES), lambda p, *_: (0, p))
    stats = pl.BlockSpec((1, 3, 2, 192), lambda p, *_: (p, 0, 0, 0))
    return pl.pallas_call(
        attend_kernel,
        out_shape=(
            jax.ShapeDtypeStruct(q.shape, BF),
            jax.ShapeDtypeStruct((width // LANES, 3, 2, 192), F32),
        ),
        grid_spec=pltpu.PrefetchScalarGridSpec(
            num_scalar_prefetch=2,
            grid=(width // LANES,),
            in_specs=[block] * 7
            + [
                pl.BlockSpec(klab.shape, lambda p, *_: (0, 0)),
                pl.BlockSpec(qlab.shape, lambda p, *_: (0, 0, 0)),
            ],
            out_specs=(block, stats),
            scratch_shapes=[pltpu.VMEM((window, LANES), BF), pltpu.VMEM((window, LANES), BF)],
        ),
        **conv_params(20_000_000_000, 20_000_000),
    )(first, last, q, around[0], k, around[1], around[2], v, around[3], klab, qlab)


def attend_back_kernel(first_ref, last_ref, q_ref, kb_ref, k_ref, ka_ref, vb_ref, v_ref, va_ref,
                       do_ref, total_ref, delta_ref, klab_ref, qlab_ref,
                       dq_ref, dk_ref, dv_ref, before_ref, after_ref,
                       kw_ref, vw_ref, dkw_ref, dvw_ref):
    count = q_ref.shape[0]
    fill_window(kw_ref, kb_ref, k_ref, ka_ref)
    fill_window(vw_ref, vb_ref, v_ref, va_ref)
    dkw_ref[...] = jnp.zeros_like(dkw_ref)
    dvw_ref[...] = jnp.zeros_like(dvw_ref)
    for n in range(3):
        rows = slice(n * 192, (n + 1) * 192)
        q = q_ref[rows, :] * jnp.asarray(0.125, BF)
        do = do_ref[rows, :]
        masks = [lane_half((192, LANES), side) for side in range(2)]
        q_half = [jnp.where(m, q, jnp.zeros_like(q)) for m in masks]
        do_half = [jnp.where(m, do, jnp.zeros_like(do)) for m in masks]
        q_lab = qlab_ref[n, 0:1, :]

        def chunk(c, dq):
            at = pl.ds(pl.multiple_of(c * CHUNK, CHUNK), CHUNK)
            kc, vc = kw_ref[at, :], vw_ref[at, :]
            same = klab_ref[at, 0:1] == q_lab
            ks = [jnp.where(lane_half((CHUNK, LANES), side), kc, jnp.zeros_like(kc)) for side in range(2)]
            dk, dv = dkw_ref[at, :], dvw_ref[at, :]
            for side in range(2):
                s = dot(kc, q_half[side], NT)
                p = jnp.exp(jnp.where(same, s - total_ref[0, n, side : side + 1, :], NEG))
                dp = dot(vc, do_half[side], NT)
                ds = (p * (dp - delta_ref[0, n, side : side + 1, :])).astype(BF)
                dv = dv + dot(p.astype(BF), do_half[side], NN)
                dk = dk + dot(ds, q_half[side], NN)
                dq = dq + dot(ds, ks[side], TN)
            dkw_ref[at, :] = dk
            dvw_ref[at, :] = dv
            return dq

        dq = lax.fori_loop(first_ref[n], last_ref[n], chunk, jnp.zeros((192, LANES), F32))
        dq_ref[rows, :] = (dq * 0.125).astype(BF)
    dk_ref[...] = dkw_ref[count : 2 * count, :]
    dv_ref[...] = dvw_ref[count : 2 * count, :]
    before_ref[0] = dkw_ref[0:count, :].astype(BF)
    before_ref[1] = dvw_ref[0:count, :].astype(BF)
    after_ref[0] = dkw_ref[2 * count : 3 * count, :].astype(BF)
    after_ref[1] = dvw_ref[2 * count : 3 * count, :].astype(BF)


def attend_back(q, k, v, around, grad, total, delta, qlab, klab, first, last):
    count, width = q.shape
    window = -(-3 * count // CHUNK) * CHUNK
    block = pl.BlockSpec((count, LANES), lambda p, *_: (0, p))
    stats = pl.BlockSpec((1, 3, 2, 192), lambda p, *_: (p, 0, 0, 0))
    pair = pl.BlockSpec((2, count, LANES), lambda p, *_: (0, 0, p))
    return pl.pallas_call(
        attend_back_kernel,
        out_shape=(
            jax.ShapeDtypeStruct(q.shape, BF),
            jax.ShapeDtypeStruct(q.shape, F32),
            jax.ShapeDtypeStruct(q.shape, F32),
            jax.ShapeDtypeStruct((2, count, width), BF),
            jax.ShapeDtypeStruct((2, count, width), BF),
        ),
        grid_spec=pltpu.PrefetchScalarGridSpec(
            num_scalar_prefetch=2,
            grid=(width // LANES,),
            in_specs=[block] * 8
            + [
                stats,
                stats,
                pl.BlockSpec(klab.shape, lambda p, *_: (0, 0)),
                pl.BlockSpec(qlab.shape, lambda p, *_: (0, 0, 0)),
            ],
            out_specs=(block, block, block, pair, pair),
            scratch_shapes=[
                pltpu.VMEM((window, LANES), BF),
                pltpu.VMEM((window, LANES), BF),
                pltpu.VMEM((window, LANES), F32),
                pltpu.VMEM((window, LANES), F32),
            ],
        ),
        **conv_params(20_000_000_000, 20_000_000),
    )(first, last, q, around[0], k, around[1], around[2], v, around[3], grad, total, delta, klab, qlab)


def on_device(
    lo_in,
    hi_in,
    image_ids,
    cn_kernel,
    cn_gain,
    cn_w1,
    cn_w2,
    cn_scale,
    ad_proj,
    ad_kernel,
    gate_w1,
    gate_w2,
    ln1_gain,
    qkv,
    out_proj,
    ln2_gain,
    fc1,
    fc2,
    d_lo_out,
    d_hi_out,
):
    micro_count, row_count, col_count, d_shard = lo_in.shape
    hi_rows = hi_in.shape[1]
    hi_cols = HCOLS
    c_shard = hi_in.shape[3] // hi_cols
    d_own, c_own = 2 * d_shard, 2 * c_shard
    tok_count = row_count * col_count
    pix_count = hi_rows * hi_cols
    mine = lax.axis_index("mb")
    row_start = lax.axis_index("tile") * row_count
    head_count = d_own // HDIM

    fast = c_shard % LANES == 0 and lax.axis_size("tp") == 1
    hi_raw = hi_in.reshape(2, hi_rows, hi_cols * c_shard)
    hi_own, hi_other = swap_micro(hi_raw)
    up, down = rim_pair(hi_raw, 3, 1)
    own_rims, other_rims = swap_micro(jnp.stack([up, down], axis=1))
    cot_own, cot_other = swap_micro(d_hi_out.reshape(2, hi_rows, hi_cols * c_shard))
    lo_low = in_order(*swap_micro(lo_in.reshape(2, tok_count, d_shard)), 1)
    lo_field = lo_low.astype(F32)

    mlp_in = gather_all(cn_w1)
    mlp_out = gather_all(cn_w2.T)
    ad_gate = gather_all(jnp.concatenate([ad_proj, gate_w1], axis=1))
    ad_matrix = [ad_gate[g, :, :d_shard] for g in range(2)]
    gate_in = [ad_gate[g, :, d_shard:] for g in range(2)]
    gh_shard = gate_w1.shape[1]
    ff_shard = fc1.shape[1]
    vit = gather_all(
        jnp.concatenate([gate_w2.T, qkv[0], qkv[1], qkv[2], out_proj.T, fc1, fc2.T], axis=1)
    )
    cuts = np.cumsum([0, gh_shard, d_shard, d_shard, d_shard, d_shard, ff_shard, ff_shard])
    gate_out, q_w, k_w, v_w, out_w, ff_in, ff_out = [
        [vit[g, :, int(cuts[i]) : int(cuts[i + 1])] for g in range(2)] for i in range(7)
    ]

    def apply(left, pair):
        return jnp.concatenate([matmul(left, pair[0]), matmul(left, pair[1])], axis=1)

    def apply_t(left, pair):
        width = pair[0].shape[1]
        return matmul_nt(left[:, :width], pair[0]) + matmul_nt(left[:, width:], pair[1])

    def cols(values):
        width = values.shape[1] // 2
        return [values[:, :width], values[:, width:]]

    canvas_ids = lax.dynamic_index_in_dim(image_ids, mine, 0, keepdims=False)
    small_ids = row_labels(canvas_ids, row_start, row_count, 1)
    lo_mid = small_ids[1 : 1 + row_count]
    hi_ids = row_labels(jnp.repeat(canvas_ids, 2), 2 * row_start, hi_rows, 3)
    hi_mid = hi_ids[3 : 3 + hi_rows]

    def both_shards(shard, axis):
        return in_order(shard, lax.ppermute(shard, "mb", SWAP), axis)

    conv_taps = both_shards(cn_kernel, 1)
    ad_taps = both_shards(ad_kernel, 1)
    hi_scale = both_shards(cn_scale, 0).astype(F32)

    own_place = mine.reshape(1).astype(jnp.int32)
    other_place = 1 - own_place
    own_rims, other_rims = [
        (jnp.pad(rims[0], ((RIM - 3, 0), (0, 0))), jnp.pad(rims[1], ((0, RIM - 3), (0, 0))))
        for rims in (own_rims, other_rims)
    ]
    seen = jnp.stack([(hi_ids[a : a + hi_rows] == hi_mid).astype(F32) for a in range(7)])
    mask = jnp.broadcast_to(seen[:, :, None], (7, hi_rows, LANES))
    wide_taps = conv_taps.astype(F32)

    def natural(own, other):
        shape = (-1, hi_cols, c_shard)
        return in_order(own.reshape(shape), other.reshape(shape), 2)

    if fast:
        conv_flat = conv_forward(hi_own, *own_rims, wide_taps, mask, own_place)
        conv_flat = conv_forward(hi_other, *other_rims, wide_taps, mask, other_place, conv_flat)
    else:
        hi_field = natural(hi_own, hi_other)
        hi_pad = jnp.concatenate(
            [
                natural(own_rims[0], other_rims[0])[-3:],
                hi_field,
                natural(own_rims[1], other_rims[1])[:3],
            ]
        )
        conv_low = depthwise(hi_pad, conv_taps, hi_ids, hi_mid, 7, False).astype(BF)
        conv_flat = conv_low.transpose(1, 0, 2).reshape(pix_count, c_own)
    conv_full = features(conv_flat)
    normed, norm_pull = jax.vjp(layer_norm, conv_full.astype(F32), cn_gain.astype(F32))
    normed_low = lax.optimization_barrier(normed.astype(BF))
    inner_act, inner_slope = zip(*[gelu_pair(matmul(normed_low, mlp_in[g])) for g in range(2)])
    branch = partial_sums(
        matmul_nt(inner_act[0], mlp_out[0]) + matmul_nt(inner_act[1], mlp_out[1])
    )
    if fast:
        hi_mine, hi_sent, pooled = join_branch(branch, hi_scale[None], hi_own, hi_other, own_place)
        pooled = pooled.transpose(1, 0, 2)
    else:
        branch_rows = branch.reshape(hi_cols, hi_rows, c_own).transpose(1, 0, 2)
        hi_sum = hi_field.astype(F32) + hi_scale * branch_rows
        pooled = jnp.mean(hi_sum.reshape(row_count, 2, col_count, 2, c_own), axis=(1, 3))
    pooled_full = features(pooled.reshape(tok_count, c_own).astype(BF))
    proj_low = apply(pooled_full, ad_matrix).astype(BF)
    proj_pad = rim_rows(proj_low.reshape(row_count, col_count, d_own), 1)
    local_conv = depthwise(proj_pad, ad_taps, small_ids, lo_mid, 3, False).reshape(
        tok_count, d_own
    )
    gate_hidden, gate_slope = gelu_pair(apply(pooled_full, gate_in))
    gate_val = jnp.tanh(partial_sums(apply_t(gate_hidden, gate_out)))
    mixed_one = lo_field + gate_val * local_conv
    mixed_full = features(mixed_one.astype(BF))
    norm_one, first_pull = jax.vjp(layer_norm, mixed_full.astype(F32), ln1_gain.astype(F32))
    norm_low = norm_one.astype(BF)
    queries = apply(norm_low, q_w).astype(BF)
    key_rows = apply(norm_low, k_w).astype(BF)
    value_rows = apply(norm_low, v_w).astype(BF)
    key_value = jnp.concatenate([key_rows, value_rows], axis=1)
    kv_before, kv_after = rim_pair(key_value, tok_count, 0)
    around = (kv_before[:, :d_own], kv_after[:, :d_own], kv_before[:, d_own:], kv_after[:, d_own:])
    near = row_labels(canvas_ids, row_start, row_count, row_count)
    key_tok = jnp.repeat(near, col_count)
    window = -(-3 * tok_count // CHUNK) * CHUNK
    key_tok = jnp.pad(key_tok, (0, window - 3 * tok_count), constant_values=-2)
    key_lab = jnp.broadcast_to(key_tok[:, None], (window, LANES))
    query_lab = jnp.broadcast_to(jnp.repeat(lo_mid, col_count).reshape(3, 1, 192), (3, 8, 192))
    edge = jnp.arange(3 * row_count)
    first_row = jnp.min(jnp.where(near[None] == lo_mid[::8][:, None], edge, 3 * row_count), axis=1)
    last_row = jnp.max(jnp.where(near[None] == lo_mid[7::8][:, None], edge, -1), axis=1) + 1
    first = (first_row * col_count // CHUNK).astype(jnp.int32)
    last = ((last_row * col_count + CHUNK - 1) // CHUNK).astype(jnp.int32)
    attended, log_total = attend(
        queries, key_rows, value_rows, around, query_lab, key_lab, first, last
    )
    mixed_two = mixed_one + partial_sums(apply_t(attended, out_w))
    mixed2_full = features(mixed_two.astype(BF))
    norm_two, second_pull = jax.vjp(layer_norm, mixed2_full.astype(F32), ln2_gain.astype(F32))
    norm2_low = norm_two.astype(BF)
    ff_hidden, ff_slope = gelu_pair(apply(norm2_low, ff_in))
    lo_result = (mixed_two + partial_sums(apply_t(ff_hidden, ff_out))).astype(BF)

    grad_low = in_order(*swap_micro(d_lo_out.reshape(2, tok_count, d_shard)), 1)
    grad_out = grad_low.astype(F32)
    ff_grad_full = features(grad_low)
    ff_pre_grad = (apply(ff_grad_full, ff_out) * ff_slope.astype(F32)).astype(BF)
    second_grad = partial_sums(apply_t(ff_pre_grad, ff_in)).astype(BF)
    g_ff = reduce_all(
        *[
            jnp.concatenate([matmul_tn(norm2_low, i), matmul_tn(ff_grad_full, o)], axis=1)
            for i, o in zip(cols(ff_pre_grad), cols(ff_hidden))
        ]
    )
    back_two, grad_ln2 = second_pull(features(second_grad).astype(F32))
    grad_two = grad_out + own_slice(back_two)
    att_grad_full = features(grad_two.astype(BF))
    att_grad = apply(att_grad_full, out_w).astype(BF)
    inner = (att_grad.astype(F32) * attended.astype(F32)).reshape(3, 192, head_count // 2, 2, HDIM)
    delta = jnp.sum(inner, axis=-1).transpose(2, 0, 3, 1)
    query_grad, key_own, value_own, to_before, to_after = attend_back(
        queries, key_rows, value_rows, around, att_grad, log_total, delta, query_lab, key_lab, first, last
    )
    devices = lax.axis_size("tile")
    steps = [(i, i + 1) for i in range(devices - 1)]
    from_before = lax.ppermute(to_after, "tile", steps)
    from_after = lax.ppermute(to_before, "tile", [(j, i) for i, j in steps])
    key_grad, value_grad = [
        (own + from_before[i].astype(F32) + from_after[i].astype(F32)).astype(BF)
        for i, own in enumerate((key_own, value_own))
    ]
    first_grad = partial_sums(
        apply_t(query_grad, q_w) + apply_t(key_grad, k_w) + apply_t(value_grad, v_w)
    ).astype(BF)
    back_one, grad_ln1 = first_pull(features(first_grad).astype(F32))
    grad_one = grad_two + own_slice(back_one)
    gate_pre_grad = (grad_one * local_conv * (1.0 - gate_val * gate_val)).astype(BF)
    gate_grad_full = features(gate_pre_grad)
    g_att = reduce_all(
        *[
            jnp.concatenate(
                [
                    matmul_tn(gate_grad_full, h),
                    matmul_tn(norm_low, q),
                    matmul_tn(norm_low, k),
                    matmul_tn(norm_low, v),
                    matmul_tn(att_grad_full, o),
                ],
                axis=1,
            )
            for h, q, k, v, o in zip(
                cols(gate_hidden), cols(query_grad), cols(key_grad), cols(value_grad), cols(attended)
            )
        ]
    )
    hidden_grad = (apply(gate_grad_full, gate_out) * gate_slope.astype(F32)).astype(BF)
    local_grad = (grad_one * gate_val).astype(BF).reshape(row_count, col_count, d_own)
    local_pad = rim_rows(local_grad, 1)
    proj_grad = (
        depthwise(local_pad, ad_taps, small_ids, lo_mid, 3, True)
        .reshape(tok_count, d_own)
        .astype(BF)
    )
    grad_ad_kernel = tap_grads(proj_pad, local_grad, small_ids, lo_mid, 3)
    g_ad = reduce_all(
        *[
            jnp.concatenate([matmul_tn(pooled_full, p), matmul_tn(pooled_full, h)], axis=1)
            for p, h in zip(cols(proj_grad), cols(hidden_grad))
        ]
    )
    pooled_grad = partial_sums(apply_t(hidden_grad, gate_in) + apply_t(proj_grad, ad_matrix))
    pool_cols = pooled_grad.reshape(row_count, col_count, c_own).transpose(1, 0, 2)
    if fast:
        scaled_grad, scale_parts = scaled_grads(
            pool_cols, branch, hi_scale[None], cot_own, cot_other, own_place
        )
        grad_scale = jnp.sum(scale_parts, axis=0)
    else:
        spread_grad = jnp.repeat(jnp.repeat(pool_cols.transpose(1, 0, 2) * 0.25, 2, 0), 2, 1)
        hi_grad = natural(cot_own, cot_other).astype(F32) + spread_grad
        grad_cols = hi_grad.transpose(1, 0, 2).reshape(pix_count, c_own)
        grad_scale = jnp.sum(grad_cols * branch, axis=0)
        scaled_grad = (grad_cols * hi_scale).astype(BF)
    branch_full = lax.optimization_barrier(features(scaled_grad))
    g_w2 = reduce_all(*[matmul_tn(branch_full, act) for act in inner_act])
    inner_grad = [
        (matmul(branch_full, mlp_out[g]) * inner_slope[g].astype(F32)).astype(BF) for g in range(2)
    ]
    g_w1 = reduce_all(*[matmul_tn(normed_low, grad) for grad in inner_grad])
    normed_grad = partial_sums(
        matmul_nt(inner_grad[0], mlp_in[0]) + matmul_nt(inner_grad[1], mlp_in[1])
    ).astype(BF)
    back_conv, grad_cn_gain = norm_pull(features(normed_grad).astype(F32))
    conv_grad = own_slice(back_conv).astype(BF)
    conv_cols = conv_grad.reshape(hi_cols, hi_rows, c_own)
    grad_up, grad_down = rim_pair(conv_cols, 3, 1)
    if fast:
        grad_rims = [
            jnp.pad(rim, ((0, 0), side, (0, 0))).reshape(hi_cols * RIM, c_own)
            for rim, side in ((grad_up, (RIM - 3, 0)), (grad_down, (0, RIM - 3)))
        ]
        ghi_sent, taps_other = conv_backward(
            conv_grad, *grad_rims, hi_other, cot_other, pool_cols, wide_taps, mask, other_place, 1, BF
        )
        ghi_mine, taps_own = conv_backward(
            conv_grad, *grad_rims, hi_own, cot_own, pool_cols, wide_taps, mask, own_place, 2, F32
        )
        grad_cn_kernel = in_order(taps_own[:49], taps_other[:49], 1)
    else:
        conv_grad = conv_cols.transpose(1, 0, 2)
        conv_pad = jnp.concatenate(
            [grad_up.transpose(1, 0, 2), conv_grad, grad_down.transpose(1, 0, 2)]
        )
        hi_back = hi_grad + depthwise(conv_pad, conv_taps, hi_ids, hi_mid, 7, True)
        grad_cn_kernel = tap_grads(hi_pad, conv_grad, hi_ids, hi_mid, 7)

    def leave(values, kind):
        own, sent = halves(values)
        other = lax.ppermute(sent.astype(BF), "mb", SWAP)
        return both_micro(own.astype(kind), other.astype(kind))

    lo_stack = leave(lo_result.reshape(row_count, col_count, d_own), BF)
    if fast:
        hi_stack, ghi_stack = [
            lax.dynamic_update_slice_in_dim(
                stack, lax.ppermute(sent, "mb", SWAP).astype(stack.dtype), 1 - mine, 0
            )
            for stack, sent in ((hi_mine, hi_sent), (ghi_mine, ghi_sent))
        ]
    else:
        hi_stack = leave(hi_sum, BF)
        ghi_stack = leave(hi_back, F32)
    glo_stack = leave(grad_one.reshape(row_count, col_count, d_own), F32)

    flat_terms = [grad_cn_kernel, grad_scale, grad_ad_kernel, grad_cn_gain, grad_ln1, grad_ln2]
    sizes = np.cumsum([0] + [item.size for item in flat_terms])
    total = lax.psum(
        jnp.concatenate([item.reshape(-1).astype(BF) for item in flat_terms]), ALL
    ).astype(F32)
    sums = [
        total[int(sizes[i]) : int(sizes[i + 1])].reshape(item.shape)
        for i, item in enumerate(flat_terms)
    ]
    g_kernel, g_scale, g_taps = [halves(item)[0] for item in sums[:3]]
    gain_sums = sums[3:]

    g_gate_w1 = g_ad[:, d_shard:]
    g_gate_w2 = g_att[:, :gh_shard].T
    g_qkv = jnp.stack([g_att[:, gh_shard + j * d_shard : gh_shard + (j + 1) * d_shard] for j in range(3)])
    g_out = g_att[:, gh_shard + 3 * d_shard :].T
    return (
        lo_stack,
        hi_stack.reshape(2, hi_rows, 1, hi_cols * c_shard),
        glo_stack,
        ghi_stack.reshape(2, hi_rows, 1, hi_cols * c_shard),
        g_kernel,
        gain_sums[0],
        g_w1,
        g_w2.T,
        g_scale,
        g_ad[:, :d_shard],
        g_taps,
        g_gate_w1,
        g_gate_w2,
        gain_sums[1],
        g_qkv,
        g_out,
        gain_sums[2],
        g_ff[:, :ff_shard],
        g_ff[:, ff_shard:].T,
    )


def solution(mesh):
    tiles, mps = mesh.shape["tile"], mesh.shape["mp"]
    fine = Mesh(mesh.devices.reshape(tiles, 2, mps // 2), ("tile", "mb", "tp"))
    mp = ("mb", "tp")
    in_specs = (
        P(None, "tile", None, mp),
        P(None, "tile", mp, None),
        P(),
        P(None, mp),
        P(),
        P("tile", mp),
        P(mp, "tile"),
        P(mp),
        P("tile", mp),
        P(None, mp),
        P("tile", mp),
        P(mp, "tile"),
        P(),
        P(None, "tile", mp),
        P(mp, "tile"),
        P(),
        P("tile", mp),
        P(mp, "tile"),
        P(None, "tile", None, mp),
        P(None, "tile", mp, None),
    )
    out_specs = (
        P(None, "tile", None, mp),
        P(None, "tile", mp, None),
        P(None, "tile", None, mp),
        P(None, "tile", mp, None),
        P(None, mp),
        P(),
        P("tile", mp),
        P(mp, "tile"),
        P(mp),
        P("tile", mp),
        P(None, mp),
        P("tile", mp),
        P(mp, "tile"),
        P(),
        P(None, "tile", mp),
        P(mp, "tile"),
        P(),
        P("tile", mp),
        P(mp, "tile"),
    )
    return jax.shard_map(
        on_device, mesh=fine, in_specs=in_specs, out_specs=out_specs, check_vma=False
    )
```

time: 5720 us -> 2290 us (0.40)
  waiting for transfers between devices: 2960 us -> 847 us
  other arithmetic: 1290 us -> 255 us
  matrix products: 976 us -> 518 us
  Pallas kernels: 0 us -> 345 us
  local copies, waits for them, and re-layouts: 290 us -> 180 us
  blocking collectives: 84.5 us -> 0 us
    reduce_scatter x34 -> x3, waiting for transfers between devices: 1970 us -> 431 us  [reduce_all(): lax.psum_scatter(both, ALL, scatter_dimension=0, tiled=True).astype(F32)]
    all_gather x30 -> x4, waiting for transfers between devices: 952 us -> 131 us  [gather_all(): full = lax.all_gather(shard, ALL, axis=0)]
    dot_general x36 -> x22, matrix products: 563 us -> 190 us  [matmul(): return jnp.dot(left, right, preferred_element_type=F32)]
    pallas_call x0 -> x8, Pallas kernels: none -> 345 us  [the longest x2 120 us: conv_backward(): pl.pallas_call(back_kernel, out_shape=(jax.ShapeDtypeStruct((slots, *x.sh...]
    convert_element_type x58 -> x22, other arithmetic: 376 us -> 40 us  [the longest x1 6.04 us: on_device(): (apply(ff_grad_full, ff_out) * ff_slope.astype(F32)).astype(BF)]
    reduce_sum x10 -> x1, other arithmetic: 302 us -> 3.19 us  [tap_grads(): jnp.sum(shifted[:, b:b + col_count] * grad_vals, axis=(0, 1))]
    add x15 -> x1, other arithmetic: 289 us -> 3.87 us  [depthwise(): summed + kernel[tap_index].astype(F32) * shifted[:, b:b + col_count]]
    ppermute x28 -> x24, waiting for transfers between devices: 10.2 us -> 283 us  [the longest x2 120 us: leave(): other = lax.ppermute(sent.astype(BF), 'mb', SWAP)]
  transfers between devices with their start and end apart: 93 -> 34, of which waited for: 61 -> 11; matrix products, arithmetic and copies ran while one was open for 22% -> 31% of each run, Pallas kernels for 0% -> 4%
where the time goes in v1:
time: 2290 us; the launch traced here: 2300 us
  waiting for transfers between devices  847 us (37%)
  matrix products  518 us (23%)
  Pallas kernels  345 us (15%)
  other arithmetic  255 us (11%)
  local copies, waits for them, and re-layouts  180 us (8%)
  starting transfers between devices  134 us (6%)
    reduce_scatter x3, waiting for transfers between devices, reduce_all(): lax.psum_scatter(both, ALL, scatter_dimension=0, tiled=True).astype(F32)  431 us
    dot_general x22, matrix products, matmul(): return jnp.dot(left, right, preferred_element_type=F32)  190 us
    dot_general x22, matrix products, matmul_nt(): lax.dot_general(left, right, (((1,), (1,)), ((), ())), preferred_element_...  179 us
    dot_general x22, matrix products, matmul_tn(): lax.dot_general(left, right, (((0,), (0,)), ((), ())), preferred_element_...  149 us
    concatenate x5, other arithmetic, reduce_all(): both = jnp.concatenate([first.astype(BF), second.astype(BF)], axis=0)  147 us
    all_gather x4, waiting for transfers between devices, gather_all(): full = lax.all_gather(shard, ALL, axis=0)  131 us
    pallas_call x2, Pallas kernels, conv_backward(): pl.pallas_call(back_kernel, out_shape=(jax.ShapeDtypeStruct((slots, *x.sh...  120 us
    ppermute x2, waiting for transfers between devices, leave(): other = lax.ppermute(sent.astype(BF), 'mb', SWAP)  120 us
  transfers between devices with their start and end apart: 34, of which 11 were waited for; matrix products, arithmetic and copies ran while one was open for 31% of the time, Pallas kernels for 4%

profile of v1, /device:TPU:0, one launch (start us, length us, event | category | flops | bytes accessed | tf_op | source)
XLA Modules:
  0.0 2295.8 jit_solution(9403474122423057921)
XLA Ops:
  76.8 53.9 %collective-permute-done.6 = bf16[768]{0:T(1024)(128)(2,1)} collective-permute-done((bf16[768]{0:T(1024)(128)(2,1)}, bf16[768]{0:T(1024)(128)(2,1)}, u32[]{:S(2)}, u32[]{:S(2)}) %collective-permute-start.6) | collective-permute-done | bytes 1568 | tf_op jit(solution)/shard_map/ppermute | solution.py:733
  151.2 35.7 %shard_map.339.into_ref = bf16[2304,1536]{1,0:T(8,128)(2,1)} custom-call(s32[1]{0:T(128)} %bitcast.3.place_ref, bf16[48,36864]{1,0:T(8,128)(2,1)} %get-tuple-element.181.x_ref.own_ref, bf16[16,36864]{1,0:T(8,128)(2,1)} %pad.49.top_ref, bf16[16,36864]{1,0:T(8,128)(2,1)} %pad.50.bot_ref, f32[49,1536]{1,0:T(8,128)} %maximum_convert_fusion.taps_ref, ...), custom_call_target="tpu_custom_call" | custom-call | flops 1387266048 | bytes 12000000 | tf_op jit(solution)/shard_map/pallas_call | solution.py:242
  194.6 35.4 %shard_map.340 = bf16[2304,1536]{1,0:T(8,128)(2,1)} custom-call(s32[1]{0:T(128)S(6)} %sub.55.place_ref, bf16[48,36864]{1,0:T(8,128)(2,1)} %copy-done.8, bf16[16,36864]{1,0:T(8,128)(2,1)} %pad.46.top_ref, bf16[16,36864]{1,0:T(8,128)(2,1)} %pad.47.bot_ref, f32[49,1536]{1,0:T(8,128)} %maximum_convert_fusion.taps_ref, ...), custom_call_target="tpu_custom_call", output_to_operand_aliasing={{}: (6, {})} | custom-call | flops 1387266048 | bytes 12000000 | tf_op jit(solution)/shard_map/pallas_call | solution.py:242
  242.9 32.7 %multiply_convert_fusion.3 = (bf16[2304,3072]{1,0:T(8,128)(2,1)}, f32[2304,3072]{1,0:T(8,128)}) fusion(bf16[2304,1536]{1,0:T(8,128)(2,1)} %fusion.16, bf16[3072,3072]{1,0:T(8,128)(2,1)} %all-gather.9.cloned.1.call-done), kind=kOutput, calls=%fused_computation.16 | convolution fusion | flops 21778661376 | bytes 58982400 | tf_op jit(solution)/shard_map/dot_general | solution.py:40
  304.9 29.9 %fusion.33 = f32[2304,1536]{1,0:T(8,128)} fusion(bf16[2304,3072]{1,0:T(8,128)(2,1)} %get-tuple-element.246, bf16[3072,3072]{1,0:T(8,128)(2,1)} %all-gather.11.cloned.1.call-done), kind=kOutput, calls=%fused_computation.62 | convolution fusion | flops 21743271936 | bytes 37748736 | tf_op jit(solution)/shard_map/dot_general | solution.py:48
  334.9 31.3 %multiply_convert_fusion.2 = (bf16[2304,3072]{1,0:T(8,128)(2,1)}, f32[2304,3072]{1,0:T(8,128)}) fusion(bf16[2304,1536]{1,0:T(8,128)(2,1)S(1)} %copy-done.27, bf16[3072,3072]{1,0:T(8,128)(2,1)} %all-gather.9.cloned.1.call-done), kind=kOutput, calls=%fused_computation.14 | convolution fusion | flops 21778661376 | bytes 58982400 | tf_op jit(solution)/shard_map/dot_general | solution.py:40
  366.2 30.8 %convolution_add_fusion.1.branch_ref = f32[2304,1536]{1,0:T(8,128)} fusion(f32[2304,1536]{1,0:T(8,128)} %fusion.33, bf16[2304,3072]{1,0:T(8,128)(2,1)} %get-tuple-element.248, bf16[3072,3072]{1,0:T(8,128)(2,1)} %all-gather.11.cloned.1.call-done), kind=kOutput, calls=%fused_computation.33 | convolution fusion | flops 21746810880 | bytes 51904512 | tf_op jit(solution)/shard_map/dot_general | solution.py:48
  435.6 102.1 %all-gather.15.cloned.1.call-done = bf16[2048,6528]{1,0:T(8,128)(2,1)} async-done(((bf16[64,6528]{1,0:T(8,128)(2,1)}), bf16[2048,6528]{1,0:T(8,128)(2,1)}) %all-gather.15.cloned.1.call-update) | async-done | bytes 26738704 | tf_op jit(solution)/shard_map/all_gather | solution.py:160
  585.0 62.0 %shard_map.342 = (bf16[576,1024]{1,0:T(8,128)(2,1)}, f32[8,3,2,192]{3,2,1,0:T(2,128)}) custom-call(s32[3]{0:T(128)} %get-tuple-element.260.first_ref, s32[3]{0:T(128)} %get-tuple-element.259.last_ref, bf16[576,1024]{1,0:T(8,128)(2,1)} %pad_maximum_fusion.7.q_ref, bf16[576,1024]{1,0:T(8,128)(2,1)} %get-tuple-element.192.kb_ref, ...), custom_call_target="tpu_custom_call" | custom-call | flops 20000000000 | bytes 20000000 | tf_op jit(solution)/shard_map/pallas_call | solution.py:554
  703.7 62.3 %shard_map.343 = (bf16[576,1024]{1,0:T(8,128)(2,1)}, f32[576,1024]{1,0:T(8,128)}, f32[576,1024]{1,0:T(8,128)}, bf16[2,576,1024]{2,1,0:T(8,128)(2,1)}, bf16[2,576,1024]{2,1,0:T(8,128)(2,1)}) custom-call(s32[3]{0:T(128)} %get-tuple-element.260.first_ref, s32[3]{0:T(128)} %get-tuple-element.259.last_ref, bf16[576,1024]{1,0:T(8,128)(2,1)} %pad_maximum_fusion.7.q_ref, ...), custom_call_target="tpu_custom_call" | custom-call | flops 20000000000 | bytes 20000000 | tf_op jit(solution)/shard_map/pallas_call | solution.py:627
  767.2 32.6 %collective-permute-start.15 = (bf16[2,576,1024]{2,1,0:T(8,128)(2,1)}, bf16[2,576,1024]{2,1,0:T(8,128)(2,1)}, u32[]{:S(2)}, u32[]{:S(2)}) collective-permute-start(bf16[2,576,1024]{2,1,0:T(8,128)(2,1)} %get-tuple-element.42), channel_id=1, source_target_pairs={{0,2},{2,4},{4,6},{6,8},{8,10},{10,12},{12,14},{14,16},{16,18},{18... | collective-permute-start | bytes 7077896 | tf_op jit(solution)/shard_map/ppermute | solution.py:842
  806.4 37.3 %collective-permute-start.20 = (bf16[48,36864]{1,0:T(8,128)(2,1)}, bf16[48,36864]{1,0:T(8,128)(2,1)}, u32[]{:S(2)}, u32[]{:S(2)}) collective-permute-start(bf16[48,36864]{1,0:T(8,128)(2,1)} %get-tuple-element.179), channel_id=1, source_target_pairs={{0,1},{1,0},{2,3},{3,2},{4,5},{5,4},{6,7},{7,6},{8,9},{9,8},{10,11... | collective-permute-start | bytes 10616840 | tf_op jit(solution)/shard_map/ppermute | solution.py:99
  936.3 38.3 %multiply_convert_fusion.1 = bf16[2304,3072]{1,0:T(8,128)(2,1)} fusion(bf16[2304,1536]{1,0:T(8,128)(2,1)} %get-tuple-element.45, f32[2304,3072]{1,0:T(8,128)} %get-tuple-element.247, bf16[3072,3072]{1,0:T(8,128)(2,1)} %all-gather.11.cloned.1.call-done), kind=kOutput, calls=%fused_computation.13 | convolution fusion | flops 21828206592 | bytes 58982400 | tf_op jit(solution)/shard_map/dot_general | solution.py:40
  974.5 29.4 %fusion.38 = f32[2304,1536]{1,0:T(8,128)} fusion(bf16[2304,3072]{1,0:T(8,128)(2,1)} %multiply_convert_fusion.1, bf16[3072,3072]{1,0:T(8,128)(2,1)} %all-gather.9.cloned.1.call-done), kind=kOutput, calls=%fused_computation.67 | convolution fusion | flops 21743271936 | bytes 37748736 | tf_op jit(solution)/shard_map/dot_general | solution.py:48
  1003.9 37.1 %multiply_convert_fusion = bf16[2304,3072]{1,0:T(8,128)(2,1)} fusion(bf16[2304,1536]{1,0:T(8,128)(2,1)S(1)} %copy-done.126, f32[2304,3072]{1,0:T(8,128)} %get-tuple-element.249, bf16[3072,3072]{1,0:T(8,128)(2,1)} %all-gather.11.cloned.1.call-done), kind=kOutput, calls=%fused_computation.12 | convolution fusion | flops 21828206592 | bytes 58982400 | tf_op jit(solution)/shard_map/dot_general | solution.py:40
  1041.0 32.4 %fusion.18 = (f32[2304]{0:T(1024)S(1)}, bf16[2304,1536]{1,0:T(8,128)(2,1)}) fusion(bf16[2304,1536]{1,0:T(8,128)(2,1)} %shard_map.340, f32[1536]{0:T(1024)S(1)} %copy-done.77, f32[2304]{0:T(1024)S(1)} %copy-done.70, f32[2304,1536]{1,0:T(8,128)} %fusion.38, bf16[2304,3072]{1,0:T(8,128)(2,1)} %multiply_convert_fusion, ...), kind=kOutput, calls=%fused_computation.36 | convolution fusion | flops 21771581440 | bytes 51929088 | tf_op jit(solution)/shard_map/dot_general | solution.py:48
  1108.5 60.5 %shard_map.345 = (f32[2,48,36864]{2,1,0:T(8,128)}, f32[56,768]{1,0:T(8,128)}) custom-call(s32[1]{0:T(128)} %bitcast.3.place_ref, bf16[2304,1536]{1,0:T(8,128)(2,1)} %copy-done.7, bf16[768,1536]{1,0:T(8,128)(2,1)} %bitcast.298, bf16[768,1536]{1,0:T(8,128)(2,1)} %bitcast.300, bf16[48,36864]{1,0:T(8,128)(2,1)} %get-tuple-element.181.x_ref.own_ref, ...), custom_call_target="tpu_custom_call" | custom-call | flops 2774532096 | bytes 25000000 | tf_op jit(solution)/shard_map/pallas_call | solution.py:348
  1169.0 59.7 %shard_map.346 = (bf16[1,48,36864]{2,1,0:T(8,128)(2,1)}, f32[56,768]{1,0:T(8,128)}) custom-call(s32[1]{0:T(128)S(6)} %sub.55.place_ref, bf16[2304,1536]{1,0:T(8,128)(2,1)} %copy-done.7, bf16[768,1536]{1,0:T(8,128)(2,1)} %bitcast.299, bf16[768,1536]{1,0:T(8,128)(2,1)} %bitcast.301, bf16[48,36864]{1,0:T(8,128)(2,1)} %copy-done.8, ...), custom_call_target="tpu_custom_call" | custom-call | flops 2774532096 | bytes 25000000 | tf_op jit(solution)/shard_map/pallas_call | solution.py:348
  1480.5 72.0 %maximum_maximum_fusion = bf16[2048,4096]{1,0:T(8,128)(2,1)} fusion(bf16[1024,2048]{1,0:T(8,128)(2,1)S(1)} %convolution_convert_fusion.4, bf16[1024,2048]{1,0:T(8,128)(2,1)S(1)} %convolution_convert_fusion.5, bf16[1024,2048]{1,0:T(8,128)(2,1)S(1)} %convolution_convert_fusion.6, bf16[1024,2048]{1,0:T(8,128)(2,1)S(1)} %convolution_convert_fusion.7), kind=kLoop, calls=%fused_computation.30 | loop fusion | flops 67108864 | bytes 33554432 | tf_op jit(solution)/shard_map/concatenate | solution.py:165
  1591.7 92.1 %collective-permute-done.13 = bf16[1,48,36864]{2,1,0:T(8,128)(2,1)} collective-permute-done((bf16[1,48,36864]{2,1,0:T(8,128)(2,1)}, bf16[1,48,36864]{2,1,0:T(8,128)(2,1)}, u32[]{:S(2)}, u32[]{:S(2)}) %collective-permute-start.13) | collective-permute-done | bytes 3538976 | tf_op jit(solution)/shard_map/ppermute | solution.py:942
  1706.9 110.0 %collective-permute-done.17 = bf16[24,24,512]{2,1,0:T(8,128)(2,1)} collective-permute-done((bf16[24,24,512]{2,1,0:T(8,128)(2,1)}, bf16[24,24,512]{2,1,0:T(8,128)(2,1)}, u32[]{:S(2)}, u32[]{:S(2)}) %collective-permute-start.17) | collective-permute-done | bytes 589856 | tf_op jit(solution)/shard_map/ppermute | solution.py:935
  1850.3 41.4 %reduce-scatter.10.cloned.1.call-done = bf16[96,3072]{1,0:T(8,128)(2,1)} async-done(((bf16[3072,3072]{1,0:T(8,128)(2,1)}), bf16[96,3072]{1,0:T(8,128)(2,1)}) %reduce-scatter.10.cloned.1.call-update) | async-done | bytes 589840 | tf_op jit(solution)/shard_map/reduce_scatter | solution.py:166
  1893.9 210.0 %reduce-scatter.12.cloned.1.call-done = bf16[96,3072]{1,0:T(8,128)(2,1)} async-done(((bf16[3072,3072]{1,0:T(8,128)(2,1)}), bf16[96,3072]{1,0:T(8,128)(2,1)}) %reduce-scatter.12.cloned.1.call-update) | async-done | bytes 589840 | tf_op jit(solution)/shard_map/reduce_scatter | solution.py:166
  2106.1 179.9 %reduce-scatter.14.cloned.1.call-done = bf16[64,4096]{1,0:T(8,128)(2,1)} async-done(((bf16[2048,4096]{1,0:T(8,128)(2,1)}), bf16[64,4096]{1,0:T(8,128)(2,1)}) %reduce-scatter.14.cloned.1.call-update) | async-done | bytes 524304 | tf_op jit(solution)/shard_map/reduce_scatter | solution.py:166
  (607 shorter events, 770.3 us)
Async XLA Ops:
  7.2 235.7 %all-gather.9.cloned.1.call-start = ((), (), s32[]{:S(2)}) async-start(), calls=%async_computation.9 | async-start | bytes 19464192 | tf_op jit(solution)/shard_map/all_gather | solution.py:160
  7.9 297.0 %all-gather.11.cloned.1.call-start = ((), (), s32[]{:S(2)}) async-start(), calls=%async_computation.10 | async-start | bytes 19464192 | tf_op jit(solution)/shard_map/all_gather | solution.py:160
  8.7 405.3 %all-gather.13.cloned.1.call-start = ((), (), s32[]{:S(2)}) async-start(), calls=%async_computation.11 | async-start | bytes 5677056 | tf_op jit(solution)/shard_map/all_gather | solution.py:160
  10.4 527.2 %all-gather.15.cloned.1.call-start = ((), (), s32[]{:S(2)}) async-start(), calls=%async_computation.12 | async-start | bytes 27574272 | tf_op jit(solution)/shard_map/all_gather | solution.py:160
  16.9 175.9 %collective-permute-start.1 = (bf16[48,36864]{1,0:T(8,128)(2,1)}, bf16[48,36864]{1,0:T(8,128)(2,1)S(1)}, u32[]{:S(2)}, u32[]{:S(2)}) collective-permute-start(bf16[48,36864]{1,0:T(8,128)(2,1)} %get-tuple-element.182), channel_id=1, source_target_pairs={{0,1},{1,0},{2,3},{3,2},{4,5},{5,4},{6,7},{7,6},{8,9},{9,8},{10,11... | collective-permute-start | bytes 10616840 | tf_op jit(solution)/shard_map/ppermute | solution.py:99
  47.0 93.9 %collective-permute-start.2 = (bf16[2,3,36864]{2,0,1:T(2,128)(2,1)}, bf16[2,3,36864]{2,0,1:T(2,128)(2,1)}, u32[]{:S(2)}, u32[]{:S(2)}) collective-permute-start(bf16[2,3,36864]{2,0,1:T(2,128)(2,1)} %get-tuple-element.184), channel_id=1, source_target_pairs={{0,2},{2,4},{4,6},{6,8},{8,10},{10,12},{12,14},{14,16},{16,18},{18... | collective-permute-start | bytes 1327112 | tf_op jit(solution)/shard_map/ppermute | solution.py:25
  49.2 93.1 %collective-permute-start.3 = (bf16[2,3,36864]{2,0,1:T(2,128)(2,1)}, bf16[2,3,36864]{2,0,1:T(2,128)(2,1)}, u32[]{:S(2)}, u32[]{:S(2)}) collective-permute-start(bf16[2,3,36864]{2,0,1:T(2,128)(2,1)} %get-tuple-element.183), channel_id=1, source_target_pairs={{2,0},{4,2},{6,4},{8,6},{10,8},{12,10},{14,12},{16,14},{18,16},{20... | collective-permute-start | bytes 1327112 | tf_op jit(solution)/shard_map/ppermute | solution.py:26
  50.4 88.6 %collective-permute-start.5 = (bf16[49,768]{1,0:T(8,128)(2,1)}, bf16[49,768]{1,0:T(8,128)(2,1)}, u32[]{:S(2)}, u32[]{:S(2)}) collective-permute-start(bf16[49,768]{1,0:T(8,128)(2,1)} %param.23), channel_id=1, source_target_pairs={{0,1},{1,0},{2,3},{3,2},{4,5},{5,4},{6,7},{7,6},{8,9},{9,8},{10,11... | collective-permute-start | bytes 225800 | tf_op jit(solution)/shard_map/ppermute | solution.py:733
  50.9 79.9 %collective-permute-start.6 = (bf16[768]{0:T(1024)(128)(2,1)}, bf16[768]{0:T(1024)(128)(2,1)}, u32[]{:S(2)}, u32[]{:S(2)}) collective-permute-start(bf16[768]{0:T(1024)(128)(2,1)} %param.27), channel_id=1, source_target_pairs={{0,1},{1,0},{2,3},{3,2},{4,5},{5,4},{6,7},{7,6},{8,9},{9,8},{10,11... | collective-permute-start | bytes 4616 | tf_op jit(solution)/shard_map/ppermute | solution.py:733
  57.2 1643.3 %all-reduce.14.cloned.1.call-start = ((), (), s32[]{:S(2)}) async-start(), calls=%async_computation.5 | async-start | bytes 360448 | tf_op jit(solution)/shard_map/psum | solution.py:953
  135.7 51.2 %collective-permute-start = (bf16[576,512]{1,0:T(8,128)(2,1)}, bf16[576,512]{1,0:T(8,128)(2,1)}, u32[]{:S(2)}, u32[]{:S(2)}) collective-permute-start(bf16[576,512]{1,0:T(8,128)(2,1)} %dynamic-slice_bitcast_fusion.5), channel_id=1, source_target_pairs={{0,1},{1,0},{2,3},{3,2},{4,5},{5,4},{6,7},{7,6},{8,9},{9,8},{10,11... | collective-permute-start | bytes 1769480 | tf_op jit(solution)/shard_map/ppermute | solution.py:99
  139.0 417.1 %collective-permute-start.14 = (bf16[576,512]{1,0:T(8,128)(2,1)}, bf16[576,512]{1,0:T(8,128)(2,1)}, u32[]{:S(2)}, u32[]{:S(2)}) collective-permute-start(bf16[576,512]{1,0:T(8,128)(2,1)} %dynamic-slice_bitcast_fusion.4), channel_id=1, source_target_pairs={{0,1},{1,0},{2,3},{3,2},{4,5},{5,4},{6,7},{7,6},{8,9},{9,8},{10,11... | collective-permute-start | bytes 1769480 | tf_op jit(solution)/shard_map/ppermute | solution.py:99
  765.9 82.4 %collective-permute-start.16 = (bf16[2,576,1024]{2,1,0:T(8,128)(2,1)}, bf16[2,576,1024]{2,1,0:T(8,128)(2,1)}, u32[]{:S(2)}, u32[]{:S(2)}) collective-permute-start(bf16[2,576,1024]{2,1,0:T(8,128)(2,1)} %get-tuple-element.43), channel_id=1, source_target_pairs={{2,0},{4,2},{6,4},{8,6},{10,8},{12,10},{14,12},{16,14},{18,16},{20... | collective-permute-start | bytes 7077896 | tf_op jit(solution)/shard_map/ppermute | solution.py:843
  767.2 81.1 %collective-permute-start.15 = (bf16[2,576,1024]{2,1,0:T(8,128)(2,1)}, bf16[2,576,1024]{2,1,0:T(8,128)(2,1)}, u32[]{:S(2)}, u32[]{:S(2)}) collective-permute-start(bf16[2,576,1024]{2,1,0:T(8,128)(2,1)} %get-tuple-element.42), channel_id=1, source_target_pairs={{0,2},{2,4},{4,6},{6,8},{8,10},{10,12},{12,14},{14,16},{16,18},{18... | collective-permute-start | bytes 7077896 | tf_op jit(solution)/shard_map/ppermute | solution.py:842
  806.4 114.7 %collective-permute-start.20 = (bf16[48,36864]{1,0:T(8,128)(2,1)}, bf16[48,36864]{1,0:T(8,128)(2,1)}, u32[]{:S(2)}, u32[]{:S(2)}) collective-permute-start(bf16[48,36864]{1,0:T(8,128)(2,1)} %get-tuple-element.179), channel_id=1, source_target_pairs={{0,1},{1,0},{2,3},{3,2},{4,5},{5,4},{6,7},{7,6},{8,9},{9,8},{10,11... | collective-permute-start | bytes 10616840 | tf_op jit(solution)/shard_map/ppermute | solution.py:99
  1239.6 602.9 %reduce-scatter.16.cloned.1.call-start = ((), (), s32[]{:S(2)}) async-start(), calls=%async_computation.13 | async-start | bytes 5677056
  1263.1 583.1 %reduce-scatter.18.cloned.1.call-start = ((), (), s32[]{:S(2)}) async-start(), calls=%async_computation.14 | async-start | bytes 10272768
  1294.9 596.8 %reduce-scatter.10.cloned.1.call-start = ((), (), s32[]{:S(2)}) async-start(), calls=%async_computation.6 | async-start | bytes 19464192 | tf_op jit(solution)/shard_map/reduce_scatter | solution.py:166
  1377.4 726.5 %reduce-scatter.12.cloned.1.call-start = ((), (), s32[]{:S(2)}) async-start(), calls=%async_computation.7 | async-start | bytes 19464192 | tf_op jit(solution)/shard_map/reduce_scatter | solution.py:166
  1459.8 826.1 %reduce-scatter.14.cloned.1.call-start = ((), (), s32[]{:S(2)}) async-start(), calls=%async_computation.8 | async-start | bytes 17301504 | tf_op jit(solution)/shard_map/reduce_scatter | solution.py:166
  1552.6 131.2 %collective-permute-start.13 = (bf16[1,48,36864]{2,1,0:T(8,128)(2,1)}, bf16[1,48,36864]{2,1,0:T(8,128)(2,1)}, u32[]{:S(2)}, u32[]{:S(2)}) collective-permute-start(bf16[1,48,36864]{2,1,0:T(8,128)(2,1)} %get-tuple-element.38), channel_id=1, source_target_pairs={{0,1},{1,0},{2,3},{3,2},{4,5},{5,4},{6,7},{7,6},{8,9},{9,8},{10,11... | collective-permute-start | bytes 10616840 | tf_op jit(solution)/shard_map/ppermute | solution.py:942
  1589.6 106.7 %collective-permute-start.12 = (bf16[24,24,512]{2,1,0:T(8,128)(2,1)S(1)}, bf16[24,24,512]{2,1,0:T(8,128)(2,1)S(1)}, u32[]{:S(2)}, u32[]{:S(2)}) collective-permute-start(bf16[24,24,512]{2,1,0:T(8,128)(2,1)S(1)} %constant_dynamic-slice_fusion.2), channel_id=1, source_target_pairs={{0,1},{1,0},{2,3},{3,2},{4,5},{5,4},{6,7},{7,6},{8,9},{9,8},{10,11... | collective-permute-start | bytes 1769480 | tf_op jit(solution)/shard_map/ppermute | solution.py:935
  1589.7 230.1 %collective-permute-start.23 = (bf16[1,48,36864]{2,1,0:T(8,128)(2,1)}, bf16[1,48,36864]{2,1,0:T(8,128)(2,1)}, u32[]{:S(2)}, u32[]{:S(2)}) collective-permute-start(bf16[1,48,36864]{2,1,0:T(8,128)(2,1)} %get-tuple-element.47), channel_id=1, source_target_pairs={{0,1},{1,0},{2,3},{3,2},{4,5},{5,4},{6,7},{7,6},{8,9},{9,8},{10,11... | collective-permute-start | bytes 10616840 | tf_op jit(solution)/shard_map/ppermute | solution.py:942
  1698.7 118.2 %collective-permute-start.17 = (bf16[24,24,512]{2,1,0:T(8,128)(2,1)}, bf16[24,24,512]{2,1,0:T(8,128)(2,1)}, u32[]{:S(2)}, u32[]{:S(2)}) collective-permute-start(bf16[24,24,512]{2,1,0:T(8,128)(2,1)} %dynamic-slice_convert_fusion), channel_id=1, source_target_pairs={{0,1},{1,0},{2,3},{3,2},{4,5},{5,4},{6,7},{7,6},{8,9},{9,8},{10,11... | collective-permute-start | bytes 1769480 | tf_op jit(solution)/shard_map/ppermute | solution.py:935
  (151 other events, 3175.5 us)
Sparse Core Ops, SparseCore 0:
  10.9 167.6 all-gather.8
  181.5 123.4 all-gather.10
  307.8 64.2 all-gather.12
  375.4 162.1 all-gather.14
  1239.7 151.8 all-reduce.13
  1397.0 111.9 reduce-scatter.15
  1511.4 151.8 reduce-scatter.17
  1669.7 221.9 reduce-scatter.9
  1898.1 205.7 reduce-scatter.11
  2106.0 179.8 reduce-scatter.13

commit v2 on v1

--- a/solution.py
+++ b/solution.py
@@ -1,3 +1,5 @@
+import functools
+
 import jax
 import jax.numpy as jnp
 import numpy as np
@@ -156,18 +158,79 @@
     return jnp.stack(results)
 
 
+def stacked_kernel(cuts, *refs):
+    count = len(cuts) - 1
+    step = pl.program_id(0)
+    for i in range(count):
+
+        @pl.when((step >= cuts[i]) & (step < cuts[i + 1]))
+        def _(i=i):
+            refs[-1][...] = dot(refs[i][...], refs[count + i][...], NN).astype(BF)
+
+
+def stacked_grads(lefts, rights):
+    widths = [item.shape[1] for item in rights]
+    if any(width % CHUNK for width in widths):
+        return jnp.concatenate(
+            [matmul_tn(left, right).astype(BF) for left, right in zip(lefts, rights)], axis=1
+        )
+    tokens, rows = lefts[0].shape
+    cuts = [int(item) for item in np.cumsum([0] + [width // CHUNK for width in widths])]
+
+    def column(i):
+        return lambda step: (0, jnp.clip(step - cuts[i], 0, cuts[i + 1] - cuts[i] - 1))
+
+    return pl.pallas_call(
+        functools.partial(stacked_kernel, cuts),
+        out_shape=jax.ShapeDtypeStruct((rows, sum(widths)), BF),
+        grid=(cuts[-1],),
+        in_specs=[pl.BlockSpec((rows, tokens), lambda step: (0, 0)) for _ in lefts]
+        + [pl.BlockSpec((tokens, CHUNK), column(i)) for i in range(len(rights))],
+        out_specs=pl.BlockSpec((rows, CHUNK), lambda step: (0, step)),
+        **conv_params(2 * tokens * rows * sum(widths), 2 * rows * sum(widths)),
+    )(*[left.T for left in lefts], *rights)
+
+
 def gather_all(shard):
     full = lax.all_gather(shard, ALL, axis=0)
     return full.reshape(2, -1, shard.shape[1])
 
 
-def reduce_all(first, second):
-    both = jnp.concatenate([first.astype(BF), second.astype(BF)], axis=0)
-    return lax.psum_scatter(both, ALL, scatter_dimension=0, tiled=True).astype(F32)
+def reduce_tiles(terms):
+    return lax.psum_scatter(terms, "tile", scatter_dimension=0, tiled=True)
+
+
+def settle(summed, widths):
+    own, sent, start = [], [], 0
+    for width in widths:
+        mine, other = halves(summed[:, start : start + 2 * width])
+        own.append(mine)
+        sent.append(other)
+        start += 2 * width
+    got = lax.ppermute(jnp.concatenate(sent, axis=1), "mb", SWAP)
+    cuts = [int(item) for item in np.cumsum([0] + list(widths))]
+    return [
+        item.astype(F32) + got[:, cuts[i] : cuts[i + 1]].astype(F32) for i, item in enumerate(own)
+    ]
+
+
+def sum_everywhere(flat):
+    devices = lax.axis_size("tile")
+    if devices & (devices - 1):
+        return lax.psum(flat, "tile")
+    bit = 1
+    while bit < devices:
+        flat = flat + lax.ppermute(flat, "tile", [(i, i ^ bit) for i in range(devices)])
+        bit *= 2
+    return flat
+
+
+def together(*values):
+    return lax.optimization_barrier(values)
 
 
 LANES = 128
-RIM = 16
+RIM = 8
 VMEM_LIMIT = 60 * 1024 * 1024
 
 
@@ -249,13 +312,13 @@
                 pl.BlockSpec(x.shape, whole),
                 pl.BlockSpec(top.shape, whole),
                 pl.BlockSpec(bot.shape, whole),
-                pl.BlockSpec((49, LANES), half),
+                pl.BlockSpec((49, LANES), lambda cb, place: (0, cb)),
                 pl.BlockSpec(mask.shape, lambda cb, place: (0, 0, 0)),
             ]
             + [pl.BlockSpec(memory_space=pl.ANY)] * len(extra),
             out_specs=pl.BlockSpec((48 * 48, LANES), half),
             scratch_shapes=[
-                pltpu.VMEM((54, 80, LANES), F32),
+                pltpu.VMEM((54, 64, LANES), F32),
                 pltpu.VMEM((2, 49, 8, LANES), F32),
             ],
         ),
@@ -281,10 +344,10 @@
     tacc_ref[...] = jnp.zeros_like(tacc_ref)
 
     def fill(w, carry):
-        gs_ref[w + 3, 0:RIM, :] = top_ref[pl.ds(pl.multiple_of(w * RIM, RIM), RIM), :].astype(F32)
+        gs_ref[w + 3, 0:RIM, :] = top_ref[w].astype(F32)
         own = pl.ds(pl.multiple_of(w * rows, rows), rows)
         gs_ref[w + 3, RIM : RIM + rows, :] = g_ref[own, :].astype(F32)
-        gs_ref[w + 3, RIM + rows :, :] = bot_ref[pl.ds(pl.multiple_of(w * RIM, RIM), RIM), :].astype(F32)
+        gs_ref[w + 3, RIM + rows :, :] = bot_ref[w].astype(F32)
         return carry
 
     lax.fori_loop(0, 48, fill, 0)
@@ -356,12 +419,12 @@
             grid=(blocks,),
             in_specs=[
                 pl.BlockSpec((48 * 48, LANES), half),
-                pl.BlockSpec((48 * RIM, LANES), half),
-                pl.BlockSpec((48 * RIM, LANES), half),
+                pl.BlockSpec((48, RIM, LANES), lambda cb, place: (0, 0, place[0] * blocks + cb)),
+                pl.BlockSpec((48, RIM, LANES), lambda cb, place: (0, 0, place[0] * blocks + cb)),
                 pl.BlockSpec(x.shape, whole),
                 pl.BlockSpec(cot.shape, whole),
                 pl.BlockSpec((24, 24, LANES), lambda cb, place: (0, 0, place[0] * blocks + cb)),
-                pl.BlockSpec((49, LANES), half),
+                pl.BlockSpec((49, LANES), lambda cb, place: (0, cb)),
                 pl.BlockSpec(mask.shape, lambda cb, place: (0, 0, 0)),
             ],
             out_specs=(
@@ -369,7 +432,7 @@
                 pl.BlockSpec((56, LANES), lambda cb, place: (0, cb)),
             ),
             scratch_shapes=[
-                pltpu.VMEM((54, 80, LANES), F32),
+                pltpu.VMEM((54, 64, LANES), F32),
                 pltpu.VMEM((2, 49, 8, LANES), F32),
                 pltpu.VMEM((49, 8, LANES), F32),
                 pltpu.VMEM((24, 48, LANES), F32),
@@ -486,6 +549,8 @@
 
 
 CHUNK = 256
+PAIRS = 2
+WIDE = PAIRS * LANES
 NT = (((1,), (1,)), ((), ()))
 TN = (((0,), (0,)), ((), ()))
 
@@ -514,43 +579,52 @@
                   klab_ref, qlab_ref, out_ref, total_ref, kw_ref, vw_ref):
     fill_window(kw_ref, kb_ref, k_ref, ka_ref)
     fill_window(vw_ref, vb_ref, v_ref, va_ref)
+    heads = [(pair, side) for pair in range(PAIRS) for side in range(2)]
+    lanes = [slice(pair * LANES, (pair + 1) * LANES) for pair in range(PAIRS)]
     for n in range(3):
         rows = slice(n * 192, (n + 1) * 192)
         q = q_ref[rows, :] * jnp.asarray(0.125, BF)
-        q_half = [jnp.where(lane_half(q.shape, side), q, jnp.zeros_like(q)) for side in range(2)]
+        q_half = []
+        for pair, side in heads:
+            own = q[:, lanes[pair]]
+            q_half.append(jnp.where(lane_half(own.shape, side), own, jnp.zeros_like(own)))
         q_lab = qlab_ref[n, 0:1, :]
 
         def chunk(c, carry):
             at = pl.ds(pl.multiple_of(c * CHUNK, CHUNK), CHUNK)
-            kc, vc = kw_ref[at, :], vw_ref[at, :]
             same = klab_ref[at, 0:1] == q_lab
             new = []
-            for side in range(2):
-                top, total, acc = carry[side]
-                s = jnp.where(same, dot(kc, q_half[side], NT), NEG)
-                best = jnp.maximum(top, jnp.max(s, axis=0, keepdims=True))
-                p = jnp.exp(s - best)
+            scores = [
+                jnp.where(same, dot(kw_ref[at, lanes[pair]], q_half[i], NT), NEG)
+                for i, (pair, side) in enumerate(heads)
+            ]
+            for i, (pair, side) in enumerate(heads):
+                top, total, acc = carry[i]
+                best = jnp.maximum(top, jnp.max(scores[i], axis=0, keepdims=True))
+                p = jnp.exp(scores[i] - best)
                 shrink = jnp.exp(top - best)
                 total = total * shrink + jnp.sum(p, axis=0, keepdims=True)
-                new.append((best, total, acc * shrink + dot(vc, p.astype(BF), TN)))
+                acc = acc * shrink + dot(vw_ref[at, lanes[pair]], p.astype(BF), TN)
+                new.append((best, total, acc))
             return tuple(new)
 
         start = (jnp.full((1, 192), NEG, F32), jnp.zeros((1, 192), F32), jnp.zeros((LANES, 192), F32))
-        done = lax.fori_loop(first_ref[n], last_ref[n], chunk, (start, start))
-        outs = []
-        for side in range(2):
-            top, total, acc = done[side]
-            outs.append(acc * (1.0 / total))
-            total_ref[0, n, side : side + 1, :] = top + jnp.log(total)
-        both = jnp.concatenate([outs[0][:64], outs[1][64:]], axis=0)
-        out_ref[rows, :] = both.T.astype(BF)
+        done = lax.fori_loop(first_ref[n], last_ref[n], chunk, (start,) * len(heads))
+        for pair in range(PAIRS):
+            outs = []
+            for side in range(2):
+                top, total, acc = done[2 * pair + side]
+                outs.append(acc * (1.0 / total))
+                total_ref[pair, n, side : side + 1, :] = top + jnp.log(total)
+            both = jnp.concatenate([outs[0][:64], outs[1][64:]], axis=0)
+            out_ref[rows, lanes[pair]] = both.T.astype(BF)
 
 
 def attend(q, k, v, around, qlab, klab, first, last):
     count, width = q.shape
     window = -(-3 * count // CHUNK) * CHUNK
-    block = pl.BlockSpec((count, LANES), lambda p, *_: (0, p))
-    stats = pl.BlockSpec((1, 3, 2, 192), lambda p, *_: (p, 0, 0, 0))
+    block = pl.BlockSpec((count, WIDE), lambda p, *_: (0, p))
+    stats = pl.BlockSpec((PAIRS, 3, 2, 192), lambda p, *_: (p, 0, 0, 0))
     return pl.pallas_call(
         attend_kernel,
         out_shape=(
@@ -559,21 +633,21 @@
         ),
         grid_spec=pltpu.PrefetchScalarGridSpec(
             num_scalar_prefetch=2,
-            grid=(width // LANES,),
+            grid=(width // WIDE,),
             in_specs=[block] * 7
             + [
                 pl.BlockSpec(klab.shape, lambda p, *_: (0, 0)),
                 pl.BlockSpec(qlab.shape, lambda p, *_: (0, 0, 0)),
             ],
             out_specs=(block, stats),
-            scratch_shapes=[pltpu.VMEM((window, LANES), BF), pltpu.VMEM((window, LANES), BF)],
+            scratch_shapes=[pltpu.VMEM((window, WIDE), BF), pltpu.VMEM((window, WIDE), BF)],
         ),
         **conv_params(20_000_000_000, 20_000_000),
     )(first, last, q, around[0], k, around[1], around[2], v, around[3], klab, qlab)
 
 
 def attend_back_kernel(first_ref, last_ref, q_ref, kb_ref, k_ref, ka_ref, vb_ref, v_ref, va_ref,
-                       do_ref, total_ref, delta_ref, klab_ref, qlab_ref,
+                       do_ref, o_ref, total_ref, klab_ref, qlab_ref,
                        dq_ref, dk_ref, dv_ref, before_ref, after_ref,
                        kw_ref, vw_ref, dkw_ref, dvw_ref):
     count = q_ref.shape[0]
@@ -581,35 +655,50 @@
     fill_window(vw_ref, vb_ref, v_ref, va_ref)
     dkw_ref[...] = jnp.zeros_like(dkw_ref)
     dvw_ref[...] = jnp.zeros_like(dvw_ref)
+    heads = [(pair, side) for pair in range(PAIRS) for side in range(2)]
+    lanes = [slice(pair * LANES, (pair + 1) * LANES) for pair in range(PAIRS)]
     for n in range(3):
         rows = slice(n * 192, (n + 1) * 192)
         q = q_ref[rows, :] * jnp.asarray(0.125, BF)
         do = do_ref[rows, :]
-        masks = [lane_half((192, LANES), side) for side in range(2)]
-        q_half = [jnp.where(m, q, jnp.zeros_like(q)) for m in masks]
-        do_half = [jnp.where(m, do, jnp.zeros_like(do)) for m in masks]
+        halves = [lane_half((192, LANES), side) for side in range(2)]
+        q_half = [jnp.where(halves[s], q[:, lanes[p]], jnp.zeros((), BF)) for p, s in heads]
+        do_half = [jnp.where(halves[s], do[:, lanes[p]], jnp.zeros((), BF)) for p, s in heads]
         q_lab = qlab_ref[n, 0:1, :]
-
-        def chunk(c, dq):
+        flow = do.astype(F32) * o_ref[rows, :].astype(F32)
+        delta = []
+        for p in range(PAIRS):
+            turned = flow[:, lanes[p]].T
+            delta += [jnp.sum(turned[s * 64 : s * 64 + 64], axis=0, keepdims=True) for s in range(2)]
+
+        def chunk(c, carry):
             at = pl.ds(pl.multiple_of(c * CHUNK, CHUNK), CHUNK)
-            kc, vc = kw_ref[at, :], vw_ref[at, :]
             same = klab_ref[at, 0:1] == q_lab
-            ks = [jnp.where(lane_half((CHUNK, LANES), side), kc, jnp.zeros_like(kc)) for side in range(2)]
-            dk, dv = dkw_ref[at, :], dvw_ref[at, :]
-            for side in range(2):
-                s = dot(kc, q_half[side], NT)
-                p = jnp.exp(jnp.where(same, s - total_ref[0, n, side : side + 1, :], NEG))
-                dp = dot(vc, do_half[side], NT)
-                ds = (p * (dp - delta_ref[0, n, side : side + 1, :])).astype(BF)
-                dv = dv + dot(p.astype(BF), do_half[side], NN)
-                dk = dk + dot(ds, q_half[side], NN)
-                dq = dq + dot(ds, ks[side], TN)
-            dkw_ref[at, :] = dk
-            dvw_ref[at, :] = dv
-            return dq
-
-        dq = lax.fori_loop(first_ref[n], last_ref[n], chunk, jnp.zeros((192, LANES), F32))
-        dq_ref[rows, :] = (dq * 0.125).astype(BF)
+            kcs = [kw_ref[at, lanes[pair]] for pair in range(PAIRS)]
+            vcs = [vw_ref[at, lanes[pair]] for pair in range(PAIRS)]
+            scores = [dot(kcs[p], q_half[i], NT) for i, (p, s) in enumerate(heads)]
+            dps = [dot(vcs[p], do_half[i], NT) for i, (p, s) in enumerate(heads)]
+            ps, dss = [], []
+            for i, (p, s) in enumerate(heads):
+                raised = jnp.where(same, scores[i] - total_ref[p, n, s : s + 1, :], NEG)
+                ps.append(jnp.exp(raised))
+            for i, (p, s) in enumerate(heads):
+                dss.append((ps[i] * (dps[i] - delta[i])).astype(BF))
+            low = [item.astype(BF) for item in ps]
+            dqs = []
+            for p in range(PAIRS):
+                e, o = 2 * p, 2 * p + 1
+                dvw_ref[at, lanes[p]] += dot(low[e], do_half[e], NN) + dot(low[o], do_half[o], NN)
+                dkw_ref[at, lanes[p]] += dot(dss[e], q_half[e], NN) + dot(dss[o], q_half[o], NN)
+                two = [dot(dss[e], kcs[p], TN), dot(dss[o], kcs[p], TN)]
+                dqs.append(carry[p] + jnp.where(lane_half((192, LANES), 0), two[0], two[1]))
+            return tuple(dqs)
+
+        dqs = lax.fori_loop(
+            first_ref[n], last_ref[n], chunk, tuple(jnp.zeros((192, LANES), F32) for _ in range(PAIRS))
+        )
+        for pair in range(PAIRS):
+            dq_ref[rows, lanes[pair]] = (dqs[pair] * 0.125).astype(BF)
     dk_ref[...] = dkw_ref[count : 2 * count, :]
     dv_ref[...] = dvw_ref[count : 2 * count, :]
     before_ref[0] = dkw_ref[0:count, :].astype(BF)
@@ -618,12 +707,12 @@
     after_ref[1] = dvw_ref[2 * count : 3 * count, :].astype(BF)
 
 
-def attend_back(q, k, v, around, grad, total, delta, qlab, klab, first, last):
+def attend_back(q, k, v, around, grad, out, total, qlab, klab, first, last):
     count, width = q.shape
     window = -(-3 * count // CHUNK) * CHUNK
-    block = pl.BlockSpec((count, LANES), lambda p, *_: (0, p))
-    stats = pl.BlockSpec((1, 3, 2, 192), lambda p, *_: (p, 0, 0, 0))
-    pair = pl.BlockSpec((2, count, LANES), lambda p, *_: (0, 0, p))
+    block = pl.BlockSpec((count, WIDE), lambda p, *_: (0, p))
+    stats = pl.BlockSpec((PAIRS, 3, 2, 192), lambda p, *_: (p, 0, 0, 0))
+    pair = pl.BlockSpec((2, count, WIDE), lambda p, *_: (0, 0, p))
     return pl.pallas_call(
         attend_back_kernel,
         out_shape=(
@@ -635,24 +724,23 @@
         ),
         grid_spec=pltpu.PrefetchScalarGridSpec(
             num_scalar_prefetch=2,
-            grid=(width // LANES,),
-            in_specs=[block] * 8
+            grid=(width // WIDE,),
+            in_specs=[block] * 9
             + [
-                stats,
                 stats,
                 pl.BlockSpec(klab.shape, lambda p, *_: (0, 0)),
                 pl.BlockSpec(qlab.shape, lambda p, *_: (0, 0, 0)),
             ],
             out_specs=(block, block, block, pair, pair),
             scratch_shapes=[
-                pltpu.VMEM((window, LANES), BF),
-                pltpu.VMEM((window, LANES), BF),
-                pltpu.VMEM((window, LANES), F32),
-                pltpu.VMEM((window, LANES), F32),
+                pltpu.VMEM((window, WIDE), BF),
+                pltpu.VMEM((window, WIDE), BF),
+                pltpu.VMEM((window, WIDE), F32),
+                pltpu.VMEM((window, WIDE), F32),
             ],
         ),
         **conv_params(20_000_000_000, 20_000_000),
-    )(first, last, q, around[0], k, around[1], around[2], v, around[3], grad, total, delta, klab, qlab)
+    )(first, last, q, around[0], k, around[1], around[2], v, around[3], grad, out, total, klab, qlab)
 
 
 def on_device(
@@ -691,27 +779,16 @@
     fast = c_shard % LANES == 0 and lax.axis_size("tp") == 1
     hi_raw = hi_in.reshape(2, hi_rows, hi_cols * c_shard)
     hi_own, hi_other = swap_micro(hi_raw)
-    up, down = rim_pair(hi_raw, 3, 1)
+    up, down = rim_pair(hi_raw, RIM, 1)
     own_rims, other_rims = swap_micro(jnp.stack([up, down], axis=1))
-    cot_own, cot_other = swap_micro(d_hi_out.reshape(2, hi_rows, hi_cols * c_shard))
+    lo_in, d_lo_out, cn_scale, ad_kernel, hi_other = together(
+        lo_in, d_lo_out, cn_scale, ad_kernel, hi_other
+    )
     lo_low = in_order(*swap_micro(lo_in.reshape(2, tok_count, d_shard)), 1)
     lo_field = lo_low.astype(F32)
 
-    mlp_in = gather_all(cn_w1)
-    mlp_out = gather_all(cn_w2.T)
-    ad_gate = gather_all(jnp.concatenate([ad_proj, gate_w1], axis=1))
-    ad_matrix = [ad_gate[g, :, :d_shard] for g in range(2)]
-    gate_in = [ad_gate[g, :, d_shard:] for g in range(2)]
-    gh_shard = gate_w1.shape[1]
-    ff_shard = fc1.shape[1]
-    vit = gather_all(
-        jnp.concatenate([gate_w2.T, qkv[0], qkv[1], qkv[2], out_proj.T, fc1, fc2.T], axis=1)
-    )
-    cuts = np.cumsum([0, gh_shard, d_shard, d_shard, d_shard, d_shard, ff_shard, ff_shard])
-    gate_out, q_w, k_w, v_w, out_w, ff_in, ff_out = [
-        [vit[g, :, int(cuts[i]) : int(cuts[i + 1])] for g in range(2)] for i in range(7)
-    ]
-
+    hid_shard, gh_shard, ff_shard = cn_w1.shape[1], gate_w1.shape[1], fc1.shape[1]
+    mlp = gather_all(jnp.concatenate([cn_w1, cn_w2.T], axis=1))
     def apply(left, pair):
         return jnp.concatenate([matmul(left, pair[0]), matmul(left, pair[1])], axis=1)
 
@@ -732,27 +809,24 @@
     def both_shards(shard, axis):
         return in_order(shard, lax.ppermute(shard, "mb", SWAP), axis)
 
-    conv_taps = both_shards(cn_kernel, 1)
+    other_kernel = lax.ppermute(cn_kernel, "mb", SWAP)
+    conv_taps = in_order(cn_kernel, other_kernel, 1)
     ad_taps = both_shards(ad_kernel, 1)
     hi_scale = both_shards(cn_scale, 0).astype(F32)
 
     own_place = mine.reshape(1).astype(jnp.int32)
     other_place = 1 - own_place
-    own_rims, other_rims = [
-        (jnp.pad(rims[0], ((RIM - 3, 0), (0, 0))), jnp.pad(rims[1], ((0, RIM - 3), (0, 0))))
-        for rims in (own_rims, other_rims)
-    ]
     seen = jnp.stack([(hi_ids[a : a + hi_rows] == hi_mid).astype(F32) for a in range(7)])
     mask = jnp.broadcast_to(seen[:, :, None], (7, hi_rows, LANES))
-    wide_taps = conv_taps.astype(F32)
+    own_taps, other_taps = cn_kernel.astype(F32), other_kernel.astype(F32)
 
     def natural(own, other):
         shape = (-1, hi_cols, c_shard)
         return in_order(own.reshape(shape), other.reshape(shape), 2)
 
     if fast:
-        conv_flat = conv_forward(hi_own, *own_rims, wide_taps, mask, own_place)
-        conv_flat = conv_forward(hi_other, *other_rims, wide_taps, mask, other_place, conv_flat)
+        conv_flat = conv_forward(hi_own, *own_rims, own_taps, mask, own_place)
+        conv_flat = conv_forward(hi_other, *other_rims, other_taps, mask, other_place, conv_flat)
     else:
         hi_field = natural(hi_own, hi_other)
         hi_pad = jnp.concatenate(
@@ -766,7 +840,34 @@
         conv_flat = conv_low.transpose(1, 0, 2).reshape(pix_count, c_own)
     conv_full = features(conv_flat)
     normed, norm_pull = jax.vjp(layer_norm, conv_full.astype(F32), cn_gain.astype(F32))
-    normed_low = lax.optimization_barrier(normed.astype(BF))
+    normed_low, mlp, gate_w2 = together(normed.astype(BF), mlp, gate_w2)
+    mlp_in = [mlp[g, :, :hid_shard] for g in range(2)]
+    mlp_out = [mlp[g, :, hid_shard:] for g in range(2)]
+    ad_shard = jnp.concatenate([ad_proj, gate_w1], axis=1)
+    narrow = gate_w2.shape[1]
+    vit = gather_all(
+        jnp.concatenate(
+            [
+                gate_w2.T,
+                qkv[0],
+                qkv[1],
+                qkv[2],
+                out_proj.T,
+                fc1,
+                fc2.T,
+                ad_shard.reshape(narrow, -1),
+            ],
+            axis=1,
+        )
+    )
+    cuts = np.cumsum([0, gh_shard, d_shard, d_shard, d_shard, d_shard, ff_shard, ff_shard])
+    gate_out, q_w, k_w, v_w, out_w, ff_in, ff_out = [
+        [vit[g, :, int(cuts[i]) : int(cuts[i + 1])] for g in range(2)] for i in range(7)
+    ]
+    ad_gate = vit[:, :, int(cuts[7]) :].reshape(2, -1, ad_shard.shape[1])
+    ad_matrix = [ad_gate[g, :, :d_shard] for g in range(2)]
+    gate_in = [ad_gate[g, :, d_shard:] for g in range(2)]
+
     inner_act, inner_slope = zip(*[gelu_pair(matmul(normed_low, mlp_in[g])) for g in range(2)])
     branch = partial_sums(
         matmul_nt(inner_act[0], mlp_out[0]) + matmul_nt(inner_act[1], mlp_out[1])
@@ -779,6 +880,8 @@
         hi_sum = hi_field.astype(F32) + hi_scale * branch_rows
         pooled = jnp.mean(hi_sum.reshape(row_count, 2, col_count, 2, c_own), axis=(1, 3))
     pooled_full = features(pooled.reshape(tok_count, c_own).astype(BF))
+    pooled_full, d_hi_out = together(pooled_full, d_hi_out)
+    cot_own, cot_other = swap_micro(d_hi_out.reshape(2, hi_rows, hi_cols * c_shard))
     proj_low = apply(pooled_full, ad_matrix).astype(BF)
     proj_pad = rim_rows(proj_low.reshape(row_count, col_count, d_own), 1)
     local_conv = depthwise(proj_pad, ad_taps, small_ids, lo_mid, 3, False).reshape(
@@ -793,9 +896,7 @@
     queries = apply(norm_low, q_w).astype(BF)
     key_rows = apply(norm_low, k_w).astype(BF)
     value_rows = apply(norm_low, v_w).astype(BF)
-    key_value = jnp.concatenate([key_rows, value_rows], axis=1)
-    kv_before, kv_after = rim_pair(key_value, tok_count, 0)
-    around = (kv_before[:, :d_own], kv_after[:, :d_own], kv_before[:, d_own:], kv_after[:, d_own:])
+    around = rim_pair(key_rows, tok_count, 0) + rim_pair(value_rows, tok_count, 0)
     near = row_labels(canvas_ids, row_start, row_count, row_count)
     key_tok = jnp.repeat(near, col_count)
     window = -(-3 * tok_count // CHUNK) * CHUNK
@@ -811,6 +912,9 @@
         queries, key_rows, value_rows, around, query_lab, key_lab, first, last
     )
     mixed_two = mixed_one + partial_sums(apply_t(attended, out_w))
+    if fast:
+        hi_got = lax.ppermute(hi_sent, "mb", SWAP)
+        mixed_two, hi_got, cot_other = together(mixed_two, hi_got, cot_other)
     mixed2_full = features(mixed_two.astype(BF))
     norm_two, second_pull = jax.vjp(layer_norm, mixed2_full.astype(F32), ln2_gain.astype(F32))
     norm2_low = norm_two.astype(BF)
@@ -822,20 +926,14 @@
     ff_grad_full = features(grad_low)
     ff_pre_grad = (apply(ff_grad_full, ff_out) * ff_slope.astype(F32)).astype(BF)
     second_grad = partial_sums(apply_t(ff_pre_grad, ff_in)).astype(BF)
-    g_ff = reduce_all(
-        *[
-            jnp.concatenate([matmul_tn(norm2_low, i), matmul_tn(ff_grad_full, o)], axis=1)
-            for i, o in zip(cols(ff_pre_grad), cols(ff_hidden))
-        ]
-    )
     back_two, grad_ln2 = second_pull(features(second_grad).astype(F32))
-    grad_two = grad_out + own_slice(back_two)
+    p_ff = stacked_grads([norm2_low, ff_grad_full], [ff_pre_grad, ff_hidden])
+    grad_two, p_ff = together(grad_out + own_slice(back_two), p_ff)
+    s_ff = reduce_tiles(p_ff)
     att_grad_full = features(grad_two.astype(BF))
     att_grad = apply(att_grad_full, out_w).astype(BF)
-    inner = (att_grad.astype(F32) * attended.astype(F32)).reshape(3, 192, head_count // 2, 2, HDIM)
-    delta = jnp.sum(inner, axis=-1).transpose(2, 0, 3, 1)
     query_grad, key_own, value_own, to_before, to_after = attend_back(
-        queries, key_rows, value_rows, around, att_grad, log_total, delta, query_lab, key_lab, first, last
+        queries, key_rows, value_rows, around, att_grad, attended, log_total, query_lab, key_lab, first, last
     )
     devices = lax.axis_size("tile")
     steps = [(i, i + 1) for i in range(devices - 1)]
@@ -852,22 +950,9 @@
     grad_one = grad_two + own_slice(back_one)
     gate_pre_grad = (grad_one * local_conv * (1.0 - gate_val * gate_val)).astype(BF)
     gate_grad_full = features(gate_pre_grad)
-    g_att = reduce_all(
-        *[
-            jnp.concatenate(
-                [
-                    matmul_tn(gate_grad_full, h),
-                    matmul_tn(norm_low, q),
-                    matmul_tn(norm_low, k),
-                    matmul_tn(norm_low, v),
-                    matmul_tn(att_grad_full, o),
-                ],
-                axis=1,
-            )
-            for h, q, k, v, o in zip(
-                cols(gate_hidden), cols(query_grad), cols(key_grad), cols(value_grad), cols(attended)
-            )
-        ]
+    p_att = stacked_grads(
+        [gate_grad_full, norm_low, att_grad_full],
+        [gate_hidden, jnp.concatenate([query_grad, key_grad, value_grad], axis=1), attended],
     )
     hidden_grad = (apply(gate_grad_full, gate_out) * gate_slope.astype(F32)).astype(BF)
     local_grad = (grad_one * gate_val).astype(BF).reshape(row_count, col_count, d_own)
@@ -878,13 +963,10 @@
         .astype(BF)
     )
     grad_ad_kernel = tap_grads(proj_pad, local_grad, small_ids, lo_mid, 3)
-    g_ad = reduce_all(
-        *[
-            jnp.concatenate([matmul_tn(pooled_full, p), matmul_tn(pooled_full, h)], axis=1)
-            for p, h in zip(cols(proj_grad), cols(hidden_grad))
-        ]
-    )
+    p_ad = matmul_tn(pooled_full, jnp.concatenate([proj_grad, hidden_grad], axis=1)).astype(BF)
     pooled_grad = partial_sums(apply_t(hidden_grad, gate_in) + apply_t(proj_grad, ad_matrix))
+    pooled_grad, p_att, p_ad, s_ff = together(pooled_grad, p_att, p_ad, s_ff)
+    s_att, s_ad = reduce_tiles(p_att), reduce_tiles(p_ad)
     pool_cols = pooled_grad.reshape(row_count, col_count, c_own).transpose(1, 0, 2)
     if fast:
         scaled_grad, scale_parts = scaled_grads(
@@ -898,37 +980,44 @@
         grad_scale = jnp.sum(grad_cols * branch, axis=0)
         scaled_grad = (grad_cols * hi_scale).astype(BF)
     branch_full = lax.optimization_barrier(features(scaled_grad))
-    g_w2 = reduce_all(*[matmul_tn(branch_full, act) for act in inner_act])
-    inner_grad = [
-        (matmul(branch_full, mlp_out[g]) * inner_slope[g].astype(F32)).astype(BF) for g in range(2)
-    ]
-    g_w1 = reduce_all(*[matmul_tn(normed_low, grad) for grad in inner_grad])
+    p_w2 = [matmul_tn(branch_full, act).astype(BF) for act in inner_act]
+    branch_full, *p_w2 = together(branch_full, *p_w2)
+    s_w2 = [reduce_tiles(item) for item in p_w2]
+    grad_first = (matmul(branch_full, mlp_out[0]) * inner_slope[0].astype(F32)).astype(BF)
+    w1_first = matmul_tn(normed_low, grad_first).astype(BF)
+    branch_full, w1_first = together(branch_full, w1_first)
+    grad_second = (matmul(branch_full, mlp_out[1]) * inner_slope[1].astype(F32)).astype(BF)
+    w1_second = matmul_tn(normed_low, grad_second).astype(BF)
+    w1_sent = jnp.where(mine == 0, w1_second, w1_first)
+    w1_own = jnp.where(mine == 0, w1_first, w1_second)
+    grad_second, w1_sent = together(grad_second, w1_sent)
+    w1_got = lax.ppermute(w1_sent, "mb", SWAP)
     normed_grad = partial_sums(
-        matmul_nt(inner_grad[0], mlp_in[0]) + matmul_nt(inner_grad[1], mlp_in[1])
+        matmul_nt(grad_first, mlp_in[0]) + matmul_nt(grad_second, mlp_in[1])
     ).astype(BF)
     back_conv, grad_cn_gain = norm_pull(features(normed_grad).astype(F32))
     conv_grad = own_slice(back_conv).astype(BF)
     conv_cols = conv_grad.reshape(hi_cols, hi_rows, c_own)
-    grad_up, grad_down = rim_pair(conv_cols, 3, 1)
+    grad_up, grad_down = rim_pair(conv_cols, RIM, 1)
     if fast:
-        grad_rims = [
-            jnp.pad(rim, ((0, 0), side, (0, 0))).reshape(hi_cols * RIM, c_own)
-            for rim, side in ((grad_up, (RIM - 3, 0)), (grad_down, (0, RIM - 3)))
-        ]
         ghi_sent, taps_other = conv_backward(
-            conv_grad, *grad_rims, hi_other, cot_other, pool_cols, wide_taps, mask, other_place, 1, BF
+            conv_grad, grad_up, grad_down, hi_other, cot_other, pool_cols, other_taps, mask, other_place, 1, BF
         )
+        w1_sum = (w1_own.astype(F32) + w1_got.astype(F32)).astype(BF)
+        conv_grad, w1_sum, ghi_sent = together(conv_grad, w1_sum, ghi_sent)
         ghi_mine, taps_own = conv_backward(
-            conv_grad, *grad_rims, hi_own, cot_own, pool_cols, wide_taps, mask, own_place, 2, F32
+            conv_grad, grad_up, grad_down, hi_own, cot_own, pool_cols, own_taps, mask, own_place, 2, F32
         )
         grad_cn_kernel = in_order(taps_own[:49], taps_other[:49], 1)
     else:
         conv_grad = conv_cols.transpose(1, 0, 2)
         conv_pad = jnp.concatenate(
-            [grad_up.transpose(1, 0, 2), conv_grad, grad_down.transpose(1, 0, 2)]
+            [grad_up.transpose(1, 0, 2)[-3:], conv_grad, grad_down.transpose(1, 0, 2)[:3]]
         )
         hi_back = hi_grad + depthwise(conv_pad, conv_taps, hi_ids, hi_mid, 7, True)
         grad_cn_kernel = tap_grads(hi_pad, conv_grad, hi_ids, hi_mid, 7)
+        w1_sum = (w1_own.astype(F32) + w1_got.astype(F32)).astype(BF)
+    g_w1 = reduce_tiles(w1_sum).astype(F32)
 
     def leave(values, kind):
         own, sent = halves(values)
@@ -937,33 +1026,34 @@
 
     lo_stack = leave(lo_result.reshape(row_count, col_count, d_own), BF)
     if fast:
+        ghi_got = lax.ppermute(ghi_sent, "mb", SWAP)
         hi_stack, ghi_stack = [
-            lax.dynamic_update_slice_in_dim(
-                stack, lax.ppermute(sent, "mb", SWAP).astype(stack.dtype), 1 - mine, 0
-            )
-            for stack, sent in ((hi_mine, hi_sent), (ghi_mine, ghi_sent))
+            lax.dynamic_update_slice_in_dim(stack, got.astype(stack.dtype), 1 - mine, 0)
+            for stack, got in ((hi_mine, hi_got), (ghi_mine, ghi_got))
         ]
     else:
         hi_stack = leave(hi_sum, BF)
         ghi_stack = leave(hi_back, F32)
     glo_stack = leave(grad_one.reshape(row_count, col_count, d_own), F32)
 
-    flat_terms = [grad_cn_kernel, grad_scale, grad_ad_kernel, grad_cn_gain, grad_ln1, grad_ln2]
-    sizes = np.cumsum([0] + [item.size for item in flat_terms])
-    total = lax.psum(
-        jnp.concatenate([item.reshape(-1).astype(BF) for item in flat_terms]), ALL
-    ).astype(F32)
-    sums = [
-        total[int(sizes[i]) : int(sizes[i + 1])].reshape(item.shape)
-        for i, item in enumerate(flat_terms)
+    (g_w2,) = settle(jnp.concatenate(s_w2, axis=1), (hid_shard,))
+    g_fc1, g_fc2 = settle(s_ff, (ff_shard, ff_shard))
+    g_gate_w2, g_q, g_k, g_v, g_out = settle(s_att, (gh_shard, d_shard, d_shard, d_shard, d_shard))
+    g_ad, g_gate_w1 = settle(s_ad, (d_shard, gh_shard))
+
+    own_terms, sent_terms = zip(*[halves(item) for item in (grad_cn_kernel, grad_scale, grad_ad_kernel)])
+    gains = [grad_cn_gain, grad_ln1, grad_ln2]
+    flat, sent = [
+        jnp.concatenate([item.reshape(-1) for item in (*terms, *gains)])
+        for terms in (own_terms, sent_terms)
     ]
-    g_kernel, g_scale, g_taps = [halves(item)[0] for item in sums[:3]]
-    gain_sums = sums[3:]
-
-    g_gate_w1 = g_ad[:, d_shard:]
-    g_gate_w2 = g_att[:, :gh_shard].T
-    g_qkv = jnp.stack([g_att[:, gh_shard + j * d_shard : gh_shard + (j + 1) * d_shard] for j in range(3)])
-    g_out = g_att[:, gh_shard + 3 * d_shard :].T
+    flat = sum_everywhere(flat + lax.ppermute(sent, "mb", SWAP))
+    sizes = np.cumsum([0] + [item.size for item in (*own_terms, *gains)])
+    g_kernel, g_scale, g_taps, *gain_sums = [
+        flat[int(sizes[i]) : int(sizes[i + 1])].reshape(item.shape)
+        for i, item in enumerate((*own_terms, *gains))
+    ]
+
     return (
         lo_stack,
         hi_stack.reshape(2, hi_rows, 1, hi_cols * c_shard),
@@ -974,16 +1064,16 @@
         g_w1,
         g_w2.T,
         g_scale,
-        g_ad[:, :d_shard],
+        g_ad,
         g_taps,
         g_gate_w1,
-        g_gate_w2,
+        g_gate_w2.T,
         gain_sums[1],
-        g_qkv,
-        g_out,
+        jnp.stack([g_q, g_k, g_v]),
+        g_out.T,
         gain_sums[2],
-        g_ff[:, :ff_shard],
-        g_ff[:, ff_shard:].T,
+        g_fc1,
+        g_fc2.T,
     )
 
 

time: 2290 us -> 1620 us (0.71)
  waiting for transfers between devices: 847 us -> 360 us
  other arithmetic: 255 us -> 135 us
  local copies, waits for them, and re-layouts: 180 us -> 146 us
  matrix products: 518 us -> 494 us
  starting transfers between devices: 134 us -> 111 us
    reduce_scatter x3 -> x6, waiting for transfers between devices: 431 us -> 33.8 us  [reduce_tiles(): return lax.psum_scatter(terms, 'tile', scatter_dimension=0, tiled=True)]
    concatenate x7 -> x5, other arithmetic: 149 us -> 6.66 us  [the longest x1 2.33 us: on_device(): mlp = gather_all(jnp.concatenate([cn_w1, cn_w2.T], axis=1))]
    ppermute x5, waiting for transfers between devices: 16.2 us -> 144 us  [swap_micro(): return (own, lax.ppermute(sent, 'mb', SWAP))]
    ppermute x2, waiting for transfers between devices: 120 us -> 12.2 us  [leave(): other = lax.ppermute(sent.astype(BF), 'mb', SWAP)]
    all_gather x4 -> x2, waiting for transfers between devices: 131 us -> 38 us  [gather_all(): full = lax.all_gather(shard, ALL, axis=0)]
    ppermute x3 -> x2, waiting for transfers between devices: 55 us -> 0.01 us  [both_shards(): return in_order(shard, lax.ppermute(shard, 'mb', SWAP), axis)]
    pallas_call x0 -> x2, Pallas kernels: none -> 50.4 us  [stacked_grads(): pl.pallas_call(functools.partial(stacked_kernel, cuts), out_shape=jax.Sha...]
    unnamed x309 -> x282, local copies, waits for them, and re-layouts: 100 us -> 51.5 us
  transfers between devices with their start and end apart: 34 -> 44, of which waited for: 11 -> 18; matrix products, arithmetic and copies ran while one was open for 31% -> 44% of each run, Pallas kernels for 4% -> 20%
where the time goes in v2:
time: 1620 us; the launch traced here: 1610 us
  matrix products  494 us (30%)
  waiting for transfers between devices  360 us (22%)
  Pallas kernels  347 us (21%)
  local copies, waits for them, and re-layouts  146 us (9%)
  other arithmetic  135 us (8%)
  starting transfers between devices  111 us (7%)
  between operations  16.6 us (1%)
    dot_general x22, matrix products, matmul(): return jnp.dot(left, right, preferred_element_type=F32)  190 us
    dot_general x22, matrix products, matmul_nt(): lax.dot_general(left, right, (((1,), (1,)), ((), ())), preferred_element_...  184 us
    ppermute x5, waiting for transfers between devices, swap_micro(): return (own, lax.ppermute(sent, 'mb', SWAP))  144 us
    dot_general x5, matrix products, matmul_tn(): lax.dot_general(left, right, (((0,), (0,)), ((), ())), preferred_element_...  121 us
    pallas_call x2, Pallas kernels, conv_backward(): pl.pallas_call(back_kernel, out_shape=(jax.ShapeDtypeStruct((slots, *x.sh...  119 us
    ppermute x1, waiting for transfers between devices, on_device(): w1_got = lax.ppermute(w1_sent, 'mb', SWAP)  81.4 us
    pallas_call x2, Pallas kernels, conv_forward(): pl.pallas_call(kernel, out_shape=jax.ShapeDtypeStruct((48 * 48, 2 * width...  72.6 us
    unnamed x282, local copies, waits for them, and re-layouts  51.5 us
  transfers between devices with their start and end apart: 44, of which 18 were waited for; matrix products, arithmetic and copies ran while one was open for 44% of the time, Pallas kernels for 20%

profile of v2, /device:TPU:0, one launch (start us, length us, event | category | flops | bytes accessed | tf_op | source)
XLA Modules:
  0.0 1610.0 jit_solution(8060654471174721245)
XLA Ops:
  47.0 36.3 %shard_map.339.into_ref = bf16[2304,1536]{1,0:T(8,128)(2,1)} custom-call(s32[1]{0:T(128)} %bitcast.4.place_ref, bf16[48,36864]{1,0:T(8,128)(2,1)} %get-tuple-element.220.x_ref.own_ref, bf16[8,36864]{1,0:T(8,128)(2,1)} %get-tuple-element.252.top_ref, bf16[8,36864]{1,0:T(8,128)(2,1)} %get-tuple-element.251.bot_ref, f32[49,768]{1,0:T(8,128)} %convert_element_type.419.taps_ref, ...), custom_call_target="tpu_custom_call" | custom-call | flops 1387266048 | bytes 12000000 | tf_op jit(solution)/shard_map/pallas_call | solution.py:305
  83.2 88.3 %collective-permute-done.4 = bf16[2,8,36864]{2,1,0:T(8,128)(2,1)} collective-permute-done((bf16[2,8,36864]{2,1,0:T(8,128)(2,1)}, bf16[2,8,36864]{2,1,0:T(8,128)(2,1)}, u32[]{:S(2)}, u32[]{:S(2)}) %collective-permute-start.4) | collective-permute-done | bytes 1179680 | tf_op jit(solution)/shard_map/ppermute | solution.py:101
  175.7 36.4 %shard_map.340 = bf16[2304,1536]{1,0:T(8,128)(2,1)} custom-call(s32[1]{0:T(128)S(6)} %sub.30.place_ref, bf16[48,36864]{1,0:T(8,128)(2,1)} %copy-done.14, bf16[8,36864]{1,0:T(8,128)(2,1)} %get-tuple-element.254.top_ref, bf16[8,36864]{1,0:T(8,128)(2,1)} %get-tuple-element.253.bot_ref, ...), custom_call_target="tpu_custom_call", output_to_operand_aliasing={{}: (6, {})} | custom-call | flops 1387266048 | bytes 12000000 | tf_op jit(solution)/shard_map/pallas_call | solution.py:305
  223.7 38.0 %all-gather.5.cloned.1.call-done = bf16[3072,6144]{1,0:T(8,128)(2,1)} async-done(((bf16[96,6144]{1,0:T(8,128)(2,1)}), bf16[3072,6144]{1,0:T(8,128)(2,1)}) %all-gather.5.cloned.1.call-update) | async-done | bytes 37748752 | tf_op jit(solution)/shard_map/all_gather | solution.py:195
  314.0 31.4 %multiply_convert_fusion.3 = (bf16[2304,3072]{1,0:T(8,128)(2,1)}, f32[2304,3072]{1,0:T(8,128)}) fusion(bf16[2304,1536]{1,0:T(8,128)(2,1)S(1)} %bitcast.348, bf16[2,1536,6144]{2,1,0:T(8,128)(2,1)} %bitcast.398), kind=kOutput, calls=%fused_computation.16 | convolution fusion | flops 21778661376 | bytes 58982400 | tf_op jit(solution)/shard_map/dot_general | solution.py:42
  345.4 29.2 %fusion.33 = f32[2304,1536]{1,0:T(8,128)} fusion(bf16[2304,3072]{1,0:T(8,128)(2,1)} %get-tuple-element.304, bf16[2,1536,6144]{2,1,0:T(8,128)(2,1)} %bitcast.399), kind=kOutput, calls=%fused_computation.57 | convolution fusion | flops 21743271936 | bytes 37748736 | tf_op jit(solution)/shard_map/dot_general | solution.py:50
  374.6 31.1 %multiply_convert_fusion.2 = (bf16[2304,3072]{1,0:T(8,128)(2,1)}, f32[2304,3072]{1,0:T(8,128)}) fusion(bf16[2304,1536]{1,0:T(8,128)(2,1)S(1)} %bitcast.348, bf16[2,1536,6144]{2,1,0:T(8,128)(2,1)} %bitcast.400), kind=kOutput, calls=%fused_computation.14 | convolution fusion | flops 21778661376 | bytes 58982400 | tf_op jit(solution)/shard_map/dot_general | solution.py:42
  405.8 30.9 %convolution_add_fusion.1.branch_ref = f32[2304,1536]{1,0:T(8,128)} fusion(f32[2304,1536]{1,0:T(8,128)} %fusion.33, bf16[2304,3072]{1,0:T(8,128)(2,1)} %get-tuple-element.306, bf16[2,1536,6144]{2,1,0:T(8,128)(2,1)} %bitcast.401), kind=kOutput, calls=%fused_computation.31 | convolution fusion | flops 21746810880 | bytes 51904512 | tf_op jit(solution)/shard_map/dot_general | solution.py:50
  548.6 32.5 %shard_map.342 = (bf16[576,1024]{1,0:T(8,128)(2,1)}, f32[8,3,2,192]{3,2,1,0:T(2,128)}) custom-call(s32[3]{0:T(128)} %get-tuple-element.318.first_ref, s32[3]{0:T(128)} %get-tuple-element.317.last_ref, bf16[576,1024]{1,0:T(8,128)(2,1)} %pad_maximum_fusion.6.q_ref, bf16[576,1024]{1,0:T(8,128)(2,1)} %copy-done.111, bf16[576,1024]{1,0:T(8,128)(2,1)} %copy-done.54, ...), custom_call_target="tpu_custom_call" | custom-call | flops 20000000000 | bytes 20000000 | tf_op jit(solution)/shard_map/pallas_call | solution.py:628
  586.3 32.0 %collective-permute-done.15.other_ref.cot_ref = bf16[48,36864]{1,0:T(8,128)(2,1)} collective-permute-done((bf16[48,36864]{1,0:T(8,128)(2,1)}, bf16[48,36864]{1,0:T(8,128)(2,1)}, u32[]{:S(2)}, u32[]{:S(2)}) %collective-permute-start.15) | collective-permute-done | bytes 3538976 | tf_op jit(solution)/shard_map/ppermute | solution.py:101
  653.5 30.5 %shard_map.343 = bf16[1024,8192]{1,0:T(8,128)(2,1)} custom-call(bf16[1024,576]{1,0:T(8,128)(2,1)} %get-tuple-element.238.refs_0_, bf16[1024,576]{1,0:T(8,128)(2,1)} %fusion.189.refs_1_, bf16[576,4096]{1,0:T(8,128)(2,1)} %copy-done.35, bf16[576,4096]{1,0:T(8,128)(2,1)} %get-tuple-element.215.refs_3_), custom_call_target="tpu_custom_call" | custom-call | flops 9663676416 | bytes 16777216 | tf_op jit(solution)/shard_map/pallas_call | solution.py:183
  690.3 42.4 %shard_map.344 = (bf16[576,1024]{1,0:T(8,128)(2,1)}, f32[576,1024]{1,0:T(8,128)}, f32[576,1024]{1,0:T(8,128)}, bf16[2,576,1024]{2,1,0:T(8,128)(2,1)}, bf16[2,576,1024]{2,1,0:T(8,128)(2,1)}) custom-call(s32[3]{0:T(128)} %get-tuple-element.318.first_ref, s32[3]{0:T(128)} %get-tuple-element.317.last_ref, bf16[576,1024]{1,0:T(8,128)(2,1)} %pad_maximum_fusion.6.q_ref, ...), custom_call_target="tpu_custom_call" | custom-call | flops 20000000000 | bytes 20000000 | tf_op jit(solution)/shard_map/pallas_call | solution.py:716
  765.5 42.7 %collective-permute-start.21 = (bf16[1,24,1024]{1,2,0:T(8,128)(2,1)}, bf16[1,24,1024]{1,2,0:T(8,128)(2,1)}, u32[]{:S(2)}, u32[]{:S(2)}) collective-permute-start(bf16[1,24,1024]{1,2,0:T(8,128)(2,1)} %get-tuple-element.239), channel_id=1, source_target_pairs={{0,2},{2,4},{4,6},{6,8},{8,10},{10,12},{12,14},{14,16},{16,18},{18... | collective-permute-start | bytes 147464 | tf_op jit(solution)/shard_map/ppermute | solution.py:36
  865.6 33.8 %reduce-scatter.7.cloned.1.call-done = bf16[64,8192]{1,0:T(8,128)(2,1)} async-done(((bf16[1024,8192]{1,0:T(8,128)(2,1)}), bf16[64,8192]{1,0:T(8,128)(2,1)}) %reduce-scatter.7.cloned.1.call-update) | async-done | bytes 1048592 | tf_op jit(solution)/shard_map/reduce_scatter | solution.py:200
  919.6 29.5 %convolution_convert_fusion.2 = bf16[1536,3072]{1,0:T(8,128)(2,1)} fusion(bf16[2304,1536]{1,0:T(8,128)(2,1)} %get-tuple-element.92, bf16[2304,3072]{1,0:T(8,128)(2,1)} %get-tuple-element.306), kind=kOutput, calls=%fused_computation.41 | convolution fusion | flops 21747990528 | bytes 30670848 | tf_op jit(solution)/shard_map/dot_general | solution.py:46
  949.1 29.0 %convolution_convert_fusion.3 = bf16[1536,3072]{1,0:T(8,128)(2,1)} fusion(bf16[2304,1536]{1,0:T(8,128)(2,1)} %get-tuple-element.92, bf16[2304,3072]{1,0:T(8,128)(2,1)} %get-tuple-element.304), kind=kOutput, calls=%fused_computation.42 | convolution fusion | flops 21747990528 | bytes 30670848 | tf_op jit(solution)/shard_map/dot_general | solution.py:46
  1031.2 36.7 %multiply_convert_fusion.1 = bf16[2304,3072]{1,0:T(8,128)(2,1)S(1)} fusion(bf16[2304,1536]{1,0:T(8,128)(2,1)} %get-tuple-element.92, f32[2304,3072]{1,0:T(8,128)} %get-tuple-element.305, bf16[2,1536,6144]{2,1,0:T(8,128)(2,1)} %bitcast.402), kind=kOutput, calls=%fused_computation.13 | convolution fusion | flops 21828206592 | bytes 58982400 | tf_op jit(solution)/shard_map/dot_general | solution.py:42
  1099.2 38.8 %multiply_convert_fusion = bf16[2304,3072]{1,0:T(8,128)(2,1)} fusion(bf16[2304,1536]{1,0:T(8,128)(2,1)} %get-tuple-element.92, f32[2304,3072]{1,0:T(8,128)} %get-tuple-element.307, bf16[2,1536,6144]{2,1,0:T(8,128)(2,1)} %bitcast.403), kind=kOutput, calls=%fused_computation.12 | convolution fusion | flops 21828206592 | bytes 58982400 | tf_op jit(solution)/shard_map/dot_general | solution.py:42
  1138.0 29.7 %broadcast_select_fusion = (bf16[1536,3072]{1,0:T(8,128)(2,1)}, bf16[1536,3072]{1,0:T(8,128)(2,1)}) fusion(bf16[1536,3072]{1,0:T(8,128)(2,1)S(1)} %bitcast.344, pred[]{:T(512)S(6)} %eq.30, bf16[2304,1536]{1,0:T(8,128)(2,1)} %fusion.16, bf16[2304,3072]{1,0:T(8,128)(2,1)} %multiply_convert_fusion), kind=kOutput, calls=%fused_computation.65 | convolution fusion | flops 21752709120 | bytes 49545216 | tf_op jit(solution)/shard_map/dot_general | solution.py:46
  1167.8 29.6 %fusion.35 = f32[2304,1536]{1,0:T(8,128)} fusion(bf16[2304,3072]{1,0:T(8,128)(2,1)} %copy-done.114, bf16[2,1536,6144]{2,1,0:T(8,128)(2,1)} %bitcast.404), kind=kOutput, calls=%fused_computation.59 | convolution fusion | flops 21743271936 | bytes 37748736 | tf_op jit(solution)/shard_map/dot_general | solution.py:50
  1198.8 32.6 %fusion.18 = (f32[2304]{0:T(1024)S(1)}, bf16[2304,1536]{1,0:T(8,128)(2,1)}) fusion(bf16[2304,1536]{1,0:T(8,128)(2,1)} %shard_map.340, f32[1536]{0:T(1024)S(1)} %copy-done.71, f32[2304]{0:T(1024)S(1)} %copy-done.63, f32[2304,1536]{1,0:T(8,128)} %fusion.35, bf16[2304,3072]{1,0:T(8,128)(2,1)} %multiply_convert_fusion, bf16[2,1536,6144]{2,1,0:T(8,128)(2,1)} %bitcast.405), kind=kOutput, calls=%fused_computation.34 | convolution fusion | flops 21771581440 | bytes 51929088 | tf_op jit(solution)/shard_map/dot_general | solution.py:50
  1260.6 59.0 %shard_map.347 = (bf16[1,48,36864]{2,1,0:T(8,128)(2,1)}, f32[56,768]{1,0:T(8,128)}) custom-call(s32[1]{0:T(128)S(6)} %sub.30.place_ref, bf16[2304,1536]{1,0:T(8,128)(2,1)} %copy-done.7, bf16[48,8,1536]{2,1,0:T(8,128)(2,1)} %copy-done.34, bf16[48,8,1536]{2,1,0:T(8,128)(2,1)} %copy-done.33, bf16[48,36864]{1,0:T(8,128)(2,1)} %copy-done.14, ...), custom_call_target="tpu_custom_call" | custom-call | flops 2774532096 | bytes 25000000 | tf_op jit(solution)/shard_map/pallas_call | solution.py:411
  1319.5 81.4 %collective-permute-done.23 = bf16[1536,3072]{1,0:T(8,128)(2,1)} collective-permute-done((bf16[1536,3072]{1,0:T(8,128)(2,1)}, bf16[1536,3072]{1,0:T(8,128)(2,1)}, u32[]{:S(2)}, u32[]{:S(2)}) %collective-permute-start.23) | collective-permute-done | bytes 9437216 | tf_op jit(solution)/shard_map/ppermute | solution.py:994
  1417.0 59.9 %shard_map.348 = (f32[2,48,36864]{2,1,0:T(8,128)}, f32[56,768]{1,0:T(8,128)}) custom-call(s32[1]{0:T(128)} %bitcast.4.place_ref, bf16[2304,1536]{1,0:T(8,128)(2,1)} %copy-done.7, bf16[48,8,1536]{2,1,0:T(8,128)(2,1)} %copy-done.34, bf16[48,8,1536]{2,1,0:T(8,128)(2,1)} %copy-done.33, bf16[48,36864]{1,0:T(8,128)(2,1)} %get-tuple-element.220.x_ref.own_ref, ...), custom_call_target="tpu_custom_call" | custom-call | flops 2774532096 | bytes 25000000 | tf_op jit(solution)/shard_map/pallas_call | solution.py:411
  (584 shorter events, 632.0 us)
Async XLA Ops:
  7.2 254.4 %all-gather.5.cloned.1.call-start = ((), (), s32[]{:S(2)}) async-start(), calls=%async_computation.12 | async-start | bytes 38928384 | tf_op jit(solution)/shard_map/all_gather | solution.py:195
  9.6 449.8 %all-gather.7.cloned.1.call-start = ((), (), s32[]{:S(2)}) async-start(), calls=%async_computation.13 | async-start | bytes 33521664 | tf_op jit(solution)/shard_map/all_gather | solution.py:195
  9.7 29.0 %collective-permute-start.5 = (bf16[49,768]{1,0:T(8,128)(2,1)}, bf16[49,768]{1,0:T(8,128)(2,1)}, u32[]{:S(2)}, u32[]{:S(2)}) collective-permute-start(bf16[49,768]{1,0:T(8,128)(2,1)} %param.23), channel_id=1, source_target_pairs={{0,1},{1,0},{2,3},{3,2},{4,5},{5,4},{6,7},{7,6},{8,9},{9,8},{10,11... | collective-permute-start | bytes 225800 | tf_op jit(solution)/shard_map/ppermute | solution.py:812
  15.9 24.4 %collective-permute-start.3 = (bf16[2,8,36864]{2,1,0:T(8,128)(2,1)}, bf16[2,8,36864]{2,1,0:T(8,128)(2,1)}, u32[]{:S(2)}, u32[]{:S(2)}) collective-permute-start(bf16[2,8,36864]{2,1,0:T(8,128)(2,1)} %get-tuple-element.222), channel_id=1, source_target_pairs={{2,0},{4,2},{6,4},{8,6},{10,8},{12,10},{14,12},{16,14},{18,16},{20... | collective-permute-start | bytes 3538952 | tf_op jit(solution)/shard_map/ppermute | solution.py:28
  17.2 23.1 %collective-permute-start.2 = (bf16[2,8,36864]{2,1,0:T(8,128)(2,1)}, bf16[2,8,36864]{2,1,0:T(8,128)(2,1)}, u32[]{:S(2)}, u32[]{:S(2)}) collective-permute-start(bf16[2,8,36864]{2,1,0:T(8,128)(2,1)} %get-tuple-element.223), channel_id=1, source_target_pairs={{0,2},{2,4},{4,6},{6,8},{8,10},{10,12},{12,14},{14,16},{16,18},{18... | collective-permute-start | bytes 3538952 | tf_op jit(solution)/shard_map/ppermute | solution.py:27
  28.5 145.4 %collective-permute-start = (bf16[48,36864]{1,0:T(8,128)(2,1)}, bf16[48,36864]{1,0:T(8,128)(2,1)S(1)}, u32[]{:S(2)}, u32[]{:S(2)}) collective-permute-start(bf16[48,36864]{1,0:T(8,128)(2,1)} %get-tuple-element.221), channel_id=1, source_target_pairs={{0,1},{1,0},{2,3},{3,2},{4,5},{5,4},{6,7},{7,6},{8,9},{9,8},{10,11... | collective-permute-start | bytes 10616840 | tf_op jit(solution)/shard_map/ppermute | solution.py:101
  43.1 128.4 %collective-permute-start.4 = (bf16[2,8,36864]{2,1,0:T(8,128)(2,1)}, bf16[2,8,36864]{2,1,0:T(8,128)(2,1)}, u32[]{:S(2)}, u32[]{:S(2)}) collective-permute-start(bf16[2,8,36864]{2,1,0:T(8,128)(2,1)} %get-tuple-element.230), channel_id=1, source_target_pairs={{0,1},{1,0},{2,3},{3,2},{4,5},{5,4},{6,7},{7,6},{8,9},{9,8},{10,11... | collective-permute-start | bytes 3538952 | tf_op jit(solution)/shard_map/ppermute | solution.py:101
  262.8 636.6 %reduce-scatter.7.cloned.1.call-start = ((), (), s32[]{:S(2)}) async-start(), calls=%async_computation.6 | async-start | bytes 17825792 | tf_op jit(solution)/shard_map/reduce_scatter | solution.py:200
  270.7 23.9 %collective-permute-start.17 = (bf16[576,512]{1,0:T(8,128)(2,1)}, bf16[576,512]{1,0:T(8,128)(2,1)}, u32[]{:S(2)}, u32[]{:S(2)}) collective-permute-start(bf16[576,512]{1,0:T(8,128)(2,1)} %get-tuple-element.246), channel_id=1, source_target_pairs={{0,1},{1,0},{2,3},{3,2},{4,5},{5,4},{6,7},{7,6},{8,9},{9,8},{10,11... | collective-permute-start | bytes 1769480 | tf_op jit(solution)/shard_map/ppermute | solution.py:101
  276.1 29.8 %collective-permute-start.1 = (bf16[576,512]{1,0:T(8,128)(2,1)}, bf16[576,512]{1,0:T(8,128)(2,1)}, u32[]{:S(2)}, u32[]{:S(2)}) collective-permute-start(bf16[576,512]{1,0:T(8,128)(2,1)} %get-tuple-element.248), channel_id=1, source_target_pairs={{0,1},{1,0},{2,3},{3,2},{4,5},{5,4},{6,7},{7,6},{8,9},{9,8},{10,11... | collective-permute-start | bytes 1769480 | tf_op jit(solution)/shard_map/ppermute | solution.py:101
  453.9 132.4 %collective-permute-start.14 = (bf16[1,48,36864]{2,1,0:T(8,128)(2,1)}, bf16[1,48,36864]{2,1,0:T(8,128)(2,1)}, u32[]{:S(2)}, u32[]{:S(2)}) collective-permute-start(bf16[1,48,36864]{2,1,0:T(8,128)(2,1)} %get-tuple-element.74), channel_id=1, source_target_pairs={{0,1},{1,0},{2,3},{3,2},{4,5},{5,4},{6,7},{7,6},{8,9},{9,8},{10,11... | collective-permute-start | bytes 10616840 | tf_op jit(solution)/shard_map/ppermute | solution.py:916
  515.1 24.1 %collective-permute-start.11 = (bf16[576,1024]{1,0:T(8,128)(2,1)S(1)}, bf16[576,1024]{1,0:T(8,128)(2,1)S(1)}, u32[]{:S(2)}, u32[]{:S(2)}) collective-permute-start(bf16[576,1024]{1,0:T(8,128)(2,1)S(1)} %pad_maximum_fusion.7.k_ref), channel_id=1, source_target_pairs={{2,0},{4,2},{6,4},{8,6},{10,8},{12,10},{14,12},{16,14},{18,16},{20... | collective-permute-start | bytes 3538952 | tf_op jit(solution)/shard_map/ppermute | solution.py:28
  518.5 27.0 %collective-permute-start.10 = (bf16[576,1024]{1,0:T(8,128)(2,1)S(1)}, bf16[576,1024]{1,0:T(8,128)(2,1)S(1)}, u32[]{:S(2)}, u32[]{:S(2)}) collective-permute-start(bf16[576,1024]{1,0:T(8,128)(2,1)S(1)} %pad_maximum_fusion.7.k_ref), channel_id=1, source_target_pairs={{0,2},{2,4},{4,6},{6,8},{8,10},{10,12},{12,14},{14,16},{16,18},{18... | collective-permute-start | bytes 3538952 | tf_op jit(solution)/shard_map/ppermute | solution.py:27
  539.2 79.1 %collective-permute-start.15 = (bf16[48,36864]{1,0:T(8,128)(2,1)}, bf16[48,36864]{1,0:T(8,128)(2,1)}, u32[]{:S(2)}, u32[]{:S(2)}) collective-permute-start(bf16[48,36864]{1,0:T(8,128)(2,1)} %get-tuple-element.219), channel_id=1, source_target_pairs={{0,1},{1,0},{2,3},{3,2},{4,5},{5,4},{6,7},{7,6},{8,9},{9,8},{10,11... | collective-permute-start | bytes 10616840 | tf_op jit(solution)/shard_map/ppermute | solution.py:101
  684.0 812.4 %reduce-scatter.15.cloned.1.call-start = ((), (), s32[]{:S(2)}) async-start(), calls=%async_computation.10 | async-start | bytes 5849088 | tf_op jit(solution)/shard_map/reduce_scatter | solution.py:200
  765.5 76.4 %collective-permute-start.21 = (bf16[1,24,1024]{1,2,0:T(8,128)(2,1)}, bf16[1,24,1024]{1,2,0:T(8,128)(2,1)}, u32[]{:S(2)}, u32[]{:S(2)}) collective-permute-start(bf16[1,24,1024]{1,2,0:T(8,128)(2,1)} %get-tuple-element.239), channel_id=1, source_target_pairs={{0,2},{2,4},{4,6},{6,8},{8,10},{10,12},{12,14},{14,16},{16,18},{18... | collective-permute-start | bytes 147464 | tf_op jit(solution)/shard_map/ppermute | solution.py:36
  808.2 35.4 %collective-permute-start.22 = (bf16[1,24,1024]{1,2,0:T(8,128)(2,1)}, bf16[1,24,1024]{1,2,0:T(8,128)(2,1)}, u32[]{:S(2)}, u32[]{:S(2)}) collective-permute-start(bf16[1,24,1024]{1,2,0:T(8,128)(2,1)} %get-tuple-element.240), channel_id=1, source_target_pairs={{2,0},{4,2},{6,4},{8,6},{10,8},{12,10},{14,12},{16,14},{18,16},{20... | collective-permute-start | bytes 147464 | tf_op jit(solution)/shard_map/ppermute | solution.py:37
  899.5 674.9 %reduce-scatter.11.cloned.1.call-start = ((), (), s32[]{:S(2)}) async-start(), calls=%async_computation.8 | async-start | bytes 10027008 | tf_op jit(solution)/shard_map/reduce_scatter | solution.py:200
  978.2 597.3 %reduce-scatter.13.cloned.1.call-start = ((), (), s32[]{:S(2)}) async-start(), calls=%async_computation.9 | async-start | bytes 10027008 | tf_op jit(solution)/shard_map/reduce_scatter | solution.py:200
  992.5 585.9 %reduce-scatter.17.cloned.1.call-start = ((), (), s32[]{:S(2)}) async-start(), calls=%async_computation.11 | async-start | bytes 10584064 | tf_op jit(solution)/shard_map/reduce_scatter | solution.py:200
  1099.2 501.6 %reduce-scatter.9.cloned.1.call-start = ((), (), s32[]{:S(2)}) async-start(), calls=%async_computation.7 | async-start | bytes 10027008 | tf_op jit(solution)/shard_map/reduce_scatter | solution.py:200
  1197.4 203.5 %collective-permute-start.23 = (bf16[1536,3072]{1,0:T(8,128)(2,1)}, bf16[1536,3072]{1,0:T(8,128)(2,1)}, u32[]{:S(2)}, u32[]{:S(2)}) collective-permute-start(bf16[1536,3072]{1,0:T(8,128)(2,1)} %get-tuple-element.95), channel_id=1, source_target_pairs={{0,1},{1,0},{2,3},{3,2},{4,5},{5,4},{6,7},{7,6},{8,9},{9,8},{10,11... | collective-permute-start | bytes 28311560 | tf_op jit(solution)/shard_map/ppermute | solution.py:994
  1414.1 137.6 %collective-permute-start.26 = (bf16[1,48,36864]{2,1,0:T(8,128)(2,1)}, bf16[1,48,36864]{2,1,0:T(8,128)(2,1)}, u32[]{:S(2)}, u32[]{:S(2)}) collective-permute-start(bf16[1,48,36864]{2,1,0:T(8,128)(2,1)} %get-tuple-element.99), channel_id=1, source_target_pairs={{0,1},{1,0},{2,3},{3,2},{4,5},{5,4},{6,7},{7,6},{8,9},{9,8},{10,11... | collective-permute-start | bytes 10616840 | tf_op jit(solution)/shard_map/ppermute | solution.py:1029
  1416.3 100.7 %collective-permute-start.35 = (bf16[64,4096]{1,0:T(8,128)(2,1)}, bf16[64,4096]{1,0:T(8,128)(2,1)}, u32[]{:S(2)}, u32[]{:S(2)}) collective-permute-start(bf16[64,4096]{1,0:T(8,128)(2,1)} %pad_maximum_fusion.11), channel_id=1, source_target_pairs={{0,1},{1,0},{2,3},{3,2},{4,5},{5,4},{6,7},{7,6},{8,9},{9,8},{10,11... | collective-permute-start | bytes 1572872 | tf_op jit(solution)/shard_map/ppermute | solution.py:210
  (150 other events, 1997.6 us)
Sparse Core Ops, SparseCore 0:
  11.5 250.1 all-gather.4
  265.2 191.4 all-gather.6
  684.1 215.2 reduce-scatter.6
  903.2 80.4 reduce-scatter.14
  988.1 110.3 reduce-scatter.10
  1102.5 111.1 reduce-scatter.12
  1218.4 128.3 reduce-scatter.16
  1417.1 121.0 reduce-scatter.8

commit v3 on v2

--- a/solution.py
+++ b/solution.py
@@ -17,24 +17,29 @@
 NEG = -1e30
 BF = jnp.bfloat16
 F32 = jnp.float32
-ALL = ("mb", "tile")
+TILE = ("chip", "core")
+ALL = ("mb", *TILE)
+
+
+def tile_count():
+    return lax.axis_size("chip") * lax.axis_size("core")
 
 
 def rim_pair(value, width, axis):
-    devices, length = lax.axis_size("tile"), value.shape[axis]
+    devices, length = tile_count(), value.shape[axis]
     up = [(i, (i + 1) % devices) for i in range(devices - 1)]
     down = [(j, i) for i, j in up]
-    before = lax.ppermute(lax.slice_in_dim(value, length - width, length, axis=axis), "tile", up)
-    after = lax.ppermute(lax.slice_in_dim(value, 0, width, axis=axis), "tile", down)
+    before = lax.ppermute(lax.slice_in_dim(value, length - width, length, axis=axis), TILE, up)
+    after = lax.ppermute(lax.slice_in_dim(value, 0, width, axis=axis), TILE, down)
     return before, after
 
 
 def rim_rows(value, width):
-    devices, length = lax.axis_size("tile"), value.shape[0]
+    devices, length = tile_count(), value.shape[0]
     up = [(i, (i + 1) % devices) for i in range(devices - 1)]
     down = [(j, i) for i, j in up]
-    before = lax.ppermute(value[length - width :], "tile", up)
-    after = lax.ppermute(value[:width], "tile", down)
+    before = lax.ppermute(value[length - width :], TILE, up)
+    after = lax.ppermute(value[:width], TILE, down)
     return jnp.concatenate([before, value, after], axis=0)
 
 
@@ -170,12 +175,13 @@
 
 def stacked_grads(lefts, rights):
     widths = [item.shape[1] for item in rights]
-    if any(width % CHUNK for width in widths):
+    step_width = next((size for size in (512, 256) if not any(width % size for width in widths)), 0)
+    if not step_width:
         return jnp.concatenate(
             [matmul_tn(left, right).astype(BF) for left, right in zip(lefts, rights)], axis=1
         )
     tokens, rows = lefts[0].shape
-    cuts = [int(item) for item in np.cumsum([0] + [width // CHUNK for width in widths])]
+    cuts = [int(item) for item in np.cumsum([0] + [width // step_width for width in widths])]
 
     def column(i):
         return lambda step: (0, jnp.clip(step - cuts[i], 0, cuts[i + 1] - cuts[i] - 1))
@@ -185,9 +191,9 @@
         out_shape=jax.ShapeDtypeStruct((rows, sum(widths)), BF),
         grid=(cuts[-1],),
         in_specs=[pl.BlockSpec((rows, tokens), lambda step: (0, 0)) for _ in lefts]
-        + [pl.BlockSpec((tokens, CHUNK), column(i)) for i in range(len(rights))],
-        out_specs=pl.BlockSpec((rows, CHUNK), lambda step: (0, step)),
-        **conv_params(2 * tokens * rows * sum(widths), 2 * rows * sum(widths)),
+        + [pl.BlockSpec((tokens, step_width), column(i)) for i in range(len(rights))],
+        out_specs=pl.BlockSpec((rows, step_width), lambda step: (0, step)),
+        **conv_params(5 * tokens * rows * sum(widths), 2 * rows * sum(widths)),
     )(*[left.T for left in lefts], *rights)
 
 
@@ -197,7 +203,27 @@
 
 
 def reduce_tiles(terms):
-    return lax.psum_scatter(terms, "tile", scatter_dimension=0, tiled=True)
+    return lax.psum_scatter(terms, TILE, scatter_dimension=0, tiled=True)
+
+
+def core_sum(terms):
+    width = terms.shape[1] // 2
+    core = lax.axis_index("core")
+    own = lax.dynamic_slice_in_dim(terms, core * width, width, 1)
+    sent = lax.dynamic_slice_in_dim(terms, (1 - core) * width, width, 1)
+    got = lax.ppermute(sent, "core", SWAP)
+    return (own.astype(F32) + got.astype(F32)).astype(BF)
+
+
+def reduce_chips(terms):
+    both = lax.psum_scatter(terms, "chip", scatter_dimension=0, tiled=True)
+    rows = both.shape[0] // 2
+    core = lax.axis_index("core")
+    own = lax.dynamic_slice_in_dim(both, core * rows, rows, 0)
+    sent = lax.dynamic_slice_in_dim(both, (1 - core) * rows, rows, 0)
+    got = lax.ppermute(sent, "core", SWAP)
+    first = core == 0
+    return jnp.concatenate([jnp.where(first, own, got), jnp.where(first, got, own)], axis=1)
 
 
 def settle(summed, widths):
@@ -215,12 +241,12 @@
 
 
 def sum_everywhere(flat):
-    devices = lax.axis_size("tile")
+    devices = tile_count()
     if devices & (devices - 1):
-        return lax.psum(flat, "tile")
+        return lax.psum(flat, TILE)
     bit = 1
     while bit < devices:
-        flat = flat + lax.ppermute(flat, "tile", [(i, i ^ bit) for i in range(devices)])
+        flat = flat + lax.ppermute(flat, TILE, [(i, i ^ bit) for i in range(devices)])
         bit *= 2
     return flat
 
@@ -323,7 +349,7 @@
             ],
         ),
         input_output_aliases={} if into is None else {6: 0},
-        **conv_params(2 * 49 * 48 * 48 * width * 8, 12_000_000),
+        **conv_params(54_000_000 * width, 12_000_000),
     )(place, x, top, bot, taps, mask, *extra)
 
 
@@ -438,7 +464,7 @@
                 pltpu.VMEM((24, 48, LANES), F32),
             ],
         ),
-        **conv_params(4 * 49 * 48 * 48 * width * 8, 25_000_000),
+        **conv_params(90_000_000 * width, 25_000_000),
     )(place, grad, top, bot, x, cot, pool, taps, mask)
 
 
@@ -642,7 +668,7 @@
             out_specs=(block, stats),
             scratch_shapes=[pltpu.VMEM((window, WIDE), BF), pltpu.VMEM((window, WIDE), BF)],
         ),
-        **conv_params(20_000_000_000, 20_000_000),
+        **conv_params(40_000_000 * width, 20_000_000),
     )(first, last, q, around[0], k, around[1], around[2], v, around[3], klab, qlab)
 
 
@@ -739,7 +765,7 @@
                 pltpu.VMEM((window, WIDE), F32),
             ],
         ),
-        **conv_params(20_000_000_000, 20_000_000),
+        **conv_params(55_000_000 * width, 20_000_000),
     )(first, last, q, around[0], k, around[1], around[2], v, around[3], grad, out, total, klab, qlab)
 
 
@@ -773,7 +799,7 @@
     tok_count = row_count * col_count
     pix_count = hi_rows * hi_cols
     mine = lax.axis_index("mb")
-    row_start = lax.axis_index("tile") * row_count
+    row_start = lax.axis_index(TILE) * row_count
     head_count = d_own // HDIM
 
     fast = c_shard % LANES == 0 and lax.axis_size("tp") == 1
@@ -781,14 +807,8 @@
     hi_own, hi_other = swap_micro(hi_raw)
     up, down = rim_pair(hi_raw, RIM, 1)
     own_rims, other_rims = swap_micro(jnp.stack([up, down], axis=1))
-    lo_in, d_lo_out, cn_scale, ad_kernel, hi_other = together(
-        lo_in, d_lo_out, cn_scale, ad_kernel, hi_other
-    )
-    lo_low = in_order(*swap_micro(lo_in.reshape(2, tok_count, d_shard)), 1)
-    lo_field = lo_low.astype(F32)
-
     hid_shard, gh_shard, ff_shard = cn_w1.shape[1], gate_w1.shape[1], fc1.shape[1]
-    mlp = gather_all(jnp.concatenate([cn_w1, cn_w2.T], axis=1))
+    mlp = gather_all(jnp.concatenate([cn_w1, cn_w2.T, ad_proj, gate_w1], axis=1))
     def apply(left, pair):
         return jnp.concatenate([matmul(left, pair[0]), matmul(left, pair[1])], axis=1)
 
@@ -811,8 +831,6 @@
 
     other_kernel = lax.ppermute(cn_kernel, "mb", SWAP)
     conv_taps = in_order(cn_kernel, other_kernel, 1)
-    ad_taps = both_shards(ad_kernel, 1)
-    hi_scale = both_shards(cn_scale, 0).astype(F32)
 
     own_place = mine.reshape(1).astype(jnp.int32)
     other_place = 1 - own_place
@@ -842,9 +860,9 @@
     normed, norm_pull = jax.vjp(layer_norm, conv_full.astype(F32), cn_gain.astype(F32))
     normed_low, mlp, gate_w2 = together(normed.astype(BF), mlp, gate_w2)
     mlp_in = [mlp[g, :, :hid_shard] for g in range(2)]
-    mlp_out = [mlp[g, :, hid_shard:] for g in range(2)]
-    ad_shard = jnp.concatenate([ad_proj, gate_w1], axis=1)
-    narrow = gate_w2.shape[1]
+    mlp_out = [mlp[g, :, hid_shard : 2 * hid_shard] for g in range(2)]
+    ad_matrix = [mlp[g, :, 2 * hid_shard : 2 * hid_shard + d_shard] for g in range(2)]
+    gate_in = [mlp[g, :, 2 * hid_shard + d_shard :] for g in range(2)]
     vit = gather_all(
         jnp.concatenate(
             [
@@ -855,7 +873,6 @@
                 out_proj.T,
                 fc1,
                 fc2.T,
-                ad_shard.reshape(narrow, -1),
             ],
             axis=1,
         )
@@ -864,11 +881,16 @@
     gate_out, q_w, k_w, v_w, out_w, ff_in, ff_out = [
         [vit[g, :, int(cuts[i]) : int(cuts[i + 1])] for g in range(2)] for i in range(7)
     ]
-    ad_gate = vit[:, :, int(cuts[7]) :].reshape(2, -1, ad_shard.shape[1])
-    ad_matrix = [ad_gate[g, :, :d_shard] for g in range(2)]
-    gate_in = [ad_gate[g, :, d_shard:] for g in range(2)]
 
     inner_act, inner_slope = zip(*[gelu_pair(matmul(normed_low, mlp_in[g])) for g in range(2)])
+    lo_in, d_lo_out, cn_scale, ad_kernel, first_act = together(
+        lo_in, d_lo_out, cn_scale, ad_kernel, inner_act[0]
+    )
+    inner_act = (first_act, inner_act[1])
+    lo_low = in_order(*swap_micro(lo_in.reshape(2, tok_count, d_shard)), 1)
+    lo_field = lo_low.astype(F32)
+    ad_taps = both_shards(ad_kernel, 1)
+    hi_scale = both_shards(cn_scale, 0).astype(F32)
     branch = partial_sums(
         matmul_nt(inner_act[0], mlp_out[0]) + matmul_nt(inner_act[1], mlp_out[1])
     )
@@ -914,7 +936,7 @@
     mixed_two = mixed_one + partial_sums(apply_t(attended, out_w))
     if fast:
         hi_got = lax.ppermute(hi_sent, "mb", SWAP)
-        mixed_two, hi_got, cot_other = together(mixed_two, hi_got, cot_other)
+        mixed_two, hi_got = together(mixed_two, hi_got)
     mixed2_full = features(mixed_two.astype(BF))
     norm_two, second_pull = jax.vjp(layer_norm, mixed2_full.astype(F32), ln2_gain.astype(F32))
     norm2_low = norm_two.astype(BF)
@@ -928,17 +950,17 @@
     second_grad = partial_sums(apply_t(ff_pre_grad, ff_in)).astype(BF)
     back_two, grad_ln2 = second_pull(features(second_grad).astype(F32))
     p_ff = stacked_grads([norm2_low, ff_grad_full], [ff_pre_grad, ff_hidden])
-    grad_two, p_ff = together(grad_out + own_slice(back_two), p_ff)
+    grad_two, p_ff, cot_other = together(grad_out + own_slice(back_two), p_ff, cot_other)
     s_ff = reduce_tiles(p_ff)
     att_grad_full = features(grad_two.astype(BF))
     att_grad = apply(att_grad_full, out_w).astype(BF)
     query_grad, key_own, value_own, to_before, to_after = attend_back(
         queries, key_rows, value_rows, around, att_grad, attended, log_total, query_lab, key_lab, first, last
     )
-    devices = lax.axis_size("tile")
+    devices = tile_count()
     steps = [(i, i + 1) for i in range(devices - 1)]
-    from_before = lax.ppermute(to_after, "tile", steps)
-    from_after = lax.ppermute(to_before, "tile", [(j, i) for i, j in steps])
+    from_before = lax.ppermute(to_after, TILE, steps)
+    from_after = lax.ppermute(to_before, TILE, [(j, i) for i, j in steps])
     key_grad, value_grad = [
         (own + from_before[i].astype(F32) + from_after[i].astype(F32)).astype(BF)
         for i, own in enumerate((key_own, value_own))
@@ -965,7 +987,7 @@
     grad_ad_kernel = tap_grads(proj_pad, local_grad, small_ids, lo_mid, 3)
     p_ad = matmul_tn(pooled_full, jnp.concatenate([proj_grad, hidden_grad], axis=1)).astype(BF)
     pooled_grad = partial_sums(apply_t(hidden_grad, gate_in) + apply_t(proj_grad, ad_matrix))
-    pooled_grad, p_att, p_ad, s_ff = together(pooled_grad, p_att, p_ad, s_ff)
+    pooled_grad, p_att, p_ad = together(pooled_grad, p_att, p_ad)
     s_att, s_ad = reduce_tiles(p_att), reduce_tiles(p_ad)
     pool_cols = pooled_grad.reshape(row_count, col_count, c_own).transpose(1, 0, 2)
     if fast:
@@ -980,34 +1002,38 @@
         grad_scale = jnp.sum(grad_cols * branch, axis=0)
         scaled_grad = (grad_cols * hi_scale).astype(BF)
     branch_full = lax.optimization_barrier(features(scaled_grad))
+    first = mine == 0
     p_w2 = [matmul_tn(branch_full, act).astype(BF) for act in inner_act]
-    branch_full, *p_w2 = together(branch_full, *p_w2)
+    branch_full, *p_w2, s_ff = together(branch_full, *p_w2, s_ff)
     s_w2 = [reduce_tiles(item) for item in p_w2]
     grad_first = (matmul(branch_full, mlp_out[0]) * inner_slope[0].astype(F32)).astype(BF)
     w1_first = matmul_tn(normed_low, grad_first).astype(BF)
     branch_full, w1_first = together(branch_full, w1_first)
+    core_first = core_sum(w1_first)
     grad_second = (matmul(branch_full, mlp_out[1]) * inner_slope[1].astype(F32)).astype(BF)
     w1_second = matmul_tn(normed_low, grad_second).astype(BF)
-    w1_sent = jnp.where(mine == 0, w1_second, w1_first)
-    w1_own = jnp.where(mine == 0, w1_first, w1_second)
-    grad_second, w1_sent = together(grad_second, w1_sent)
-    w1_got = lax.ppermute(w1_sent, "mb", SWAP)
+    grad_second, w1_second = together(grad_second, w1_second)
+    core_second = core_sum(w1_second)
     normed_grad = partial_sums(
         matmul_nt(grad_first, mlp_in[0]) + matmul_nt(grad_second, mlp_in[1])
     ).astype(BF)
     back_conv, grad_cn_gain = norm_pull(features(normed_grad).astype(F32))
-    conv_grad = own_slice(back_conv).astype(BF)
+    conv_grad, core_first, core_second = together(
+        own_slice(back_conv).astype(BF), core_first, core_second
+    )
+    w1_sent, w1_own = jnp.where(first, core_second, core_first), jnp.where(first, core_first, core_second)
+    w1_got = lax.ppermute(w1_sent, "mb", SWAP)
     conv_cols = conv_grad.reshape(hi_cols, hi_rows, c_own)
     grad_up, grad_down = rim_pair(conv_cols, RIM, 1)
     if fast:
         ghi_sent, taps_other = conv_backward(
             conv_grad, grad_up, grad_down, hi_other, cot_other, pool_cols, other_taps, mask, other_place, 1, BF
         )
-        w1_sum = (w1_own.astype(F32) + w1_got.astype(F32)).astype(BF)
-        conv_grad, w1_sum, ghi_sent = together(conv_grad, w1_sum, ghi_sent)
+        conv_grad, ghi_sent, w1_got = together(conv_grad, ghi_sent, w1_got)
         ghi_mine, taps_own = conv_backward(
             conv_grad, grad_up, grad_down, hi_own, cot_own, pool_cols, own_taps, mask, own_place, 2, F32
         )
+        w1_sum = (w1_own.astype(F32) + w1_got.astype(F32)).astype(BF)
         grad_cn_kernel = in_order(taps_own[:49], taps_other[:49], 1)
     else:
         conv_grad = conv_cols.transpose(1, 0, 2)
@@ -1017,7 +1043,25 @@
         hi_back = hi_grad + depthwise(conv_pad, conv_taps, hi_ids, hi_mid, 7, True)
         grad_cn_kernel = tap_grads(hi_pad, conv_grad, hi_ids, hi_mid, 7)
         w1_sum = (w1_own.astype(F32) + w1_got.astype(F32)).astype(BF)
-    g_w1 = reduce_tiles(w1_sum).astype(F32)
+    w1_sum, s_att, s_ad, *s_w2 = together(w1_sum, s_att, s_ad, *s_w2)
+
+    own_terms, sent_terms = zip(*[halves(item) for item in (grad_cn_kernel, grad_scale, grad_ad_kernel)])
+    gains = [grad_cn_gain, grad_ln1, grad_ln2]
+    flat, sent = [
+        jnp.concatenate([item.reshape(-1) for item in (*terms, *gains)])
+        for terms in (own_terms, sent_terms)
+    ]
+    flat, sent, w1_sum = together(flat, sent, w1_sum)
+    g_w1 = reduce_chips(w1_sum).astype(F32)
+    flat = flat + lax.ppermute(sent, "mb", SWAP)
+    if fast:
+        ghi_got = lax.ppermute(ghi_sent, "mb", SWAP)
+    flat = sum_everywhere(flat)
+    sizes = np.cumsum([0] + [item.size for item in (*own_terms, *gains)])
+    g_kernel, g_scale, g_taps, *gain_sums = [
+        flat[int(sizes[i]) : int(sizes[i + 1])].reshape(item.shape)
+        for i, item in enumerate((*own_terms, *gains))
+    ]
 
     def leave(values, kind):
         own, sent = halves(values)
@@ -1026,7 +1070,6 @@
 
     lo_stack = leave(lo_result.reshape(row_count, col_count, d_own), BF)
     if fast:
-        ghi_got = lax.ppermute(ghi_sent, "mb", SWAP)
         hi_stack, ghi_stack = [
             lax.dynamic_update_slice_in_dim(stack, got.astype(stack.dtype), 1 - mine, 0)
             for stack, got in ((hi_mine, hi_got), (ghi_mine, ghi_got))
@@ -1040,19 +1083,6 @@
     g_fc1, g_fc2 = settle(s_ff, (ff_shard, ff_shard))
     g_gate_w2, g_q, g_k, g_v, g_out = settle(s_att, (gh_shard, d_shard, d_shard, d_shard, d_shard))
     g_ad, g_gate_w1 = settle(s_ad, (d_shard, gh_shard))
-
-    own_terms, sent_terms = zip(*[halves(item) for item in (grad_cn_kernel, grad_scale, grad_ad_kernel)])
-    gains = [grad_cn_gain, grad_ln1, grad_ln2]
-    flat, sent = [
-        jnp.concatenate([item.reshape(-1) for item in (*terms, *gains)])
-        for terms in (own_terms, sent_terms)
-    ]
-    flat = sum_everywhere(flat + lax.ppermute(sent, "mb", SWAP))
-    sizes = np.cumsum([0] + [item.size for item in (*own_terms, *gains)])
-    g_kernel, g_scale, g_taps, *gain_sums = [
-        flat[int(sizes[i]) : int(sizes[i + 1])].reshape(item.shape)
-        for i, item in enumerate((*own_terms, *gains))
-    ]
 
     return (
         lo_stack,
@@ -1079,50 +1109,50 @@
 
 def solution(mesh):
     tiles, mps = mesh.shape["tile"], mesh.shape["mp"]
-    fine = Mesh(mesh.devices.reshape(tiles, 2, mps // 2), ("tile", "mb", "tp"))
+    fine = Mesh(mesh.devices.reshape(tiles // 2, 2, 2, mps // 2), (*TILE, "mb", "tp"))
     mp = ("mb", "tp")
     in_specs = (
-        P(None, "tile", None, mp),
-        P(None, "tile", mp, None),
+        P(None, TILE, None, mp),
+        P(None, TILE, mp, None),
         P(),
         P(None, mp),
         P(),
-        P("tile", mp),
-        P(mp, "tile"),
+        P(TILE, mp),
+        P(mp, TILE),
         P(mp),
-        P("tile", mp),
+        P(TILE, mp),
         P(None, mp),
-        P("tile", mp),
-        P(mp, "tile"),
+        P(TILE, mp),
+        P(mp, TILE),
         P(),
-        P(None, "tile", mp),
-        P(mp, "tile"),
+        P(None, TILE, mp),
+        P(mp, TILE),
         P(),
-        P("tile", mp),
-        P(mp, "tile"),
-        P(None, "tile", None, mp),
-        P(None, "tile", mp, None),
+        P(TILE, mp),
+        P(mp, TILE),
+        P(None, TILE, None, mp),
+        P(None, TILE, mp, None),
     )
     out_specs = (
-        P(None, "tile", None, mp),
-        P(None, "tile", mp, None),
-        P(None, "tile", None, mp),
-        P(None, "tile", mp, None),
+        P(None, TILE, None, mp),
+        P(None, TILE, mp, None),
+        P(None, TILE, None, mp),
+        P(None, TILE, mp, None),
         P(None, mp),
         P(),
-        P("tile", mp),
-        P(mp, "tile"),
+        P(TILE, mp),
+        P(mp, TILE),
         P(mp),
-        P("tile", mp),
+        P(TILE, mp),
         P(None, mp),
-        P("tile", mp),
-        P(mp, "tile"),
+        P(TILE, mp),
+        P(mp, TILE),
         P(),
-        P(None, "tile", mp),
-        P(mp, "tile"),
+        P(None, TILE, mp),
+        P(mp, TILE),
         P(),
-        P("tile", mp),
-        P(mp, "tile"),
+        P(TILE, mp),
+        P(mp, TILE),
     )
     return jax.shard_map(
         on_device, mesh=fine, in_specs=in_specs, out_specs=out_specs, check_vma=False

time: 1620 us -> 1550 us (0.957)
  waiting for transfers between devices: 360 us -> 223 us
  starting transfers between devices: 111 us -> 171 us
  local copies, waits for them, and re-layouts: 146 us -> 128 us
    ppermute x1, waiting for transfers between devices: 81.4 us -> 13.9 us  [on_device(): w1_got = lax.ppermute(w1_sent, 'mb', SWAP)]
    ppermute x15 -> x18, starting transfers between devices: 72.6 us -> 133 us  [the longest x4 66 us: sum_everywhere(): lax.ppermute(flat, TILE, [(i, i ^ bit) for i in range(devices)])]
    ppermute x5, waiting for transfers between devices: 144 us -> 88.2 us  [swap_micro(): return (own, lax.ppermute(sent, 'mb', SWAP))]
    all_gather x2, waiting for transfers between devices: 38 us -> 62.6 us  [gather_all(): full = lax.all_gather(shard, ALL, axis=0)]
    ppermute x15 -> x18, waiting for transfers between devices: 33.1 us -> 12.2 us  [the longest x4 10.9 us: sum_everywhere(): lax.ppermute(flat, TILE, [(i, i ^ bit) for i in range(devices)])]
    unnamed x282 -> x293, local copies, waits for them, and re-layouts: 51.5 us -> 47.7 us
  transfers between devices with their start and end apart: 44 -> 47, of which waited for: 18 -> 9; matrix products, arithmetic and copies ran while one was open for 44% -> 49% of each run, Pallas kernels for 20% -> 23%
where the time goes in v3:
time: 1550 us; the launch traced here: 1540 us
  matrix products  500 us (32%)
  Pallas kernels  359 us (23%)
  waiting for transfers between devices  223 us (14%)
  starting transfers between devices  171 us (11%)
  other arithmetic  143 us (9%)
  local copies, waits for them, and re-layouts  128 us (8%)
  between operations  16.6 us (1%)
    dot_general x22, matrix products, matmul(): return jnp.dot(left, right, preferred_element_type=F32)  195 us
    dot_general x22, matrix products, matmul_nt(): lax.dot_general(left, right, (((1,), (1,)), ((), ())), preferred_element_...  189 us
    pallas_call x2, Pallas kernels, conv_backward(): pl.pallas_call(back_kernel, out_shape=(jax.ShapeDtypeStruct((slots, *x.sh...  119 us
    dot_general x5, matrix products, matmul_tn(): lax.dot_general(left, right, (((0,), (0,)), ((), ())), preferred_element_...  117 us
    ppermute x5, waiting for transfers between devices, swap_micro(): return (own, lax.ppermute(sent, 'mb', SWAP))  88.2 us
    pallas_call x2, Pallas kernels, conv_forward(): pl.pallas_call(kernel, out_shape=jax.ShapeDtypeStruct((48 * 48, 2 * width...  72.7 us
    ppermute x4, starting transfers between devices, sum_everywhere(): lax.ppermute(flat, TILE, [(i, i ^ bit) for i in range(devices)])  66 us
    all_gather x2, waiting for transfers between devices, gather_all(): full = lax.all_gather(shard, ALL, axis=0)  62.6 us
  transfers between devices with their start and end apart: 47, of which 9 were waited for; matrix products, arithmetic and copies ran while one was open for 49% of the time, Pallas kernels for 23%

profile of v3, /device:TPU:0, one launch (start us, length us, event | category | flops | bytes accessed | tf_op | source)
XLA Modules:
  0.0 1540.0 jit_solution(917090349115232953)
XLA Ops:
  41.9 36.4 %shard_map.339.into_ref = bf16[2304,1536]{1,0:T(8,128)(2,1)} custom-call(s32[1]{0:T(128)} %bitcast.place_ref, bf16[48,36864]{1,0:T(8,128)(2,1)} %get-tuple-element.242.x_ref.own_ref, bf16[8,36864]{1,0:T(8,128)(2,1)} %get-tuple-element.274.top_ref, bf16[8,36864]{1,0:T(8,128)(2,1)} %get-tuple-element.273.bot_ref, f32[49,768]{1,0:T(8,128)} %convert_element_type.436.taps_ref, ...), custom_call_target="tpu_custom_call" | custom-call | flops 41472000000 | bytes 12000000 | tf_op jit(solution)/shard_map/pallas_call | solution.py:331
  78.3 88.2 %collective-permute-done.3 = bf16[2,8,36864]{2,1,0:T(8,128)(2,1)} collective-permute-done((bf16[2,8,36864]{2,1,0:T(8,128)(2,1)}, bf16[2,8,36864]{2,1,0:T(8,128)(2,1)}, u32[]{:S(2)}, u32[]{:S(2)}) %collective-permute-start.3) | collective-permute-done | bytes 1179680 | tf_op jit(solution)/shard_map/ppermute | solution.py:106
  168.9 36.3 %shard_map.340 = bf16[2304,1536]{1,0:T(8,128)(2,1)} custom-call(s32[1]{0:T(128)S(6)} %sub.31.place_ref, bf16[48,36864]{1,0:T(8,128)(2,1)} %collective-permute-done.x_ref.other_ref, bf16[8,36864]{1,0:T(8,128)(2,1)} %get-tuple-element.276.top_ref, bf16[8,36864]{1,0:T(8,128)(2,1)} %get-tuple-element.275.bot_ref, ...), custom_call_target="tpu_custom_call", output_to_operand_aliasing={{}: (6, {})} | custom-call | flops 41472000000 | bytes 12000000 | tf_op jit(solution)/shard_map/pallas_call | solution.py:331
  218.0 62.6 %all-gather.5.cloned.1.call-done = bf16[3072,7040]{1,0:T(8,128)(2,1)} async-done(((bf16[96,7040]{1,0:T(8,128)(2,1)}), bf16[3072,7040]{1,0:T(8,128)(2,1)}) %all-gather.5.cloned.1.call-update) | async-done | bytes 43253776 | tf_op jit(solution)/shard_map/all_gather | solution.py:201
  286.9 32.7 %multiply_convert_fusion.3 = (bf16[2304,3072]{1,0:T(8,128)(2,1)}, f32[2304,3072]{1,0:T(8,128)}) fusion(bf16[2304,1536]{1,0:T(8,128)(2,1)} %fusion.16, bf16[2,1536,7040]{2,1,0:T(8,128)(2,1)} %bitcast.374), kind=kOutput, calls=%fused_computation.16 | convolution fusion | flops 21778661376 | bytes 58982400 | tf_op jit(solution)/shard_map/dot_general | solution.py:47
  327.7 29.6 %fusion.33 = f32[2304,1536]{1,0:T(8,128)} fusion(bf16[2304,3072]{1,0:T(8,128)(2,1)} %get-tuple-element.78, bf16[2,1536,7040]{2,1,0:T(8,128)(2,1)} %bitcast.375), kind=kOutput, calls=%fused_computation.56 | convolution fusion | flops 21743271936 | bytes 37748736 | tf_op jit(solution)/shard_map/dot_general | solution.py:55
  357.3 31.4 %multiply_convert_fusion.2 = (bf16[2304,3072]{1,0:T(8,128)(2,1)}, f32[2304,3072]{1,0:T(8,128)}) fusion(bf16[2304,1536]{1,0:T(8,128)(2,1)S(1)} %bitcast.349, bf16[2,1536,7040]{2,1,0:T(8,128)(2,1)} %bitcast.376), kind=kOutput, calls=%fused_computation.14 | convolution fusion | flops 21778661376 | bytes 58982400 | tf_op jit(solution)/shard_map/dot_general | solution.py:47
  388.7 30.5 %convolution_add_fusion.1.branch_ref = f32[2304,1536]{1,0:T(8,128)} fusion(f32[2304,1536]{1,0:T(8,128)} %fusion.33, bf16[2304,3072]{1,0:T(8,128)(2,1)} %get-tuple-element.330, bf16[2,1536,7040]{2,1,0:T(8,128)(2,1)} %bitcast.377), kind=kOutput, calls=%fused_computation.30 | convolution fusion | flops 21746810880 | bytes 51904512 | tf_op jit(solution)/shard_map/dot_general | solution.py:55
  523.8 41.3 %shard_map.342 = (bf16[576,1024]{1,0:T(8,128)(2,1)}, f32[8,3,2,192]{3,2,1,0:T(2,128)}) custom-call(s32[3]{0:T(128)} %get-tuple-element.340.first_ref, s32[3]{0:T(128)} %get-tuple-element.339.last_ref, bf16[576,1024]{1,0:T(8,128)(2,1)} %pad_maximum_fusion.6.q_ref, bf16[576,1024]{1,0:T(8,128)(2,1)} %copy-done.114, bf16[576,1024]{1,0:T(8,128)(2,1)} %copy-done.52, ...), custom_call_target="tpu_custom_call" | custom-call | flops 40960000000 | bytes 20000000 | tf_op jit(solution)/shard_map/pallas_call | solution.py:654
  606.5 22.4 %shard_map.343 = bf16[1024,8192]{1,0:T(8,128)(2,1)} custom-call(bf16[1024,576]{1,0:T(8,128)(2,1)} %get-tuple-element.260.refs_0_, bf16[1024,576]{1,0:T(8,128)(2,1)} %fusion.209.refs_1_, bf16[576,4096]{1,0:T(8,128)(2,1)} %copy-done.30, bf16[576,4096]{1,0:T(8,128)(2,1)} %get-tuple-element.237.refs_3_), custom_call_target="tpu_custom_call" | custom-call | flops 24159191040 | bytes 16777216 | tf_op jit(solution)/shard_map/pallas_call | solution.py:189
  635.2 53.6 %shard_map.344 = (bf16[576,1024]{1,0:T(8,128)(2,1)}, f32[576,1024]{1,0:T(8,128)}, f32[576,1024]{1,0:T(8,128)}, bf16[2,576,1024]{2,1,0:T(8,128)(2,1)}, bf16[2,576,1024]{2,1,0:T(8,128)(2,1)}) custom-call(s32[3]{0:T(128)} %get-tuple-element.340.first_ref, s32[3]{0:T(128)} %get-tuple-element.339.last_ref, bf16[576,1024]{1,0:T(8,128)(2,1)} %pad_maximum_fusion.6.q_ref, ...), custom_call_target="tpu_custom_call" | custom-call | flops 56320000000 | bytes 20000000 | tf_op jit(solution)/shard_map/pallas_call | solution.py:742
  747.2 38.6 %collective-permute-start.21 = (bf16[1,24,1024]{1,2,0:T(8,128)(2,1)}, bf16[1,24,1024]{1,2,0:T(8,128)(2,1)}, u32[]{:S(2)}, u32[]{:S(2)}) collective-permute-start(bf16[1,24,1024]{1,2,0:T(8,128)(2,1)} %get-tuple-element.261), channel_id=1, source_target_pairs={{0,2},{2,4},{4,6},{6,8},{8,10},{10,12},{12,14},{14,16},{16,18},{18... | collective-permute-start | bytes 147464 | tf_op jit(solution)/shard_map/ppermute | solution.py:41
  890.3 29.4 %convolution_convert_fusion.2 = bf16[1536,3072]{1,0:T(8,128)(2,1)} fusion(bf16[2304,1536]{1,0:T(8,128)(2,1)} %get-tuple-element.103, bf16[2304,3072]{1,0:T(8,128)(2,1)} %get-tuple-element.330), kind=kOutput, calls=%fused_computation.40 | convolution fusion | flops 21747990528 | bytes 30670848 | tf_op jit(solution)/shard_map/dot_general | solution.py:51
  919.7 28.9 %convolution_convert_fusion.3 = bf16[1536,3072]{1,0:T(8,128)(2,1)} fusion(bf16[2304,1536]{1,0:T(8,128)(2,1)} %get-tuple-element.103, bf16[2304,3072]{1,0:T(8,128)(2,1)} %get-tuple-element.78), kind=kOutput, calls=%fused_computation.41 | convolution fusion | flops 21747990528 | bytes 30670848 | tf_op jit(solution)/shard_map/dot_general | solution.py:51
  956.2 37.2 %multiply_convert_fusion.1 = bf16[2304,3072]{1,0:T(8,128)(2,1)S(1)} fusion(bf16[2304,1536]{1,0:T(8,128)(2,1)} %get-tuple-element.103, f32[2304,3072]{1,0:T(8,128)} %get-tuple-element.329, bf16[2,1536,7040]{2,1,0:T(8,128)(2,1)} %bitcast.386), kind=kOutput, calls=%fused_computation.13 | convolution fusion | flops 21828206592 | bytes 58982400 | tf_op jit(solution)/shard_map/dot_general | solution.py:47
  993.5 26.0 %convolution_convert_fusion.1 = bf16[1536,3072]{1,0:T(8,128)(2,1)} fusion(bf16[2304,1536]{1,0:T(8,128)(2,1)S(1)} %bitcast.351, bf16[2304,3072]{1,0:T(8,128)(2,1)S(1)} %multiply_convert_fusion.1), kind=kOutput, calls=%fused_computation.39 | convolution fusion | flops 21747990528 | bytes 30670848 | tf_op jit(solution)/shard_map/dot_general | solution.py:51
  1019.5 36.8 %multiply_convert_fusion = bf16[2304,3072]{1,0:T(8,128)(2,1)S(1)} fusion(bf16[2304,1536]{1,0:T(8,128)(2,1)} %get-tuple-element.103, f32[2304,3072]{1,0:T(8,128)} %get-tuple-element.331, bf16[2,1536,7040]{2,1,0:T(8,128)(2,1)} %bitcast.387), kind=kOutput, calls=%fused_computation.12 | convolution fusion | flops 21828206592 | bytes 58982400 | tf_op jit(solution)/shard_map/dot_general | solution.py:47
  1061.4 25.9 %convolution_convert_fusion = bf16[1536,3072]{1,0:T(8,128)(2,1)} fusion(bf16[2304,1536]{1,0:T(8,128)(2,1)S(1)} %bitcast.351, bf16[2304,3072]{1,0:T(8,128)(2,1)S(1)} %multiply_convert_fusion), kind=kOutput, calls=%fused_computation.38 | convolution fusion | flops 21747990528 | bytes 30670848 | tf_op jit(solution)/shard_map/dot_general | solution.py:51
  1099.4 29.6 %fusion.35 = f32[2304,1536]{1,0:T(8,128)} fusion(bf16[2304,3072]{1,0:T(8,128)(2,1)} %copy-done.121, bf16[2,1536,7040]{2,1,0:T(8,128)(2,1)} %bitcast.388), kind=kOutput, calls=%fused_computation.58 | convolution fusion | flops 21743271936 | bytes 37748736 | tf_op jit(solution)/shard_map/dot_general | solution.py:55
  1129.0 34.9 %fusion.18 = (f32[2304]{0:T(1024)S(1)}, bf16[2304,1536]{1,0:T(8,128)(2,1)}) fusion(bf16[2304,1536]{1,0:T(8,128)(2,1)} %shard_map.340, f32[1536]{0:T(1024)S(1)} %copy-done.71, f32[2304]{0:T(1024)S(1)} %copy-done.62, f32[2304,1536]{1,0:T(8,128)} %fusion.35, bf16[2304,3072]{1,0:T(8,128)(2,1)} %copy-done.120, bf16[2,1536,7040]{2,1,0:T(8,128)(2,1)} %bitcast.389), kind=kOutput, calls=%fused_computation.33 | convolution fusion | flops 21771581440 | bytes 51929088 | tf_op jit(solution)/shard_map/dot_general | solution.py:55
  1212.2 59.1 %shard_map.347 = (bf16[1,48,36864]{2,1,0:T(8,128)(2,1)}, f32[56,768]{1,0:T(8,128)}) custom-call(s32[1]{0:T(128)S(6)} %sub.31.place_ref, bf16[2304,1536]{1,0:T(8,128)(2,1)} %add_convert_fusion.g_ref, bf16[48,8,1536]{2,1,0:T(8,128)(2,1)} %copy-done.118, bf16[48,8,1536]{2,1,0:T(8,128)(2,1)} %copy-done.117, ...), custom_call_target="tpu_custom_call" | custom-call | flops 69120000000 | bytes 25000000 | tf_op jit(solution)/shard_map/pallas_call | solution.py:437
  1287.3 59.9 %shard_map.348 = (f32[2,48,36864]{2,1,0:T(8,128)}, f32[56,768]{1,0:T(8,128)}) custom-call(s32[1]{0:T(128)} %bitcast.place_ref, bf16[2304,1536]{1,0:T(8,128)(2,1)} %add_convert_fusion.g_ref, bf16[48,8,1536]{2,1,0:T(8,128)(2,1)} %copy-done.118, bf16[48,8,1536]{2,1,0:T(8,128)(2,1)} %copy-done.117, bf16[48,36864]{1,0:T(8,128)(2,1)} %get-tuple-element.242.x_ref.own_ref, ...), custom_call_target="tpu_custom_call" | custom-call | flops 69120000000 | bytes 25000000 | tf_op jit(solution)/shard_map/pallas_call | solution.py:437
  1400.1 50.7 %collective-permute-start.30 = (f32[46592]{0:T(1024)S(1)}, f32[46592]{0:T(1024)S(1)}, u32[]{:S(2)}, u32[]{:S(2)}) collective-permute-start(f32[46592]{0:T(1024)S(1)} %add.426), channel_id=1, source_target_pairs={{0,2},{2,0},{4,6},{6,4},{8,10},{10,8},{12,14},{14,12},{16,18},{18,... | collective-permute-start | bytes 559112 | tf_op jit(solution)/shard_map/ppermute | solution.py:249
  1479.9 44.5 %reduce-scatter.17.cloned.1.call-done = bf16[192,1536]{1,0:T(8,128)(2,1)} async-done(((bf16[1536,1536]{1,0:T(8,128)(2,1)}), bf16[192,1536]{1,0:T(8,128)(2,1)}) %reduce-scatter.17.cloned.1.call-update) | async-done | bytes 589840 | tf_op jit(solution)/shard_map/reduce_scatter | solution.py:219
  (604 shorter events, 556.6 us)
Async XLA Ops:
  7.2 273.4 %all-gather.5.cloned.1.call-start = ((), (), s32[]{:S(2)}) async-start(), calls=%async_computation.12 | async-start | bytes 44605440 | tf_op jit(solution)/shard_map/all_gather | solution.py:201
  9.8 462.0 %all-gather.7.cloned.1.call-start = ((), (), s32[]{:S(2)}) async-start(), calls=%async_computation.13 | async-start | bytes 27574272 | tf_op jit(solution)/shard_map/all_gather | solution.py:201
  27.5 141.4 %collective-permute-start = (bf16[48,36864]{1,0:T(8,128)(2,1)S(1)}, bf16[48,36864]{1,0:T(8,128)(2,1)}, u32[]{:S(2)}, u32[]{:S(2)}) collective-permute-start(bf16[48,36864]{1,0:T(8,128)(2,1)S(1)} %get-tuple-element.243), channel_id=1, source_target_pairs={{0,1},{1,0},{2,3},{3,2},{4,5},{5,4},{6,7},{7,6},{8,9},{9,8},{10,11... | collective-permute-start | bytes 10616840 | tf_op jit(solution)/shard_map/ppermute | solution.py:106
  38.1 128.5 %collective-permute-start.3 = (bf16[2,8,36864]{2,1,0:T(8,128)(2,1)}, bf16[2,8,36864]{2,1,0:T(8,128)(2,1)}, u32[]{:S(2)}, u32[]{:S(2)}) collective-permute-start(bf16[2,8,36864]{2,1,0:T(8,128)(2,1)} %get-tuple-element.252), channel_id=1, source_target_pairs={{0,1},{1,0},{2,3},{3,2},{4,5},{5,4},{6,7},{7,6},{8,9},{9,8},{10,11... | collective-permute-start | bytes 3538952 | tf_op jit(solution)/shard_map/ppermute | solution.py:106
  281.7 670.6 %reduce-scatter.7.cloned.1.call-start = ((), (), s32[]{:S(2)}) async-start(), calls=%async_computation.6 | async-start | bytes 17825792 | tf_op jit(solution)/shard_map/reduce_scatter | solution.py:206
  319.6 99.6 %collective-permute-start.6 = (bf16[768]{0:T(1024)(128)(2,1)}, bf16[768]{0:T(1024)(128)(2,1)}, u32[]{:S(2)}, u32[]{:S(2)}) collective-permute-start(bf16[768]{0:T(1024)(128)(2,1)} %param.27), channel_id=1, source_target_pairs={{0,1},{1,0},{2,3},{3,2},{4,5},{5,4},{6,7},{7,6},{8,9},{9,8},{10,11... | collective-permute-start | bytes 4616 | tf_op jit(solution)/shard_map/ppermute | solution.py:830
  319.9 137.0 %collective-permute-start.7 = (bf16[9,512]{1,0:T(8,128)(2,1)}, bf16[9,512]{1,0:T(8,128)(2,1)}, u32[]{:S(2)}, u32[]{:S(2)}) collective-permute-start(bf16[9,512]{1,0:T(8,128)(2,1)} %param.29), channel_id=1, source_target_pairs={{0,1},{1,0},{2,3},{3,2},{4,5},{5,4},{6,7},{7,6},{8,9},{9,8},{10,11... | collective-permute-start | bytes 27656 | tf_op jit(solution)/shard_map/ppermute | solution.py:830
  323.7 142.2 %collective-permute-start.16 = (bf16[576,512]{1,0:T(8,128)(2,1)}, bf16[576,512]{1,0:T(8,128)(2,1)}, u32[]{:S(2)}, u32[]{:S(2)}) collective-permute-start(bf16[576,512]{1,0:T(8,128)(2,1)} %get-tuple-element.268), channel_id=1, source_target_pairs={{0,1},{1,0},{2,3},{3,2},{4,5},{5,4},{6,7},{7,6},{8,9},{9,8},{10,11... | collective-permute-start | bytes 1769480 | tf_op jit(solution)/shard_map/ppermute | solution.py:106
  325.9 141.3 %collective-permute-start.5 = (bf16[576,512]{1,0:T(8,128)(2,1)}, bf16[576,512]{1,0:T(8,128)(2,1)}, u32[]{:S(2)}, u32[]{:S(2)}) collective-permute-start(bf16[576,512]{1,0:T(8,128)(2,1)} %get-tuple-element.270), channel_id=1, source_target_pairs={{0,1},{1,0},{2,3},{3,2},{4,5},{5,4},{6,7},{7,6},{8,9},{9,8},{10,11... | collective-permute-start | bytes 1769480 | tf_op jit(solution)/shard_map/ppermute | solution.py:106
  456.9 113.5 %collective-permute-start.14 = (bf16[1,48,36864]{2,1,0:T(8,128)(2,1)}, bf16[1,48,36864]{2,1,0:T(8,128)(2,1)}, u32[]{:S(2)}, u32[]{:S(2)}) collective-permute-start(bf16[1,48,36864]{2,1,0:T(8,128)(2,1)} %get-tuple-element.85), channel_id=1, source_target_pairs={{0,1},{1,0},{2,3},{3,2},{4,5},{5,4},{6,7},{7,6},{8,9},{9,8},{10,11... | collective-permute-start | bytes 10616840 | tf_op jit(solution)/shard_map/ppermute | solution.py:938
  519.0 109.9 %collective-permute-start.17 = (bf16[48,36864]{1,0:T(8,128)(2,1)}, bf16[48,36864]{1,0:T(8,128)(2,1)}, u32[]{:S(2)}, u32[]{:S(2)}) collective-permute-start(bf16[48,36864]{1,0:T(8,128)(2,1)} %get-tuple-element.241), channel_id=1, source_target_pairs={{0,1},{1,0},{2,3},{3,2},{4,5},{5,4},{6,7},{7,6},{8,9},{9,8},{10,11... | collective-permute-start | bytes 10616840 | tf_op jit(solution)/shard_map/ppermute | solution.py:106
  629.0 742.6 %reduce-scatter.11.cloned.1.call-start = ((), (), s32[]{:S(2)}) async-start(), calls=%async_computation.8 | async-start | bytes 5849088 | tf_op jit(solution)/shard_map/reduce_scatter | solution.py:206
  718.6 131.3 %collective-permute-start.15 = (bf16[24,24,512]{2,1,0:T(8,128)(2,1)}, bf16[24,24,512]{2,1,0:T(8,128)(2,1)}, u32[]{:S(2)}, u32[]{:S(2)}) collective-permute-start(bf16[24,24,512]{2,1,0:T(8,128)(2,1)} %constant_dynamic-slice_fusion.11), channel_id=1, source_target_pairs={{0,1},{1,0},{2,3},{3,2},{4,5},{5,4},{6,7},{7,6},{8,9},{9,8},{10,11... | collective-permute-start | bytes 1769480 | tf_op jit(solution)/shard_map/ppermute | solution.py:1068
  845.8 525.8 %reduce-scatter.9.cloned.1.call-start = ((), (), s32[]{:S(2)}) async-start(), calls=%async_computation.7 | async-start | bytes 10584064 | tf_op jit(solution)/shard_map/reduce_scatter | solution.py:206
  867.4 82.8 %collective-permute-start.20 = (bf16[24,24,512]{2,1,0:T(8,128)(2,1)S(1)}, bf16[24,24,512]{2,1,0:T(8,128)(2,1)S(1)}, u32[]{:S(2)}, u32[]{:S(2)}) collective-permute-start(bf16[24,24,512]{2,1,0:T(8,128)(2,1)S(1)} %dynamic-slice_convert_fusion), channel_id=1, source_target_pairs={{0,1},{1,0},{2,3},{3,2},{4,5},{5,4},{6,7},{7,6},{8,9},{9,8},{10,11... | collective-permute-start | bytes 1769480 | tf_op jit(solution)/shard_map/ppermute | solution.py:1068
  948.6 422.9 %reduce-scatter.13.cloned.1.call-start = ((), (), s32[]{:S(2)}) async-start(), calls=%async_computation.9 | async-start | bytes 10027008 | tf_op jit(solution)/shard_map/reduce_scatter | solution.py:206
  955.5 227.0 %collective-permute-start.38 = (bf16[64,4096]{1,0:T(8,128)(2,1)}, bf16[64,4096]{1,0:T(8,128)(2,1)}, u32[]{:S(2)}, u32[]{:S(2)}) collective-permute-start(bf16[64,4096]{1,0:T(8,128)(2,1)} %pad_maximum_fusion.11), channel_id=1, source_target_pairs={{0,1},{1,0},{2,3},{3,2},{4,5},{5,4},{6,7},{7,6},{8,9},{9,8},{10,11... | collective-permute-start | bytes 1572872 | tf_op jit(solution)/shard_map/ppermute | solution.py:236
  1087.3 284.2 %reduce-scatter.15.cloned.1.call-start = ((), (), s32[]{:S(2)}) async-start(), calls=%async_computation.10 | async-start | bytes 10027008 | tf_op jit(solution)/shard_map/reduce_scatter | solution.py:206
  1092.6 93.1 %collective-permute-start.23 = (bf16[1536,1536]{1,0:T(8,128)(2,1)}, bf16[1536,1536]{1,0:T(8,128)(2,1)}, u32[]{:S(2)}, u32[]{:S(2)}) collective-permute-start(bf16[1536,1536]{1,0:T(8,128)(2,1)} %constant_dynamic-slice_fusion.9), channel_id=1, source_target_pairs={{0,2},{2,0},{1,3},{3,1},{4,6},{6,4},{5,7},{7,5},{8,10},{10,8},{9,1... | collective-permute-start | bytes 14155784 | tf_op jit(solution)/shard_map/ppermute | solution.py:214
  1097.8 93.1 %collective-permute-start.24 = (bf16[1536,1536]{1,0:T(8,128)(2,1)}, bf16[1536,1536]{1,0:T(8,128)(2,1)}, u32[]{:S(2)}, u32[]{:S(2)}) collective-permute-start(bf16[1536,1536]{1,0:T(8,128)(2,1)} %constant_dynamic-slice_fusion.8), channel_id=1, source_target_pairs={{0,2},{2,0},{1,3},{3,1},{4,6},{6,4},{5,7},{7,5},{8,10},{10,8},{9,1... | collective-permute-start | bytes 14155784 | tf_op jit(solution)/shard_map/ppermute | solution.py:214
  1182.4 342.0 %reduce-scatter.17.cloned.1.call-start = ((), (), s32[]{:S(2)}) async-start(), calls=%async_computation.11 | async-start | bytes 5308416 | tf_op jit(solution)/shard_map/reduce_scatter | solution.py:219
  1208.5 76.7 %collective-permute-start.27 = (bf16[1536,1536]{1,0:T(8,128)(2,1)}, bf16[1536,1536]{1,0:T(8,128)(2,1)}, u32[]{:S(2)}, u32[]{:S(2)}) collective-permute-start(bf16[1536,1536]{1,0:T(8,128)(2,1)} %broadcast_select_fusion), channel_id=1, source_target_pairs={{0,1},{1,0},{2,3},{3,2},{4,5},{5,4},{6,7},{7,6},{8,9},{9,8},{10,11... | collective-permute-start | bytes 14155784 | tf_op jit(solution)/shard_map/ppermute | solution.py:1025
  1285.1 86.5 %collective-permute-start.28 = (bf16[1,48,36864]{2,1,0:T(8,128)(2,1)}, bf16[1,48,36864]{2,1,0:T(8,128)(2,1)S(1)}, u32[]{:S(2)}, u32[]{:S(2)}) collective-permute-start(bf16[1,48,36864]{2,1,0:T(8,128)(2,1)} %get-tuple-element.113), channel_id=1, source_target_pairs={{0,1},{1,0},{2,3},{3,2},{4,5},{5,4},{6,7},{7,6},{8,9},{9,8},{10,11... | collective-permute-start | bytes 10616840 | tf_op jit(solution)/shard_map/ppermute | solution.py:1058
  1395.2 130.3 %collective-permute-start.35 = (bf16[96,3072]{1,0:T(8,128)(2,1)S(1)}, bf16[96,3072]{1,0:T(8,128)(2,1)S(1)}, u32[]{:S(2)}, u32[]{:S(2)}) collective-permute-start(bf16[96,3072]{1,0:T(8,128)(2,1)S(1)} %constant_dynamic-slice_fusion.4), channel_id=1, source_target_pairs={{0,1},{1,0},{2,3},{3,2},{4,5},{5,4},{6,7},{7,6},{8,9},{9,8},{10,11... | collective-permute-start | bytes 1769480 | tf_op jit(solution)/shard_map/ppermute | solution.py:236
  (159 other events, 2319.0 us)
Sparse Core Ops, SparseCore 0:
  11.5 269.0 all-gather.4
  284.1 160.3 all-gather.6
  629.1 233.3 reduce-scatter.6
  866.3 89.2 reduce-scatter.10
  960.1 132.9 reduce-scatter.8
  1097.6 144.2 reduce-scatter.12
  1246.0 111.2 reduce-scatter.14
  1371.7 152.6 reduce-scatter.16

commit v4 on v3

--- a/solution.py
+++ b/solution.py
@@ -215,8 +215,21 @@
     return (own.astype(F32) + got.astype(F32)).astype(BF)
 
 
+def pass_half(first, second):
+    mine = lax.axis_index("mb") == 0
+    own = jnp.where(mine, first, second)
+    return own, lax.ppermute(jnp.where(mine, second, first), "mb", SWAP)
+
+
+def add_low(own, got):
+    return (own.astype(F32) + got.astype(F32)).astype(BF)
+
+
 def reduce_chips(terms):
-    both = lax.psum_scatter(terms, "chip", scatter_dimension=0, tiled=True)
+    return lax.psum_scatter(terms, "chip", scatter_dimension=0, tiled=True)
+
+
+def all_columns(both):
     rows = both.shape[0] // 2
     core = lax.axis_index("core")
     own = lax.dynamic_slice_in_dim(both, core * rows, rows, 0)
@@ -1002,17 +1015,18 @@
         grad_scale = jnp.sum(grad_cols * branch, axis=0)
         scaled_grad = (grad_cols * hi_scale).astype(BF)
     branch_full = lax.optimization_barrier(features(scaled_grad))
-    first = mine == 0
     p_w2 = [matmul_tn(branch_full, act).astype(BF) for act in inner_act]
     branch_full, *p_w2, s_ff = together(branch_full, *p_w2, s_ff)
-    s_w2 = [reduce_tiles(item) for item in p_w2]
+    core_w2 = [core_sum(item) for item in p_w2]
     grad_first = (matmul(branch_full, mlp_out[0]) * inner_slope[0].astype(F32)).astype(BF)
     w1_first = matmul_tn(normed_low, grad_first).astype(BF)
-    branch_full, w1_first = together(branch_full, w1_first)
+    branch_full, w1_first, *core_w2 = together(branch_full, w1_first, *core_w2)
+    w2_own, w2_got = pass_half(*core_w2)
     core_first = core_sum(w1_first)
     grad_second = (matmul(branch_full, mlp_out[1]) * inner_slope[1].astype(F32)).astype(BF)
     w1_second = matmul_tn(normed_low, grad_second).astype(BF)
-    grad_second, w1_second = together(grad_second, w1_second)
+    grad_second, w1_second, w2_got = together(grad_second, w1_second, w2_got)
+    s_w2 = reduce_chips(add_low(w2_own, w2_got))
     core_second = core_sum(w1_second)
     normed_grad = partial_sums(
         matmul_nt(grad_first, mlp_in[0]) + matmul_nt(grad_second, mlp_in[1])
@@ -1021,20 +1035,20 @@
     conv_grad, core_first, core_second = together(
         own_slice(back_conv).astype(BF), core_first, core_second
     )
-    w1_sent, w1_own = jnp.where(first, core_second, core_first), jnp.where(first, core_first, core_second)
-    w1_got = lax.ppermute(w1_sent, "mb", SWAP)
+    w1_own, w1_got = pass_half(core_first, core_second)
     conv_cols = conv_grad.reshape(hi_cols, hi_rows, c_own)
     grad_up, grad_down = rim_pair(conv_cols, RIM, 1)
     if fast:
         ghi_sent, taps_other = conv_backward(
             conv_grad, grad_up, grad_down, hi_other, cot_other, pool_cols, other_taps, mask, other_place, 1, BF
         )
-        conv_grad, ghi_sent, w1_got = together(conv_grad, ghi_sent, w1_got)
+        w1_got, s_att, s_ad, s_w2 = together(w1_got, s_att, s_ad, s_w2)
+        w1_sum = add_low(w1_own, w1_got)
+        conv_grad, ghi_sent, w1_sum = together(conv_grad, ghi_sent, w1_sum)
         ghi_mine, taps_own = conv_backward(
             conv_grad, grad_up, grad_down, hi_own, cot_own, pool_cols, own_taps, mask, own_place, 2, F32
         )
-        w1_sum = (w1_own.astype(F32) + w1_got.astype(F32)).astype(BF)
-        grad_cn_kernel = in_order(taps_own[:49], taps_other[:49], 1)
+        tap_sums = jnp.concatenate([taps_own, taps_other])
     else:
         conv_grad = conv_cols.transpose(1, 0, 2)
         conv_pad = jnp.concatenate(
@@ -1042,26 +1056,28 @@
         )
         hi_back = hi_grad + depthwise(conv_pad, conv_taps, hi_ids, hi_mid, 7, True)
         grad_cn_kernel = tap_grads(hi_pad, conv_grad, hi_ids, hi_mid, 7)
-        w1_sum = (w1_own.astype(F32) + w1_got.astype(F32)).astype(BF)
-    w1_sum, s_att, s_ad, *s_w2 = together(w1_sum, s_att, s_ad, *s_w2)
-
-    own_terms, sent_terms = zip(*[halves(item) for item in (grad_cn_kernel, grad_scale, grad_ad_kernel)])
+        tap_sums = jnp.concatenate(halves(grad_cn_kernel))
+        w1_sum = add_low(w1_own, w1_got)
+
+    g_w1 = reduce_chips(w1_sum)
+    own_terms, sent_terms = zip(*[halves(item) for item in (grad_scale, grad_ad_kernel)])
     gains = [grad_cn_gain, grad_ln1, grad_ln2]
     flat, sent = [
         jnp.concatenate([item.reshape(-1) for item in (*terms, *gains)])
         for terms in (own_terms, sent_terms)
     ]
-    flat, sent, w1_sum = together(flat, sent, w1_sum)
-    g_w1 = reduce_chips(w1_sum).astype(F32)
-    flat = flat + lax.ppermute(sent, "mb", SWAP)
-    if fast:
-        ghi_got = lax.ppermute(ghi_sent, "mb", SWAP)
-    flat = sum_everywhere(flat)
+    flat = sum_everywhere(flat + lax.ppermute(sent, "mb", SWAP))
     sizes = np.cumsum([0] + [item.size for item in (*own_terms, *gains)])
-    g_kernel, g_scale, g_taps, *gain_sums = [
+    g_scale, g_taps, *gain_sums = [
         flat[int(sizes[i]) : int(sizes[i + 1])].reshape(item.shape)
         for i, item in enumerate((*own_terms, *gains))
     ]
+    if fast:
+        ghi_got = lax.ppermute(ghi_sent, "mb", SWAP)
+        tap_sums, ghi_got = together(tap_sums, ghi_got)
+    tap_sums = sum_everywhere(tap_sums)
+    tap_rows = tap_sums.shape[0] // 2
+    g_kernel = (tap_sums[:tap_rows] + lax.ppermute(tap_sums[tap_rows:], "mb", SWAP))[: cn_kernel.shape[0]]
 
     def leave(values, kind):
         own, sent = halves(values)
@@ -1079,16 +1095,19 @@
         ghi_stack = leave(hi_back, F32)
     glo_stack = leave(grad_one.reshape(row_count, col_count, d_own), F32)
 
-    (g_w2,) = settle(jnp.concatenate(s_w2, axis=1), (hid_shard,))
+    hi_stack = hi_stack.reshape(2, hi_rows, 1, hi_cols * c_shard)
+    ghi_stack, g_w1 = together(ghi_stack.reshape(2, hi_rows, -1, 128), g_w1)
+    ghi_stack = ghi_stack.reshape(2, hi_rows, 1, hi_cols * c_shard)
+    g_w1, g_w2 = all_columns(g_w1).astype(F32), all_columns(s_w2).astype(F32)
     g_fc1, g_fc2 = settle(s_ff, (ff_shard, ff_shard))
     g_gate_w2, g_q, g_k, g_v, g_out = settle(s_att, (gh_shard, d_shard, d_shard, d_shard, d_shard))
     g_ad, g_gate_w1 = settle(s_ad, (d_shard, gh_shard))
 
     return (
         lo_stack,
-        hi_stack.reshape(2, hi_rows, 1, hi_cols * c_shard),
+        hi_stack,
         glo_stack,
-        ghi_stack.reshape(2, hi_rows, 1, hi_cols * c_shard),
+        ghi_stack,
         g_kernel,
         gain_sums[0],
         g_w1,

time: 1550 us -> 1580 us (1.019)
  waiting for transfers between devices: 223 us -> 267 us
  other arithmetic: 143 us -> 167 us
  Pallas kernels: 359 us -> 339 us
    ppermute x3 -> x6, waiting for transfers between devices: 15.2 us -> 81.9 us  [the longest x2 79 us: pass_half(): return (own, lax.ppermute(jnp.where(mine, second, first), 'mb', SWAP))]
    reduce_scatter x1 -> x2, waiting for transfers between devices: 44.5 us -> 0.01 us  [reduce_chips(): return lax.psum_scatter(terms, 'chip', scatter_dimension=0, tiled=True)]
    ppermute x2, starting transfers between devices: 2.85 us -> 40.6 us  [leave(): other = lax.ppermute(sent.astype(BF), 'mb', SWAP)]
    ppermute x2, starting transfers between devices: 40.7 us -> 9.32 us  [rim_rows(): before = lax.ppermute(value[length - width:], TILE, up)]
    ppermute x4 -> x8, starting transfers between devices: 66 us -> 35 us  [sum_everywhere(): lax.ppermute(flat, TILE, [(i, i ^ bit) for i in range(devices)])]
    ppermute x1, starting transfers between devices: 10.2 us -> 30.4 us  [on_device(): from_before = lax.ppermute(to_after, TILE, steps)]
    ppermute x1, waiting for transfers between devices: 0.01 us -> 19.7 us  [on_device(): ghi_got = lax.ppermute(ghi_sent, 'mb', SWAP)]
    unnamed x293 -> x322, local copies, waits for them, and re-layouts: 47.7 us -> 33.5 us
  transfers between devices with their start and end apart: 47 -> 54, of which waited for: 9 -> 10; matrix products, arithmetic and copies ran while one was open for 49% -> 48% of each run, Pallas kernels for 23% -> 22%
where the time goes in v4:
time: 1580 us; the launch traced here: 1570 us
  matrix products  499 us (32%)
  Pallas kernels  339 us (21%)
  waiting for transfers between devices  267 us (17%)
  other arithmetic  167 us (11%)
  starting transfers between devices  165 us (10%)
  local copies, waits for them, and re-layouts  121 us (8%)
  between operations  16.8 us (1%)
    dot_general x22, matrix products, matmul(): return jnp.dot(left, right, preferred_element_type=F32)  196 us
    dot_general x22, matrix products, matmul_nt(): lax.dot_general(left, right, (((1,), (1,)), ((), ())), preferred_element_...  187 us
    pallas_call x2, Pallas kernels, conv_backward(): pl.pallas_call(back_kernel, out_shape=(jax.ShapeDtypeStruct((slots, *x.sh...  119 us
    dot_general x5, matrix products, matmul_tn(): lax.dot_general(left, right, (((0,), (0,)), ((), ())), preferred_element_...  116 us
    ppermute x5, waiting for transfers between devices, swap_micro(): return (own, lax.ppermute(sent, 'mb', SWAP))  88.3 us
    ppermute x2, waiting for transfers between devices, pass_half(): return (own, lax.ppermute(jnp.where(mine, second, first), 'mb', SWAP))  79 us
    pallas_call x2, Pallas kernels, conv_forward(): pl.pallas_call(kernel, out_shape=jax.ShapeDtypeStruct((48 * 48, 2 * width...  72.7 us
    all_gather x2, waiting for transfers between devices, gather_all(): full = lax.all_gather(shard, ALL, axis=0)  62.6 us
  transfers between devices with their start and end apart: 54, of which 10 were waited for; matrix products, arithmetic and copies ran while one was open for 48% of the time, Pallas kernels for 22%

profile of v4, /device:TPU:0, one launch (start us, length us, event | category | flops | bytes accessed | tf_op | source)
XLA Modules:
  0.0 1574.3 jit_solution(4966379228010851790)
XLA Ops:
  41.9 36.4 %shard_map.339.into_ref = bf16[2304,1536]{1,0:T(8,128)(2,1)} custom-call(s32[1]{0:T(128)} %bitcast.place_ref, bf16[48,36864]{1,0:T(8,128)(2,1)} %get-tuple-element.248.x_ref.own_ref, bf16[8,36864]{1,0:T(8,128)(2,1)} %get-tuple-element.280.top_ref, bf16[8,36864]{1,0:T(8,128)(2,1)} %get-tuple-element.279.bot_ref, f32[49,768]{1,0:T(8,128)} %convert_element_type.460.taps_ref, ...), custom_call_target="tpu_custom_call" | custom-call | flops 41472000000 | bytes 12000000 | tf_op jit(solution)/shard_map/pallas_call | solution.py:344
  78.3 88.3 %collective-permute-done.3 = bf16[2,8,36864]{2,1,0:T(8,128)(2,1)} collective-permute-done((bf16[2,8,36864]{2,1,0:T(8,128)(2,1)}, bf16[2,8,36864]{2,1,0:T(8,128)(2,1)}, u32[]{:S(2)}, u32[]{:S(2)}) %collective-permute-start.3) | collective-permute-done | bytes 1179680 | tf_op jit(solution)/shard_map/ppermute | solution.py:106
  168.9 36.4 %shard_map.340 = bf16[2304,1536]{1,0:T(8,128)(2,1)} custom-call(s32[1]{0:T(128)S(6)} %sub.31.place_ref, bf16[48,36864]{1,0:T(8,128)(2,1)} %collective-permute-done.x_ref.other_ref, bf16[8,36864]{1,0:T(8,128)(2,1)} %get-tuple-element.282.top_ref, bf16[8,36864]{1,0:T(8,128)(2,1)} %get-tuple-element.281.bot_ref, ...), custom_call_target="tpu_custom_call", output_to_operand_aliasing={{}: (6, {})} | custom-call | flops 41472000000 | bytes 12000000 | tf_op jit(solution)/shard_map/pallas_call | solution.py:344
  218.1 62.6 %all-gather.5.cloned.1.call-done = bf16[3072,7040]{1,0:T(8,128)(2,1)} async-done(((bf16[96,7040]{1,0:T(8,128)(2,1)}), bf16[3072,7040]{1,0:T(8,128)(2,1)}) %all-gather.5.cloned.1.call-update) | async-done | bytes 43253776 | tf_op jit(solution)/shard_map/all_gather | solution.py:201
  286.9 32.7 %multiply_convert_fusion.3 = (bf16[2304,3072]{1,0:T(8,128)(2,1)}, f32[2304,3072]{1,0:T(8,128)}) fusion(bf16[2304,1536]{1,0:T(8,128)(2,1)} %fusion.16, bf16[2,1536,7040]{2,1,0:T(8,128)(2,1)} %bitcast.380), kind=kOutput, calls=%fused_computation.16 | convolution fusion | flops 21778661376 | bytes 58982400 | tf_op jit(solution)/shard_map/dot_general | solution.py:47
  327.6 29.6 %fusion.33 = f32[2304,1536]{1,0:T(8,128)} fusion(bf16[2304,3072]{1,0:T(8,128)(2,1)} %get-tuple-element.81, bf16[2,1536,7040]{2,1,0:T(8,128)(2,1)} %bitcast.381), kind=kOutput, calls=%fused_computation.56 | convolution fusion | flops 21743271936 | bytes 37748736 | tf_op jit(solution)/shard_map/dot_general | solution.py:55
  357.2 31.5 %multiply_convert_fusion.2 = (bf16[2304,3072]{1,0:T(8,128)(2,1)}, f32[2304,3072]{1,0:T(8,128)}) fusion(bf16[2304,1536]{1,0:T(8,128)(2,1)S(1)} %bitcast.355, bf16[2,1536,7040]{2,1,0:T(8,128)(2,1)} %bitcast.382), kind=kOutput, calls=%fused_computation.14 | convolution fusion | flops 21778661376 | bytes 58982400 | tf_op jit(solution)/shard_map/dot_general | solution.py:47
  388.8 30.5 %convolution_add_fusion.1.branch_ref = f32[2304,1536]{1,0:T(8,128)} fusion(f32[2304,1536]{1,0:T(8,128)} %fusion.33, bf16[2304,3072]{1,0:T(8,128)(2,1)} %get-tuple-element.336, bf16[2,1536,7040]{2,1,0:T(8,128)(2,1)} %bitcast.383), kind=kOutput, calls=%fused_computation.30 | convolution fusion | flops 21746810880 | bytes 51904512 | tf_op jit(solution)/shard_map/dot_general | solution.py:55
  523.8 32.5 %shard_map.342 = (bf16[576,1024]{1,0:T(8,128)(2,1)}, f32[8,3,2,192]{3,2,1,0:T(2,128)}) custom-call(s32[3]{0:T(128)} %get-tuple-element.346.first_ref, s32[3]{0:T(128)} %get-tuple-element.345.last_ref, bf16[576,1024]{1,0:T(8,128)(2,1)} %pad_maximum_fusion.6.q_ref, bf16[576,1024]{1,0:T(8,128)(2,1)} %copy-done.122, bf16[576,1024]{1,0:T(8,128)(2,1)} %copy-done.55, ...), custom_call_target="tpu_custom_call" | custom-call | flops 40960000000 | bytes 20000000 | tf_op jit(solution)/shard_map/pallas_call | solution.py:667
  626.3 42.4 %shard_map.344 = (bf16[576,1024]{1,0:T(8,128)(2,1)}, f32[576,1024]{1,0:T(8,128)}, f32[576,1024]{1,0:T(8,128)}, bf16[2,576,1024]{2,1,0:T(8,128)(2,1)}, bf16[2,576,1024]{2,1,0:T(8,128)(2,1)}) custom-call(s32[3]{0:T(128)} %get-tuple-element.346.first_ref, s32[3]{0:T(128)} %get-tuple-element.345.last_ref, bf16[576,1024]{1,0:T(8,128)(2,1)} %pad_maximum_fusion.6.q_ref, ...), custom_call_target="tpu_custom_call" | custom-call | flops 56320000000 | bytes 20000000 | tf_op jit(solution)/shard_map/pallas_call | solution.py:755
  668.8 30.4 %collective-permute-start.18 = (bf16[2,576,1024]{2,1,0:T(8,128)(2,1)}, bf16[2,576,1024]{2,1,0:T(8,128)(2,1)}, u32[]{:S(2)}, u32[]{:S(2)}) collective-permute-start(bf16[2,576,1024]{2,1,0:T(8,128)(2,1)} %get-tuple-element.98), channel_id=1, source_target_pairs={{0,2},{2,4},{4,6},{6,8},{8,10},{10,12},{12,14},{14,16},{16,18},{18... | collective-permute-start | bytes 7077896 | tf_op jit(solution)/shard_map/ppermute | solution.py:975
  896.7 29.8 %convolution_convert_fusion.2 = bf16[1536,3072]{1,0:T(8,128)(2,1)} fusion(bf16[2304,1536]{1,0:T(8,128)(2,1)} %get-tuple-element.108, bf16[2304,3072]{1,0:T(8,128)(2,1)} %get-tuple-element.336), kind=kOutput, calls=%fused_computation.40 | convolution fusion | flops 21747990528 | bytes 30670848 | tf_op jit(solution)/shard_map/dot_general | solution.py:51
  926.6 25.2 %convolution_convert_fusion.3 = bf16[1536,3072]{1,0:T(8,128)(2,1)} fusion(bf16[2304,1536]{1,0:T(8,128)(2,1)S(1)} %copy-done.120, bf16[2304,3072]{1,0:T(8,128)(2,1)S(1)} %bitcast.428), kind=kOutput, calls=%fused_computation.41 | convolution fusion | flops 21747990528 | bytes 30670848 | tf_op jit(solution)/shard_map/dot_general | solution.py:51
  974.4 36.4 %multiply_convert_fusion.1 = bf16[2304,3072]{1,0:T(8,128)(2,1)} fusion(bf16[2304,1536]{1,0:T(8,128)(2,1)S(1)} %bitcast.426, f32[2304,3072]{1,0:T(8,128)} %get-tuple-element.335, bf16[2,1536,7040]{2,1,0:T(8,128)(2,1)} %bitcast.392), kind=kOutput, calls=%fused_computation.13 | convolution fusion | flops 21828206592 | bytes 58982400 | tf_op jit(solution)/shard_map/dot_general | solution.py:47
  1010.8 29.4 %fusion.35 = f32[2304,1536]{1,0:T(8,128)} fusion(bf16[2304,3072]{1,0:T(8,128)(2,1)} %multiply_convert_fusion.1, bf16[2,1536,7040]{2,1,0:T(8,128)(2,1)} %bitcast.393), kind=kOutput, calls=%fused_computation.58 | convolution fusion | flops 21743271936 | bytes 37748736 | tf_op jit(solution)/shard_map/dot_general | solution.py:55
  1040.3 27.6 %convolution_convert_fusion.1 = bf16[1536,3072]{1,0:T(8,128)(2,1)S(1)} fusion(bf16[2304,1536]{1,0:T(8,128)(2,1)} %fusion.16, bf16[2304,3072]{1,0:T(8,128)(2,1)} %multiply_convert_fusion.1), kind=kOutput, calls=%fused_computation.39 | convolution fusion | flops 21747990528 | bytes 30670848 | tf_op jit(solution)/shard_map/dot_general | solution.py:51
  1089.5 38.5 %multiply_convert_fusion = bf16[2304,3072]{1,0:T(8,128)(2,1)} fusion(bf16[2304,1536]{1,0:T(8,128)(2,1)} %get-tuple-element.108, f32[2304,3072]{1,0:T(8,128)} %get-tuple-element.337, bf16[2,1536,7040]{2,1,0:T(8,128)(2,1)} %bitcast.394), kind=kOutput, calls=%fused_computation.12 | convolution fusion | flops 21828206592 | bytes 58982400 | tf_op jit(solution)/shard_map/dot_general | solution.py:47
  1128.1 27.6 %convolution_convert_fusion = bf16[1536,3072]{1,0:T(8,128)(2,1)} fusion(bf16[2304,1536]{1,0:T(8,128)(2,1)S(1)} %bitcast.357, bf16[2304,3072]{1,0:T(8,128)(2,1)} %multiply_convert_fusion), kind=kOutput, calls=%fused_computation.38 | convolution fusion | flops 21747990528 | bytes 30670848 | tf_op jit(solution)/shard_map/dot_general | solution.py:51
  1155.7 36.4 %collective-permute-done.25 = bf16[1536,1536]{1,0:T(8,128)(2,1)} collective-permute-done((bf16[1536,1536]{1,0:T(8,128)(2,1)S(1)}, bf16[1536,1536]{1,0:T(8,128)(2,1)}, u32[]{:S(2)}, u32[]{:S(2)}) %collective-permute-start.25) | collective-permute-done | bytes 4718624 | tf_op jit(solution)/shard_map/ppermute | solution.py:221
  1192.1 32.8 %fusion.18 = (f32[2304]{0:T(1024)S(1)}, bf16[2304,1536]{1,0:T(8,128)(2,1)}) fusion(bf16[2304,1536]{1,0:T(8,128)(2,1)} %shard_map.340, f32[1536]{0:T(1024)S(1)} %copy-done.78, f32[2304]{0:T(1024)S(1)} %copy-done.71, f32[2304,1536]{1,0:T(8,128)} %fusion.35, bf16[2304,3072]{1,0:T(8,128)(2,1)} %multiply_convert_fusion, bf16[2,1536,7040]{2,1,0:T(8,128)(2,1)} %bitcast.395), kind=kOutput, calls=%fused_computation.33 | convolution fusion | flops 21771581440 | bytes 51929088 | tf_op jit(solution)/shard_map/dot_general | solution.py:55
  1241.1 27.4 %collective-permute-start.39 = (f32[8960]{0:T(1024)S(1)}, f32[8960]{0:T(1024)S(1)}, u32[]{:S(2)}, u32[]{:S(2)}) collective-permute-start(f32[8960]{0:T(1024)S(1)} %add.452), channel_id=1, source_target_pairs={{0,4},{2,6},{4,0},{6,2},{8,12},{10,14},{12,8},{14,10},{16,20},{18,... | collective-permute-start | bytes 107528 | tf_op jit(solution)/shard_map/ppermute | solution.py:262
  1313.5 59.1 %shard_map.347 = (bf16[1,48,36864]{2,1,0:T(8,128)(2,1)}, f32[56,768]{1,0:T(8,128)}) custom-call(s32[1]{0:T(128)S(6)} %sub.31.place_ref, bf16[2304,1536]{1,0:T(8,128)(2,1)} %add_convert_fusion.g_ref, bf16[48,8,1536]{2,1,0:T(8,128)(2,1)} %copy-done.126, bf16[48,8,1536]{2,1,0:T(8,128)(2,1)} %copy-done.125, ...), custom_call_target="tpu_custom_call" | custom-call | flops 69120000000 | bytes 25000000 | tf_op jit(solution)/shard_map/pallas_call | solution.py:450
  1372.6 42.6 %collective-permute-done.30 = bf16[1536,1536]{1,0:T(8,128)(2,1)} collective-permute-done((bf16[1536,1536]{1,0:T(8,128)(2,1)}, bf16[1536,1536]{1,0:T(8,128)(2,1)}, u32[]{:S(2)}, u32[]{:S(2)}) %collective-permute-start.30) | collective-permute-done | bytes 4718624 | tf_op jit(solution)/shard_map/ppermute | solution.py:221
  1434.6 59.8 %shard_map.348 = (f32[2,48,36864]{2,1,0:T(8,128)}, f32[56,768]{1,0:T(8,128)}) custom-call(s32[1]{0:T(128)} %bitcast.place_ref, bf16[2304,1536]{1,0:T(8,128)(2,1)} %add_convert_fusion.g_ref, bf16[48,8,1536]{2,1,0:T(8,128)(2,1)} %copy-done.126, bf16[48,8,1536]{2,1,0:T(8,128)(2,1)} %copy-done.125, bf16[48,36864]{1,0:T(8,128)(2,1)} %get-tuple-element.248.x_ref.own_ref, ...), custom_call_target="tpu_custom_call" | custom-call | flops 69120000000 | bytes 25000000 | tf_op jit(solution)/shard_map/pallas_call | solution.py:450
  (657 shorter events, 631.8 us)
Async XLA Ops:
  7.2 273.4 %all-gather.5.cloned.1.call-start = ((), (), s32[]{:S(2)}) async-start(), calls=%async_computation.10 | async-start | bytes 44605440 | tf_op jit(solution)/shard_map/all_gather | solution.py:201
  9.8 462.2 %all-gather.7.cloned.1.call-start = ((), (), s32[]{:S(2)}) async-start(), calls=%async_computation.11 | async-start | bytes 27574272 | tf_op jit(solution)/shard_map/all_gather | solution.py:201
  27.5 141.4 %collective-permute-start = (bf16[48,36864]{1,0:T(8,128)(2,1)S(1)}, bf16[48,36864]{1,0:T(8,128)(2,1)}, u32[]{:S(2)}, u32[]{:S(2)}) collective-permute-start(bf16[48,36864]{1,0:T(8,128)(2,1)S(1)} %get-tuple-element.249), channel_id=1, source_target_pairs={{0,1},{1,0},{2,3},{3,2},{4,5},{5,4},{6,7},{7,6},{8,9},{9,8},{10,11... | collective-permute-start | bytes 10616840 | tf_op jit(solution)/shard_map/ppermute | solution.py:106
  38.1 128.5 %collective-permute-start.3 = (bf16[2,8,36864]{2,1,0:T(8,128)(2,1)}, bf16[2,8,36864]{2,1,0:T(8,128)(2,1)}, u32[]{:S(2)}, u32[]{:S(2)}) collective-permute-start(bf16[2,8,36864]{2,1,0:T(8,128)(2,1)} %get-tuple-element.258), channel_id=1, source_target_pairs={{0,1},{1,0},{2,3},{3,2},{4,5},{5,4},{6,7},{7,6},{8,9},{9,8},{10,11... | collective-permute-start | bytes 3538952 | tf_op jit(solution)/shard_map/ppermute | solution.py:106
  281.7 677.2 %reduce-scatter.6.cloned.1.call-start = ((), (), s32[]{:S(2)}) async-start(), calls=%async_computation.5 | async-start | bytes 17825792 | tf_op jit(solution)/shard_map/reduce_scatter | solution.py:206
  319.6 99.6 %collective-permute-start.6 = (bf16[768]{0:T(1024)(128)(2,1)}, bf16[768]{0:T(1024)(128)(2,1)}, u32[]{:S(2)}, u32[]{:S(2)}) collective-permute-start(bf16[768]{0:T(1024)(128)(2,1)} %param.27), channel_id=1, source_target_pairs={{0,1},{1,0},{2,3},{3,2},{4,5},{5,4},{6,7},{7,6},{8,9},{9,8},{10,11... | collective-permute-start | bytes 4616 | tf_op jit(solution)/shard_map/ppermute | solution.py:843
  319.9 137.1 %collective-permute-start.7 = (bf16[9,512]{1,0:T(8,128)(2,1)}, bf16[9,512]{1,0:T(8,128)(2,1)}, u32[]{:S(2)}, u32[]{:S(2)}) collective-permute-start(bf16[9,512]{1,0:T(8,128)(2,1)} %param.29), channel_id=1, source_target_pairs={{0,1},{1,0},{2,3},{3,2},{4,5},{5,4},{6,7},{7,6},{8,9},{9,8},{10,11... | collective-permute-start | bytes 27656 | tf_op jit(solution)/shard_map/ppermute | solution.py:843
  323.6 142.4 %collective-permute-start.16 = (bf16[576,512]{1,0:T(8,128)(2,1)}, bf16[576,512]{1,0:T(8,128)(2,1)}, u32[]{:S(2)}, u32[]{:S(2)}) collective-permute-start(bf16[576,512]{1,0:T(8,128)(2,1)} %get-tuple-element.274), channel_id=1, source_target_pairs={{0,1},{1,0},{2,3},{3,2},{4,5},{5,4},{6,7},{7,6},{8,9},{9,8},{10,11... | collective-permute-start | bytes 1769480 | tf_op jit(solution)/shard_map/ppermute | solution.py:106
  325.9 141.5 %collective-permute-start.5 = (bf16[576,512]{1,0:T(8,128)(2,1)}, bf16[576,512]{1,0:T(8,128)(2,1)}, u32[]{:S(2)}, u32[]{:S(2)}) collective-permute-start(bf16[576,512]{1,0:T(8,128)(2,1)} %get-tuple-element.276), channel_id=1, source_target_pairs={{0,1},{1,0},{2,3},{3,2},{4,5},{5,4},{6,7},{7,6},{8,9},{9,8},{10,11... | collective-permute-start | bytes 1769480 | tf_op jit(solution)/shard_map/ppermute | solution.py:106
  457.0 104.6 %collective-permute-start.14 = (bf16[1,48,36864]{2,1,0:T(8,128)(2,1)}, bf16[1,48,36864]{2,1,0:T(8,128)(2,1)}, u32[]{:S(2)}, u32[]{:S(2)}) collective-permute-start(bf16[1,48,36864]{2,1,0:T(8,128)(2,1)} %get-tuple-element.88), channel_id=1, source_target_pairs={{0,1},{1,0},{2,3},{3,2},{4,5},{5,4},{6,7},{7,6},{8,9},{9,8},{10,11... | collective-permute-start | bytes 10616840 | tf_op jit(solution)/shard_map/ppermute | solution.py:951
  519.0 101.0 %collective-permute-start.17 = (bf16[48,36864]{1,0:T(8,128)(2,1)}, bf16[48,36864]{1,0:T(8,128)(2,1)}, u32[]{:S(2)}, u32[]{:S(2)}) collective-permute-start(bf16[48,36864]{1,0:T(8,128)(2,1)} %get-tuple-element.247), channel_id=1, source_target_pairs={{0,1},{1,0},{2,3},{3,2},{4,5},{5,4},{6,7},{7,6},{8,9},{9,8},{10,11... | collective-permute-start | bytes 10616840 | tf_op jit(solution)/shard_map/ppermute | solution.py:106
  620.1 752.5 %reduce-scatter.10.cloned.1.call-start = ((), (), s32[]{:S(2)}) async-start(), calls=%async_computation.7 | async-start | bytes 5849088 | tf_op jit(solution)/shard_map/reduce_scatter | solution.py:206
  718.6 120.3 %collective-permute-start.15 = (bf16[24,24,512]{2,1,0:T(8,128)(2,1)}, bf16[24,24,512]{2,1,0:T(8,128)(2,1)}, u32[]{:S(2)}, u32[]{:S(2)}) collective-permute-start(bf16[24,24,512]{2,1,0:T(8,128)(2,1)} %constant_dynamic-slice_fusion.13), channel_id=1, source_target_pairs={{0,1},{1,0},{2,3},{3,2},{4,5},{5,4},{6,7},{7,6},{8,9},{9,8},{10,11... | collective-permute-start | bytes 1769480 | tf_op jit(solution)/shard_map/ppermute | solution.py:1084
  834.7 537.9 %reduce-scatter.8.cloned.1.call-start = ((), (), s32[]{:S(2)}) async-start(), calls=%async_computation.6 | async-start | bytes 10584064 | tf_op jit(solution)/shard_map/reduce_scatter | solution.py:206
  856.5 100.5 %collective-permute-start.20 = (bf16[24,24,512]{2,1,0:T(8,128)(2,1)S(1)}, bf16[24,24,512]{2,1,0:T(8,128)(2,1)S(1)}, u32[]{:S(2)}, u32[]{:S(2)}) collective-permute-start(bf16[24,24,512]{2,1,0:T(8,128)(2,1)S(1)} %dynamic-slice_convert_fusion), channel_id=1, source_target_pairs={{0,1},{1,0},{2,3},{3,2},{4,5},{5,4},{6,7},{7,6},{8,9},{9,8},{10,11... | collective-permute-start | bytes 1769480 | tf_op jit(solution)/shard_map/ppermute | solution.py:1084
  951.8 463.4 %reduce-scatter.12.cloned.1.call-start = ((), (), s32[]{:S(2)}) async-start(), calls=%async_computation.8 | async-start | bytes 5308416 | tf_op jit(solution)/shard_map/reduce_scatter | solution.py:229
  962.0 105.9 %collective-permute-start.46 = (bf16[64,4096]{1,0:T(8,128)(2,1)}, bf16[64,4096]{1,0:T(8,128)(2,1)}, u32[]{:S(2)}, u32[]{:S(2)}) collective-permute-start(bf16[64,4096]{1,0:T(8,128)(2,1)} %pad_maximum_fusion.11), channel_id=1, source_target_pairs={{0,1},{1,0},{2,3},{3,2},{4,5},{5,4},{6,7},{7,6},{8,9},{9,8},{10,11... | collective-permute-start | bytes 1572872 | tf_op jit(solution)/shard_map/ppermute | solution.py:249
  971.9 99.1 %collective-permute-start.24 = (bf16[1536,1536]{1,0:T(8,128)(2,1)}, bf16[1536,1536]{1,0:T(8,128)(2,1)}, u32[]{:S(2)}, u32[]{:S(2)}) collective-permute-start(bf16[1536,1536]{1,0:T(8,128)(2,1)} %constant_dynamic-slice_fusion.10), channel_id=1, source_target_pairs={{0,2},{2,0},{1,3},{3,1},{4,6},{6,4},{5,7},{7,5},{8,10},{10,8},{9,1... | collective-permute-start | bytes 14155784 | tf_op jit(solution)/shard_map/ppermute | solution.py:214
  974.4 102.5 %collective-permute-start.23 = (bf16[1536,1536]{1,0:T(8,128)(2,1)}, bf16[1536,1536]{1,0:T(8,128)(2,1)}, u32[]{:S(2)}, u32[]{:S(2)}) collective-permute-start(bf16[1536,1536]{1,0:T(8,128)(2,1)} %constant_dynamic-slice_fusion.11), channel_id=1, source_target_pairs={{0,2},{2,0},{1,3},{3,1},{4,6},{6,4},{5,7},{7,5},{8,10},{10,8},{9,1... | collective-permute-start | bytes 14155784 | tf_op jit(solution)/shard_map/ppermute | solution.py:214
  1086.5 198.5 %collective-permute-start.26 = (bf16[1536,1536]{1,0:T(8,128)(2,1)}, bf16[1536,1536]{1,0:T(8,128)(2,1)}, u32[]{:S(2)}, u32[]{:S(2)}) collective-permute-start(bf16[1536,1536]{1,0:T(8,128)(2,1)} %constant_dynamic-slice_fusion.9), channel_id=1, source_target_pairs={{0,2},{2,0},{1,3},{3,1},{4,6},{6,4},{5,7},{7,5},{8,10},{10,8},{9,1... | collective-permute-start | bytes 14155784 | tf_op jit(solution)/shard_map/ppermute | solution.py:214
  1087.7 104.3 %collective-permute-start.25 = (bf16[1536,1536]{1,0:T(8,128)(2,1)S(1)}, bf16[1536,1536]{1,0:T(8,128)(2,1)}, u32[]{:S(2)}, u32[]{:S(2)}) collective-permute-start(bf16[1536,1536]{1,0:T(8,128)(2,1)S(1)} %broadcast_select_fusion.1), channel_id=1, source_target_pairs={{0,1},{1,0},{2,3},{3,2},{4,5},{5,4},{6,7},{7,6},{8,9},{9,8},{10,11... | collective-permute-start | bytes 14155784 | tf_op jit(solution)/shard_map/ppermute | solution.py:221
  1282.3 277.4 %reduce-scatter.14.cloned.1.call-start = ((), (), s32[]{:S(2)}) async-start(), calls=%async_computation.9 | async-start | bytes 5308416 | tf_op jit(solution)/shard_map/reduce_scatter | solution.py:229
  1310.7 104.5 %collective-permute-start.30 = (bf16[1536,1536]{1,0:T(8,128)(2,1)}, bf16[1536,1536]{1,0:T(8,128)(2,1)}, u32[]{:S(2)}, u32[]{:S(2)}) collective-permute-start(bf16[1536,1536]{1,0:T(8,128)(2,1)} %broadcast_select_fusion), channel_id=1, source_target_pairs={{0,1},{1,0},{2,3},{3,2},{4,5},{5,4},{6,7},{7,6},{8,9},{9,8},{10,11... | collective-permute-start | bytes 14155784 | tf_op jit(solution)/shard_map/ppermute | solution.py:221
  1432.6 98.8 %collective-permute-start.45 = (bf16[64,2432]{1,0:T(8,128)(2,1)}, bf16[64,2432]{1,0:T(8,128)(2,1)}, u32[]{:S(2)}, u32[]{:S(2)}) collective-permute-start(bf16[64,2432]{1,0:T(8,128)(2,1)} %dynamic-slice_dynamic-update-slice_fusion), channel_id=1, source_target_pairs={{0,1},{1,0},{2,3},{3,2},{4,5},{5,4},{6,7},{7,6},{8,9},{9,8},{10,11... | collective-permute-start | bytes 933896 | tf_op jit(solution)/shard_map/ppermute | solution.py:249
  (182 other events, 3293.7 us)
Sparse Core Ops, SparseCore 0:
  11.5 269.0 all-gather.4
  284.1 160.3 all-gather.6
  620.2 244.2 reduce-scatter.5
  868.2 90.0 reduce-scatter.9
  962.9 137.4 reduce-scatter.7
  1282.4 107.6 reduce-scatter.11
  1427.3 93.1 reduce-scatter.13

commit v5 on v3

--- a/solution.py
+++ b/solution.py
@@ -215,8 +215,20 @@
     return (own.astype(F32) + got.astype(F32)).astype(BF)
 
 
-def reduce_chips(terms):
-    both = lax.psum_scatter(terms, "chip", scatter_dimension=0, tiled=True)
+def add_low(own, got):
+    return (own.astype(F32) + got.astype(F32)).astype(BF)
+
+
+def chip_step(terms, bit):
+    pairs = terms.reshape(terms.shape[0] // 2, 2, *terms.shape[1:])
+    side = (lax.axis_index("chip") // bit) % 2
+    own = lax.dynamic_index_in_dim(pairs, side, 1, keepdims=False)
+    sent = lax.dynamic_index_in_dim(pairs, 1 - side, 1, keepdims=False)
+    got = lax.ppermute(sent, "chip", [(i, i ^ bit) for i in range(lax.axis_size("chip"))])
+    return own, got
+
+
+def all_columns(both):
     rows = both.shape[0] // 2
     core = lax.axis_index("core")
     own = lax.dynamic_slice_in_dim(both, core * rows, rows, 0)
@@ -1014,27 +1026,29 @@
     w1_second = matmul_tn(normed_low, grad_second).astype(BF)
     grad_second, w1_second = together(grad_second, w1_second)
     core_second = core_sum(w1_second)
-    normed_grad = partial_sums(
-        matmul_nt(grad_first, mlp_in[0]) + matmul_nt(grad_second, mlp_in[1])
-    ).astype(BF)
+    normed_part = matmul_nt(grad_first, mlp_in[0])
+    normed_part, core_first, core_second = together(normed_part, core_first, core_second)
+    w1_own = jnp.where(first, core_first, core_second)
+    w1_sent = jnp.where(first, core_second, core_first)
+    piece = w1_sent.shape[1] // 2
+    w1_got = [
+        lax.ppermute(item, "mb", SWAP) for item in (w1_sent[:, :piece], w1_sent[:, piece:])
+    ]
+    normed_grad = partial_sums(normed_part + matmul_nt(grad_second, mlp_in[1])).astype(BF)
     back_conv, grad_cn_gain = norm_pull(features(normed_grad).astype(F32))
-    conv_grad, core_first, core_second = together(
-        own_slice(back_conv).astype(BF), core_first, core_second
-    )
-    w1_sent, w1_own = jnp.where(first, core_second, core_first), jnp.where(first, core_first, core_second)
-    w1_got = lax.ppermute(w1_sent, "mb", SWAP)
+    conv_grad, w1_got[0] = together(own_slice(back_conv).astype(BF), w1_got[0])
     conv_cols = conv_grad.reshape(hi_cols, hi_rows, c_own)
     grad_up, grad_down = rim_pair(conv_cols, RIM, 1)
     if fast:
         ghi_sent, taps_other = conv_backward(
             conv_grad, grad_up, grad_down, hi_other, cot_other, pool_cols, other_taps, mask, other_place, 1, BF
         )
-        conv_grad, ghi_sent, w1_got = together(conv_grad, ghi_sent, w1_got)
+        conv_grad, ghi_sent, w1_got[1] = together(conv_grad, ghi_sent, w1_got[1])
+        w1_sum = add_low(w1_own, jnp.concatenate(w1_got, axis=1))
         ghi_mine, taps_own = conv_backward(
             conv_grad, grad_up, grad_down, hi_own, cot_own, pool_cols, own_taps, mask, own_place, 2, F32
         )
-        w1_sum = (w1_own.astype(F32) + w1_got.astype(F32)).astype(BF)
-        grad_cn_kernel = in_order(taps_own[:49], taps_other[:49], 1)
+        tap_sums = jnp.concatenate([taps_own, taps_other])
     else:
         conv_grad = conv_cols.transpose(1, 0, 2)
         conv_pad = jnp.concatenate(
@@ -1042,26 +1056,39 @@
         )
         hi_back = hi_grad + depthwise(conv_pad, conv_taps, hi_ids, hi_mid, 7, True)
         grad_cn_kernel = tap_grads(hi_pad, conv_grad, hi_ids, hi_mid, 7)
-        w1_sum = (w1_own.astype(F32) + w1_got.astype(F32)).astype(BF)
-    w1_sum, s_att, s_ad, *s_w2 = together(w1_sum, s_att, s_ad, *s_w2)
-
-    own_terms, sent_terms = zip(*[halves(item) for item in (grad_cn_kernel, grad_scale, grad_ad_kernel)])
-    gains = [grad_cn_gain, grad_ln1, grad_ln2]
-    flat, sent = [
-        jnp.concatenate([item.reshape(-1) for item in (*terms, *gains)])
-        for terms in (own_terms, sent_terms)
-    ]
-    flat, sent, w1_sum = together(flat, sent, w1_sum)
-    g_w1 = reduce_chips(w1_sum).astype(F32)
-    flat = flat + lax.ppermute(sent, "mb", SWAP)
+        tap_sums = jnp.concatenate(halves(grad_cn_kernel))
+        w1_sum = add_low(w1_own, jnp.concatenate(w1_got, axis=1))
+
+    chips = lax.axis_size("chip")
+    w1_sum = w1_sum.reshape(chips, w1_sum.shape[0] // chips, w1_sum.shape[1])
+    if chips & (chips - 1):
+        w1_sum = lax.psum_scatter(w1_sum, "chip", scatter_dimension=0, tiled=True)
+    else:
+        own, got = chip_step(w1_sum, 1)
+        tap_sums, got, s_att, s_ad = together(tap_sums, got, s_att, s_ad)
+        w1_sum, bit = add_low(own, got), 2
+        while bit < chips:
+            w1_sum, bit = add_low(*chip_step(w1_sum, bit)), 2 * bit
+
+    own_terms, sent_terms = zip(*[halves(item) for item in (grad_scale, grad_ad_kernel)])
+    others = (*own_terms, *sent_terms, grad_cn_gain, grad_ln1, grad_ln2)
+    sizes = [int(item) for item in np.cumsum([0] + [item.size for item in others])]
+    flat = jnp.concatenate([item.reshape(-1) for item in others])
+    flat = jnp.pad(flat, (0, -sizes[-1] % (8 * c_shard))).reshape(-1, c_shard)
+    tap_rows = tap_sums.shape[0] // 2
+    small = jnp.concatenate([tap_sums, flat])
     if fast:
         ghi_got = lax.ppermute(ghi_sent, "mb", SWAP)
-    flat = sum_everywhere(flat)
-    sizes = np.cumsum([0] + [item.size for item in (*own_terms, *gains)])
-    g_kernel, g_scale, g_taps, *gain_sums = [
-        flat[int(sizes[i]) : int(sizes[i + 1])].reshape(item.shape)
-        for i, item in enumerate((*own_terms, *gains))
+        small, ghi_got = together(small, ghi_got)
+    small = sum_everywhere(small)
+    got = lax.ppermute(small[tap_rows:], "mb", SWAP)
+    g_kernel = (small[:tap_rows] + got[:tap_rows])[: cn_kernel.shape[0]]
+    flat, got = small[2 * tap_rows :].reshape(-1), got[tap_rows:].reshape(-1)
+    pieces = [
+        (flat[sizes[i] : sizes[i + 1]] + got[sizes[j] : sizes[j + 1]]).reshape(others[i].shape)
+        for i, j in ((0, 2), (1, 3), (4, 4), (5, 5), (6, 6))
     ]
+    g_scale, g_taps, *gain_sums = pieces
 
     def leave(values, kind):
         own, sent = halves(values)
@@ -1080,15 +1107,19 @@
     glo_stack = leave(grad_one.reshape(row_count, col_count, d_own), F32)
 
     (g_w2,) = settle(jnp.concatenate(s_w2, axis=1), (hid_shard,))
+    hi_stack = hi_stack.reshape(2, hi_rows, 1, hi_cols * c_shard)
+    ghi_stack, w1_sum = together(ghi_stack.reshape(2, hi_rows, -1, 128), w1_sum)
+    ghi_stack = ghi_stack.reshape(2, hi_rows, 1, hi_cols * c_shard)
+    g_w1 = all_columns(w1_sum.reshape(-1, w1_sum.shape[-1])).astype(F32)
     g_fc1, g_fc2 = settle(s_ff, (ff_shard, ff_shard))
     g_gate_w2, g_q, g_k, g_v, g_out = settle(s_att, (gh_shard, d_shard, d_shard, d_shard, d_shard))
     g_ad, g_gate_w1 = settle(s_ad, (d_shard, gh_shard))
 
     return (
         lo_stack,
-        hi_stack.reshape(2, hi_rows, 1, hi_cols * c_shard),
+        hi_stack,
         glo_stack,
-        ghi_stack.reshape(2, hi_rows, 1, hi_cols * c_shard),
+        ghi_stack,
         g_kernel,
         gain_sums[0],
         g_w1,

time: 1550 us -> 1530 us (0.987)
  Pallas kernels: 359 us -> 325 us
  starting transfers between devices: 171 us -> 192 us
  local copies, waits for them, and re-layouts: 128 us -> 110 us
    ppermute x4, starting transfers between devices: 66 us -> 0.95 us  [sum_everywhere(): lax.ppermute(flat, TILE, [(i, i ^ bit) for i in range(devices)])]
    ppermute x3 -> x7, starting transfers between devices: 3.63 us -> 63.6 us  [the longest x3 58.9 us: chip_step(): lax.ppermute(sent, 'chip', [(i, i ^ bit) for i in range(lax.axis_size('ch...]
    reduce_scatter x1 -> x0, waiting for transfers between devices: 44.5 us -> none  [reduce_chips(): both = lax.psum_scatter(terms, 'chip', scatter_dimension=0, tiled=True)]
    ppermute x4, waiting for transfers between devices: 10.9 us -> 38.5 us  [sum_everywhere(): lax.ppermute(flat, TILE, [(i, i ^ bit) for i in range(devices)])]
    ppermute x4, waiting for transfers between devices: 0.9 us -> 22.2 us  [settle(): got = lax.ppermute(jnp.concatenate(sent, axis=1), 'mb', SWAP)]
    ppermute x2, starting transfers between devices: 2.85 us -> 23.6 us  [leave(): other = lax.ppermute(sent.astype(BF), 'mb', SWAP)]
    pallas_call x1, Pallas kernels: 53.6 us -> 35 us  [attend_back(): pl.pallas_call(attend_back_kernel, out_shape=(jax.ShapeDtypeStruct(q.shap...]
    ppermute x2, starting transfers between devices: 40.7 us -> 22.4 us  [rim_rows(): before = lax.ppermute(value[length - width:], TILE, up)]
  transfers between devices with their start and end apart: 47 -> 50, of which waited for: 9 -> 12; matrix products, arithmetic and copies ran while one was open for 49% -> 48% of each run, Pallas kernels for 23% -> 21%
where the time goes in v5:
time: 1530 us; the launch traced here: 1520 us
  matrix products  508 us (33%)
  Pallas kernels  325 us (21%)
  waiting for transfers between devices  226 us (15%)
  starting transfers between devices  192 us (13%)
  other arithmetic  139 us (9%)
  local copies, waits for them, and re-layouts  110 us (7%)
  between operations  16.9 us (1%)
    dot_general x22, matrix products, matmul(): return jnp.dot(left, right, preferred_element_type=F32)  201 us
    dot_general x22, matrix products, matmul_nt(): lax.dot_general(left, right, (((1,), (1,)), ((), ())), preferred_element_...  190 us
    pallas_call x2, Pallas kernels, conv_backward(): pl.pallas_call(back_kernel, out_shape=(jax.ShapeDtypeStruct((slots, *x.sh...  119 us
    dot_general x5, matrix products, matmul_tn(): lax.dot_general(left, right, (((0,), (0,)), ((), ())), preferred_element_...  117 us
    ppermute x5, waiting for transfers between devices, swap_micro(): return (own, lax.ppermute(sent, 'mb', SWAP))  88.3 us
    pallas_call x2, Pallas kernels, conv_forward(): pl.pallas_call(kernel, out_shape=jax.ShapeDtypeStruct((48 * 48, 2 * width...  72.7 us
    all_gather x2, waiting for transfers between devices, gather_all(): full = lax.all_gather(shard, ALL, axis=0)  62.6 us
    ppermute x3, starting transfers between devices, chip_step(): lax.ppermute(sent, 'chip', [(i, i ^ bit) for i in range(lax.axis_size('ch...  58.9 us
  transfers between devices with their start and end apart: 50, of which 12 were waited for; matrix products, arithmetic and copies ran while one was open for 48% of the time, Pallas kernels for 21%

profile of v5, /device:TPU:0, one launch (start us, length us, event | category | flops | bytes accessed | tf_op | source)
XLA Modules:
  0.0 1516.5 jit_solution(10616571326911102971)
XLA Ops:
  41.9 36.4 %shard_map.339.into_ref = bf16[2304,1536]{1,0:T(8,128)(2,1)} custom-call(s32[1]{0:T(128)} %bitcast.place_ref, bf16[48,36864]{1,0:T(8,128)(2,1)} %get-tuple-element.246.x_ref.own_ref, bf16[8,36864]{1,0:T(8,128)(2,1)} %get-tuple-element.280.top_ref, bf16[8,36864]{1,0:T(8,128)(2,1)} %get-tuple-element.279.bot_ref, f32[49,768]{1,0:T(8,128)} %convert_element_type.475.taps_ref, ...), custom_call_target="tpu_custom_call" | custom-call | flops 41472000000 | bytes 12000000 | tf_op jit(solution)/shard_map/pallas_call | solution.py:343
  78.3 88.3 %collective-permute-done.3 = bf16[2,8,36864]{2,1,0:T(8,128)(2,1)} collective-permute-done((bf16[2,8,36864]{2,1,0:T(8,128)(2,1)}, bf16[2,8,36864]{2,1,0:T(8,128)(2,1)}, u32[]{:S(2)}, u32[]{:S(2)}) %collective-permute-start.3) | collective-permute-done | bytes 1179680 | tf_op jit(solution)/shard_map/ppermute | solution.py:106
  168.9 36.4 %shard_map.340 = bf16[2304,1536]{1,0:T(8,128)(2,1)} custom-call(s32[1]{0:T(128)S(6)} %sub.45.place_ref, bf16[48,36864]{1,0:T(8,128)(2,1)} %collective-permute-done.x_ref.other_ref, bf16[8,36864]{1,0:T(8,128)(2,1)} %get-tuple-element.282.top_ref, bf16[8,36864]{1,0:T(8,128)(2,1)} %get-tuple-element.281.bot_ref, ...), custom_call_target="tpu_custom_call", output_to_operand_aliasing={{}: (6, {})} | custom-call | flops 41472000000 | bytes 12000000 | tf_op jit(solution)/shard_map/pallas_call | solution.py:343
  218.0 62.6 %all-gather.5.cloned.1.call-done = bf16[3072,7040]{1,0:T(8,128)(2,1)} async-done(((bf16[96,7040]{1,0:T(8,128)(2,1)}), bf16[3072,7040]{1,0:T(8,128)(2,1)}) %all-gather.5.cloned.1.call-update) | async-done | bytes 43253776 | tf_op jit(solution)/shard_map/all_gather | solution.py:201
  286.9 32.6 %multiply_convert_fusion.3 = (bf16[2304,3072]{1,0:T(8,128)(2,1)}, f32[2304,3072]{1,0:T(8,128)}) fusion(bf16[2304,1536]{1,0:T(8,128)(2,1)} %fusion.16, bf16[2,1536,7040]{2,1,0:T(8,128)(2,1)} %bitcast.398), kind=kOutput, calls=%fused_computation.16 | convolution fusion | flops 21778661376 | bytes 58982400 | tf_op jit(solution)/shard_map/dot_general | solution.py:47
  327.6 29.6 %fusion.33 = f32[2304,1536]{1,0:T(8,128)} fusion(bf16[2304,3072]{1,0:T(8,128)(2,1)} %get-tuple-element.80, bf16[2,1536,7040]{2,1,0:T(8,128)(2,1)} %bitcast.399), kind=kOutput, calls=%fused_computation.56 | convolution fusion | flops 21743271936 | bytes 37748736 | tf_op jit(solution)/shard_map/dot_general | solution.py:55
  357.2 31.4 %multiply_convert_fusion.2 = (bf16[2304,3072]{1,0:T(8,128)(2,1)}, f32[2304,3072]{1,0:T(8,128)}) fusion(bf16[2304,1536]{1,0:T(8,128)(2,1)S(1)} %bitcast.373, bf16[2,1536,7040]{2,1,0:T(8,128)(2,1)} %bitcast.400), kind=kOutput, calls=%fused_computation.14 | convolution fusion | flops 21778661376 | bytes 58982400 | tf_op jit(solution)/shard_map/dot_general | solution.py:47
  388.6 30.5 %convolution_add_fusion.1.branch_ref = f32[2304,1536]{1,0:T(8,128)} fusion(f32[2304,1536]{1,0:T(8,128)} %fusion.33, bf16[2304,3072]{1,0:T(8,128)(2,1)} %get-tuple-element.324, bf16[2,1536,7040]{2,1,0:T(8,128)(2,1)} %bitcast.401), kind=kOutput, calls=%fused_computation.30 | convolution fusion | flops 21746810880 | bytes 51904512 | tf_op jit(solution)/shard_map/dot_general | solution.py:55
  523.8 26.6 %shard_map.342 = (bf16[576,1024]{1,0:T(8,128)(2,1)}, f32[8,3,2,192]{3,2,1,0:T(2,128)}) custom-call(s32[3]{0:T(128)} %get-tuple-element.334.first_ref, s32[3]{0:T(128)} %get-tuple-element.333.last_ref, bf16[576,1024]{1,0:T(8,128)(2,1)} %pad_maximum_fusion.6.q_ref, bf16[576,1024]{1,0:T(8,128)(2,1)} %copy-done.118, bf16[576,1024]{1,0:T(8,128)(2,1)} %copy-done.56, ...), custom_call_target="tpu_custom_call" | custom-call | flops 40960000000 | bytes 20000000 | tf_op jit(solution)/shard_map/pallas_call | solution.py:666
  591.7 22.4 %shard_map.343 = bf16[1024,8192]{1,0:T(8,128)(2,1)} custom-call(bf16[1024,576]{1,0:T(8,128)(2,1)} %get-tuple-element.266.refs_0_, bf16[1024,576]{1,0:T(8,128)(2,1)} %fusion.210.refs_1_, bf16[576,4096]{1,0:T(8,128)(2,1)} %copy-done.34, bf16[576,4096]{1,0:T(8,128)(2,1)} %get-tuple-element.241.refs_3_), custom_call_target="tpu_custom_call" | custom-call | flops 24159191040 | bytes 16777216 | tf_op jit(solution)/shard_map/pallas_call | solution.py:189
  620.6 35.0 %shard_map.344 = (bf16[576,1024]{1,0:T(8,128)(2,1)}, f32[576,1024]{1,0:T(8,128)}, f32[576,1024]{1,0:T(8,128)}, bf16[2,576,1024]{2,1,0:T(8,128)(2,1)}, bf16[2,576,1024]{2,1,0:T(8,128)(2,1)}) custom-call(s32[3]{0:T(128)} %get-tuple-element.334.first_ref, s32[3]{0:T(128)} %get-tuple-element.333.last_ref, bf16[576,1024]{1,0:T(8,128)(2,1)} %pad_maximum_fusion.6.q_ref, ...), custom_call_target="tpu_custom_call" | custom-call | flops 56320000000 | bytes 20000000 | tf_op jit(solution)/shard_map/pallas_call | solution.py:754
  655.6 23.4 %collective-permute-start.18 = (bf16[2,576,1024]{2,1,0:T(8,128)(2,1)}, bf16[2,576,1024]{2,1,0:T(8,128)(2,1)}, u32[]{:S(2)}, u32[]{:S(2)}) collective-permute-start(bf16[2,576,1024]{2,1,0:T(8,128)(2,1)} %get-tuple-element.97), channel_id=1, source_target_pairs={{0,2},{2,4},{4,6},{6,8},{8,10},{10,12},{12,14},{14,16},{16,18},{18... | collective-permute-start | bytes 7077896 | tf_op jit(solution)/shard_map/ppermute | solution.py:974
  699.4 20.8 %collective-permute-start.15 = (bf16[24,24,512]{2,1,0:T(8,128)(2,1)}, bf16[24,24,512]{2,1,0:T(8,128)(2,1)}, u32[]{:S(2)}, u32[]{:S(2)}) collective-permute-start(bf16[24,24,512]{2,1,0:T(8,128)(2,1)} %constant_dynamic-slice_fusion.11), channel_id=1, source_target_pairs={{0,1},{1,0},{2,3},{3,2},{4,5},{5,4},{6,7},{7,6},{8,9},{9,8},{10,11... | collective-permute-start | bytes 1769480 | tf_op jit(solution)/shard_map/ppermute | solution.py:1095
  872.9 29.2 %convolution_convert_fusion.2 = bf16[1536,3072]{1,0:T(8,128)(2,1)} fusion(bf16[2304,1536]{1,0:T(8,128)(2,1)} %get-tuple-element.106, bf16[2304,3072]{1,0:T(8,128)(2,1)} %get-tuple-element.324), kind=kOutput, calls=%fused_computation.40 | convolution fusion | flops 21747990528 | bytes 30670848 | tf_op jit(solution)/shard_map/dot_general | solution.py:51
  902.1 28.7 %convolution_convert_fusion.3 = bf16[1536,3072]{1,0:T(8,128)(2,1)} fusion(bf16[2304,1536]{1,0:T(8,128)(2,1)} %get-tuple-element.106, bf16[2304,3072]{1,0:T(8,128)(2,1)} %get-tuple-element.80), kind=kOutput, calls=%fused_computation.41 | convolution fusion | flops 21747990528 | bytes 30670848 | tf_op jit(solution)/shard_map/dot_general | solution.py:51
  934.9 38.7 %multiply_convert_fusion.1 = bf16[2304,3072]{1,0:T(8,128)(2,1)} fusion(bf16[2304,1536]{1,0:T(8,128)(2,1)} %get-tuple-element.106, f32[2304,3072]{1,0:T(8,128)} %get-tuple-element.323, bf16[2,1536,7040]{2,1,0:T(8,128)(2,1)} %bitcast.410), kind=kOutput, calls=%fused_computation.13 | convolution fusion | flops 21828206592 | bytes 58982400 | tf_op jit(solution)/shard_map/dot_general | solution.py:47
  973.6 26.2 %convolution_convert_fusion.1 = bf16[1536,3072]{1,0:T(8,128)(2,1)S(1)} fusion(bf16[2304,1536]{1,0:T(8,128)(2,1)S(1)} %bitcast.375, bf16[2304,3072]{1,0:T(8,128)(2,1)} %multiply_convert_fusion.1), kind=kOutput, calls=%fused_computation.39 | convolution fusion | flops 21747990528 | bytes 30670848 | tf_op jit(solution)/shard_map/dot_general | solution.py:51
  999.8 42.2 %multiply_convert_fusion = bf16[2304,3072]{1,0:T(8,128)(2,1)} fusion(bf16[2304,1536]{1,0:T(8,128)(2,1)} %get-tuple-element.106, f32[2304,3072]{1,0:T(8,128)} %get-tuple-element.325, bf16[2,1536,7040]{2,1,0:T(8,128)(2,1)} %bitcast.411), kind=kOutput, calls=%fused_computation.12 | convolution fusion | flops 21828206592 | bytes 58982400 | tf_op jit(solution)/shard_map/dot_general | solution.py:47
  1042.0 26.3 %convolution_convert_fusion = bf16[1536,3072]{1,0:T(8,128)(2,1)S(1)} fusion(bf16[2304,1536]{1,0:T(8,128)(2,1)S(1)} %bitcast.375, bf16[2304,3072]{1,0:T(8,128)(2,1)} %multiply_convert_fusion), kind=kOutput, calls=%fused_computation.38 | convolution fusion | flops 21747990528 | bytes 30670848 | tf_op jit(solution)/shard_map/dot_general | solution.py:51
  1087.0 29.6 %fusion.35 = f32[2304,1536]{1,0:T(8,128)} fusion(bf16[2304,3072]{1,0:T(8,128)(2,1)} %multiply_convert_fusion.1, bf16[2,1536,7040]{2,1,0:T(8,128)(2,1)} %bitcast.412), kind=kOutput, calls=%fused_computation.58 | convolution fusion | flops 21743271936 | bytes 37748736 | tf_op jit(solution)/shard_map/dot_general | solution.py:55
  1134.1 35.0 %fusion.18 = (f32[2304]{0:T(1024)S(1)}, bf16[2304,1536]{1,0:T(8,128)(2,1)}) fusion(bf16[2304,1536]{1,0:T(8,128)(2,1)} %shard_map.340, f32[1536]{0:T(1024)S(1)} %copy-done.72, f32[2304]{0:T(1024)S(1)} %copy-done.63, f32[2304,1536]{1,0:T(8,128)} %fusion.35, bf16[2304,3072]{1,0:T(8,128)(2,1)} %multiply_convert_fusion, bf16[2,1536,7040]{2,1,0:T(8,128)(2,1)} %bitcast.413), kind=kOutput, calls=%fused_computation.33 | convolution fusion | flops 21771581440 | bytes 51929088 | tf_op jit(solution)/shard_map/dot_general | solution.py:55
  1201.4 59.1 %shard_map.347 = (bf16[1,48,36864]{2,1,0:T(8,128)(2,1)}, f32[56,768]{1,0:T(8,128)}) custom-call(s32[1]{0:T(128)S(6)} %sub.45.place_ref, bf16[2304,1536]{1,0:T(8,128)(2,1)} %copy-done.18, bf16[48,8,1536]{2,1,0:T(8,128)(2,1)} %collective-permute-done.26.top_ref, bf16[48,8,1536]{2,1,0:T(8,128)(2,1)} %collective-permute-done.27.bot_ref, ...), custom_call_target="tpu_custom_call" | custom-call | flops 69120000000 | bytes 25000000 | tf_op jit(solution)/shard_map/pallas_call | solution.py:449
  1268.9 50.5 %collective-permute-start.29 = (bf16[4,192,1536]{2,1,0:T(8,128)(2,1)}, bf16[4,192,1536]{2,1,0:T(8,128)(2,1)S(1)}, u32[]{:S(2)}, u32[]{:S(2)}) collective-permute-start(bf16[4,192,1536]{2,1,0:T(8,128)(2,1)} %dynamic-slice_bitcast_fusion.4), channel_id=1, source_target_pairs={{0,4},{4,0},{8,12},{12,8},{16,20},{20,16},{24,28},{28,24},{1,5},{5... | collective-permute-start | bytes 7077896 | tf_op jit(solution)/shard_map/ppermute | solution.py:227
  1321.7 60.1 %shard_map.348 = (f32[2,48,36864]{2,1,0:T(8,128)}, f32[56,768]{1,0:T(8,128)}) custom-call(s32[1]{0:T(128)} %bitcast.place_ref, bf16[2304,1536]{1,0:T(8,128)(2,1)} %copy-done.18, bf16[48,8,1536]{2,1,0:T(8,128)(2,1)} %collective-permute-done.26.top_ref, bf16[48,8,1536]{2,1,0:T(8,128)(2,1)} %collective-permute-done.27.bot_ref, ...), custom_call_target="tpu_custom_call" | custom-call | flops 69120000000 | bytes 25000000 | tf_op jit(solution)/shard_map/pallas_call | solution.py:449
  (618 shorter events, 598.2 us)
Async XLA Ops:
  7.2 273.4 %all-gather.5.cloned.1.call-start = ((), (), s32[]{:S(2)}) async-start(), calls=%async_computation.10 | async-start | bytes 44605440 | tf_op jit(solution)/shard_map/all_gather | solution.py:201
  9.8 461.6 %all-gather.7.cloned.1.call-start = ((), (), s32[]{:S(2)}) async-start(), calls=%async_computation.11 | async-start | bytes 27574272 | tf_op jit(solution)/shard_map/all_gather | solution.py:201
  27.5 141.4 %collective-permute-start = (bf16[48,36864]{1,0:T(8,128)(2,1)S(1)}, bf16[48,36864]{1,0:T(8,128)(2,1)}, u32[]{:S(2)}, u32[]{:S(2)}) collective-permute-start(bf16[48,36864]{1,0:T(8,128)(2,1)S(1)} %get-tuple-element.247), channel_id=1, source_target_pairs={{0,1},{1,0},{2,3},{3,2},{4,5},{5,4},{6,7},{7,6},{8,9},{9,8},{10,11... | collective-permute-start | bytes 10616840 | tf_op jit(solution)/shard_map/ppermute | solution.py:106
  38.0 128.5 %collective-permute-start.3 = (bf16[2,8,36864]{2,1,0:T(8,128)(2,1)}, bf16[2,8,36864]{2,1,0:T(8,128)(2,1)}, u32[]{:S(2)}, u32[]{:S(2)}) collective-permute-start(bf16[2,8,36864]{2,1,0:T(8,128)(2,1)} %get-tuple-element.258), channel_id=1, source_target_pairs={{0,1},{1,0},{2,3},{3,2},{4,5},{5,4},{6,7},{7,6},{8,9},{9,8},{10,11... | collective-permute-start | bytes 3538952 | tf_op jit(solution)/shard_map/ppermute | solution.py:106
  281.7 650.1 %reduce-scatter.6.cloned.1.call-start = ((), (), s32[]{:S(2)}) async-start(), calls=%async_computation.5 | async-start | bytes 17825792 | tf_op jit(solution)/shard_map/reduce_scatter | solution.py:206
  319.5 99.6 %collective-permute-start.6 = (bf16[768]{0:T(1024)(128)(2,1)}, bf16[768]{0:T(1024)(128)(2,1)}, u32[]{:S(2)}, u32[]{:S(2)}) collective-permute-start(bf16[768]{0:T(1024)(128)(2,1)} %param.27), channel_id=1, source_target_pairs={{0,1},{1,0},{2,3},{3,2},{4,5},{5,4},{6,7},{7,6},{8,9},{9,8},{10,11... | collective-permute-start | bytes 4616 | tf_op jit(solution)/shard_map/ppermute | solution.py:842
  319.8 136.6 %collective-permute-start.7 = (bf16[9,512]{1,0:T(8,128)(2,1)}, bf16[9,512]{1,0:T(8,128)(2,1)}, u32[]{:S(2)}, u32[]{:S(2)}) collective-permute-start(bf16[9,512]{1,0:T(8,128)(2,1)} %param.29), channel_id=1, source_target_pairs={{0,1},{1,0},{2,3},{3,2},{4,5},{5,4},{6,7},{7,6},{8,9},{9,8},{10,11... | collective-permute-start | bytes 27656 | tf_op jit(solution)/shard_map/ppermute | solution.py:842
  323.6 141.8 %collective-permute-start.16 = (bf16[576,512]{1,0:T(8,128)(2,1)}, bf16[576,512]{1,0:T(8,128)(2,1)}, u32[]{:S(2)}, u32[]{:S(2)}) collective-permute-start(bf16[576,512]{1,0:T(8,128)(2,1)} %get-tuple-element.274), channel_id=1, source_target_pairs={{0,1},{1,0},{2,3},{3,2},{4,5},{5,4},{6,7},{7,6},{8,9},{9,8},{10,11... | collective-permute-start | bytes 1769480 | tf_op jit(solution)/shard_map/ppermute | solution.py:106
  325.8 140.9 %collective-permute-start.5 = (bf16[576,512]{1,0:T(8,128)(2,1)}, bf16[576,512]{1,0:T(8,128)(2,1)}, u32[]{:S(2)}, u32[]{:S(2)}) collective-permute-start(bf16[576,512]{1,0:T(8,128)(2,1)} %get-tuple-element.276), channel_id=1, source_target_pairs={{0,1},{1,0},{2,3},{3,2},{4,5},{5,4},{6,7},{7,6},{8,9},{9,8},{10,11... | collective-permute-start | bytes 1769480 | tf_op jit(solution)/shard_map/ppermute | solution.py:106
  456.4 99.2 %collective-permute-start.14 = (bf16[1,48,36864]{2,1,0:T(8,128)(2,1)}, bf16[1,48,36864]{2,1,0:T(8,128)(2,1)}, u32[]{:S(2)}, u32[]{:S(2)}) collective-permute-start(bf16[1,48,36864]{2,1,0:T(8,128)(2,1)} %get-tuple-element.87), channel_id=1, source_target_pairs={{0,1},{1,0},{2,3},{3,2},{4,5},{5,4},{6,7},{7,6},{8,9},{9,8},{10,11... | collective-permute-start | bytes 10616840 | tf_op jit(solution)/shard_map/ppermute | solution.py:950
  519.0 95.2 %collective-permute-start.17 = (bf16[48,36864]{1,0:T(8,128)(2,1)}, bf16[48,36864]{1,0:T(8,128)(2,1)}, u32[]{:S(2)}, u32[]{:S(2)}) collective-permute-start(bf16[48,36864]{1,0:T(8,128)(2,1)} %get-tuple-element.245), channel_id=1, source_target_pairs={{0,1},{1,0},{2,3},{3,2},{4,5},{5,4},{6,7},{7,6},{8,9},{9,8},{10,11... | collective-permute-start | bytes 10616840 | tf_op jit(solution)/shard_map/ppermute | solution.py:106
  614.2 768.5 %reduce-scatter.10.cloned.1.call-start = ((), (), s32[]{:S(2)}) async-start(), calls=%async_computation.7 | async-start | bytes 5849088 | tf_op jit(solution)/shard_map/reduce_scatter | solution.py:206
  655.6 69.7 %collective-permute-start.18 = (bf16[2,576,1024]{2,1,0:T(8,128)(2,1)}, bf16[2,576,1024]{2,1,0:T(8,128)(2,1)}, u32[]{:S(2)}, u32[]{:S(2)}) collective-permute-start(bf16[2,576,1024]{2,1,0:T(8,128)(2,1)} %get-tuple-element.97), channel_id=1, source_target_pairs={{0,2},{2,4},{4,6},{6,8},{8,10},{10,12},{12,14},{14,16},{16,18},{18... | collective-permute-start | bytes 7077896 | tf_op jit(solution)/shard_map/ppermute | solution.py:974
  699.4 132.6 %collective-permute-start.15 = (bf16[24,24,512]{2,1,0:T(8,128)(2,1)}, bf16[24,24,512]{2,1,0:T(8,128)(2,1)}, u32[]{:S(2)}, u32[]{:S(2)}) collective-permute-start(bf16[24,24,512]{2,1,0:T(8,128)(2,1)} %constant_dynamic-slice_fusion.11), channel_id=1, source_target_pairs={{0,1},{1,0},{2,3},{3,2},{4,5},{5,4},{6,7},{7,6},{8,9},{9,8},{10,11... | collective-permute-start | bytes 1769480 | tf_op jit(solution)/shard_map/ppermute | solution.py:1095
  747.3 54.5 %collective-permute-start.21 = (bf16[1,24,1024]{1,2,0:T(8,128)(2,1)}, bf16[1,24,1024]{1,2,0:T(8,128)(2,1)}, u32[]{:S(2)}, u32[]{:S(2)}) collective-permute-start(bf16[1,24,1024]{1,2,0:T(8,128)(2,1)} %get-tuple-element.267), channel_id=1, source_target_pairs={{0,2},{2,4},{4,6},{6,8},{8,10},{10,12},{12,14},{14,16},{16,18},{18... | collective-permute-start | bytes 147464 | tf_op jit(solution)/shard_map/ppermute | solution.py:41
  827.8 554.9 %reduce-scatter.8.cloned.1.call-start = ((), (), s32[]{:S(2)}) async-start(), calls=%async_computation.6 | async-start | bytes 10584064 | tf_op jit(solution)/shard_map/reduce_scatter | solution.py:206
  849.0 343.8 %collective-permute-start.20 = (bf16[24,24,512]{2,1,0:T(8,128)(2,1)}, bf16[24,24,512]{2,1,0:T(8,128)(2,1)}, u32[]{:S(2)}, u32[]{:S(2)}) collective-permute-start(bf16[24,24,512]{2,1,0:T(8,128)(2,1)} %dynamic-slice_convert_fusion), channel_id=1, source_target_pairs={{0,1},{1,0},{2,3},{3,2},{4,5},{5,4},{6,7},{7,6},{8,9},{9,8},{10,11... | collective-permute-start | bytes 1769480 | tf_op jit(solution)/shard_map/ppermute | solution.py:1095
  930.8 560.6 %reduce-scatter.12.cloned.1.call-start = ((), (), s32[]{:S(2)}) async-start(), calls=%async_computation.8 | async-start | bytes 10027008 | tf_op jit(solution)/shard_map/reduce_scatter | solution.py:206
  934.9 261.0 %collective-permute-start.42 = (bf16[64,4096]{1,0:T(8,128)(2,1)}, bf16[64,4096]{1,0:T(8,128)(2,1)}, u32[]{:S(2)}, u32[]{:S(2)}) collective-permute-start(bf16[64,4096]{1,0:T(8,128)(2,1)} %pad_maximum_fusion.11), channel_id=1, source_target_pairs={{0,1},{1,0},{2,3},{3,2},{4,5},{5,4},{6,7},{7,6},{8,9},{9,8},{10,11... | collective-permute-start | bytes 1572872 | tf_op jit(solution)/shard_map/ppermute | solution.py:248
  1086.9 405.6 %reduce-scatter.14.cloned.1.call-start = ((), (), s32[]{:S(2)}) async-start(), calls=%async_computation.9 | async-start | bytes 10027008 | tf_op jit(solution)/shard_map/reduce_scatter | solution.py:206
  1132.8 53.0 %collective-permute-start.25 = (bf16[1536,768]{1,0:T(8,128)(2,1)}, bf16[1536,768]{1,0:T(8,128)(2,1)S(1)}, u32[]{:S(2)}, u32[]{:S(2)}) collective-permute-start(bf16[1536,768]{1,0:T(8,128)(2,1)} %get-tuple-element.251), channel_id=1, source_target_pairs={{0,1},{1,0},{2,3},{3,2},{4,5},{5,4},{6,7},{7,6},{8,9},{9,8},{10,11... | collective-permute-start | bytes 7077896 | tf_op jit(solution)/shard_map/ppermute | solution.py:1035
  1200.0 60.5 %collective-permute-start.28 = (bf16[1536,768]{1,0:T(8,128)(2,1)}, bf16[1536,768]{1,0:T(8,128)(2,1)}, u32[]{:S(2)}, u32[]{:S(2)}) collective-permute-start(bf16[1536,768]{1,0:T(8,128)(2,1)} %get-tuple-element.250), channel_id=1, source_target_pairs={{0,1},{1,0},{2,3},{3,2},{4,5},{5,4},{6,7},{7,6},{8,9},{9,8},{10,11... | collective-permute-start | bytes 7077896 | tf_op jit(solution)/shard_map/ppermute | solution.py:1035
  1268.9 113.8 %collective-permute-start.29 = (bf16[4,192,1536]{2,1,0:T(8,128)(2,1)}, bf16[4,192,1536]{2,1,0:T(8,128)(2,1)S(1)}, u32[]{:S(2)}, u32[]{:S(2)}) collective-permute-start(bf16[4,192,1536]{2,1,0:T(8,128)(2,1)} %dynamic-slice_bitcast_fusion.4), channel_id=1, source_target_pairs={{0,4},{4,0},{8,12},{12,8},{16,20},{20,16},{24,28},{28,24},{1,5},{5... | collective-permute-start | bytes 7077896 | tf_op jit(solution)/shard_map/ppermute | solution.py:227
  1319.5 100.8 %collective-permute-start.30 = (bf16[1,48,36864]{2,1,0:T(8,128)(2,1)}, bf16[1,48,36864]{2,1,0:T(8,128)(2,1)}, u32[]{:S(2)}, u32[]{:S(2)}) collective-permute-start(bf16[1,48,36864]{2,1,0:T(8,128)(2,1)} %get-tuple-element.124), channel_id=1, source_target_pairs={{0,1},{1,0},{2,3},{3,2},{4,5},{5,4},{6,7},{7,6},{8,9},{9,8},{10,11... | collective-permute-start | bytes 10616840 | tf_op jit(solution)/shard_map/ppermute | solution.py:1081
  (161 other events, 2289.7 us)
Sparse Core Ops, SparseCore 0:
  11.5 269.0 all-gather.4
  284.1 160.3 all-gather.6
  614.3 240.6 reduce-scatter.5
  858.7 91.5 reduce-scatter.9
  954.9 132.6 reduce-scatter.7
  1092.1 144.2 reduce-scatter.11
  1240.5 116.5 reduce-scatter.13

commit v6 on v5

--- a/solution.py
+++ b/solution.py
@@ -252,15 +252,16 @@
     ]
 
 
-def sum_everywhere(flat):
+def pair_sum(values, axis, pairs):
+    low = values.astype(BF)
+    return low.astype(F32) + lax.ppermute(low, axis, pairs).astype(F32)
+
+
+def sum_tiles(values, bits):
     devices = tile_count()
-    if devices & (devices - 1):
-        return lax.psum(flat, TILE)
-    bit = 1
-    while bit < devices:
-        flat = flat + lax.ppermute(flat, TILE, [(i, i ^ bit) for i in range(devices)])
-        bit *= 2
-    return flat
+    for bit in bits:
+        values = pair_sum(values, TILE, [(i, i ^ bit) for i in range(devices)])
+    return values
 
 
 def together(*values):
@@ -927,9 +928,10 @@
     mixed_full = features(mixed_one.astype(BF))
     norm_one, first_pull = jax.vjp(layer_norm, mixed_full.astype(F32), ln1_gain.astype(F32))
     norm_low = norm_one.astype(BF)
-    queries = apply(norm_low, q_w).astype(BF)
     key_rows = apply(norm_low, k_w).astype(BF)
     value_rows = apply(norm_low, v_w).astype(BF)
+    query_in, key_rows, value_rows = together(norm_low, key_rows, value_rows)
+    queries = apply(query_in, q_w).astype(BF)
     around = rim_pair(key_rows, tok_count, 0) + rim_pair(value_rows, tok_count, 0)
     near = row_labels(canvas_ids, row_start, row_count, row_count)
     key_tok = jnp.repeat(near, col_count)
@@ -962,8 +964,7 @@
     second_grad = partial_sums(apply_t(ff_pre_grad, ff_in)).astype(BF)
     back_two, grad_ln2 = second_pull(features(second_grad).astype(F32))
     p_ff = stacked_grads([norm2_low, ff_grad_full], [ff_pre_grad, ff_hidden])
-    grad_two, p_ff, cot_other = together(grad_out + own_slice(back_two), p_ff, cot_other)
-    s_ff = reduce_tiles(p_ff)
+    grad_two, cot_other = together(grad_out + own_slice(back_two), cot_other)
     att_grad_full = features(grad_two.astype(BF))
     att_grad = apply(att_grad_full, out_w).astype(BF)
     query_grad, key_own, value_own, to_before, to_after = attend_back(
@@ -973,6 +974,8 @@
     steps = [(i, i + 1) for i in range(devices - 1)]
     from_before = lax.ppermute(to_after, TILE, steps)
     from_after = lax.ppermute(to_before, TILE, [(j, i) for i, j in steps])
+    p_ff, from_before = together(p_ff, from_before)
+    s_ff = reduce_tiles(p_ff)
     key_grad, value_grad = [
         (own + from_before[i].astype(F32) + from_after[i].astype(F32)).astype(BF)
         for i, own in enumerate((key_own, value_own))
@@ -1016,7 +1019,7 @@
     branch_full = lax.optimization_barrier(features(scaled_grad))
     first = mine == 0
     p_w2 = [matmul_tn(branch_full, act).astype(BF) for act in inner_act]
-    branch_full, *p_w2, s_ff = together(branch_full, *p_w2, s_ff)
+    branch_full, *p_w2 = together(branch_full, *p_w2)
     s_w2 = [reduce_tiles(item) for item in p_w2]
     grad_first = (matmul(branch_full, mlp_out[0]) * inner_slope[0].astype(F32)).astype(BF)
     w1_first = matmul_tn(normed_low, grad_first).astype(BF)
@@ -1024,19 +1027,20 @@
     core_first = core_sum(w1_first)
     grad_second = (matmul(branch_full, mlp_out[1]) * inner_slope[1].astype(F32)).astype(BF)
     w1_second = matmul_tn(normed_low, grad_second).astype(BF)
-    grad_second, w1_second = together(grad_second, w1_second)
+    grad_second, w1_second, s_ff = together(grad_second, w1_second, s_ff)
     core_second = core_sum(w1_second)
     normed_part = matmul_nt(grad_first, mlp_in[0])
     normed_part, core_first, core_second = together(normed_part, core_first, core_second)
     w1_own = jnp.where(first, core_first, core_second)
     w1_sent = jnp.where(first, core_second, core_first)
-    piece = w1_sent.shape[1] // 2
+    piece = w1_sent.shape[1] // (3 * LANES) * LANES
     w1_got = [
         lax.ppermute(item, "mb", SWAP) for item in (w1_sent[:, :piece], w1_sent[:, piece:])
     ]
     normed_grad = partial_sums(normed_part + matmul_nt(grad_second, mlp_in[1])).astype(BF)
+    normed_grad, w1_got[0] = together(normed_grad, w1_got[0])
     back_conv, grad_cn_gain = norm_pull(features(normed_grad).astype(F32))
-    conv_grad, w1_got[0] = together(own_slice(back_conv).astype(BF), w1_got[0])
+    conv_grad = own_slice(back_conv).astype(BF)
     conv_cols = conv_grad.reshape(hi_cols, hi_rows, c_own)
     grad_up, grad_down = rim_pair(conv_cols, RIM, 1)
     if fast:
@@ -1077,10 +1081,15 @@
     flat = jnp.pad(flat, (0, -sizes[-1] % (8 * c_shard))).reshape(-1, c_shard)
     tap_rows = tap_sums.shape[0] // 2
     small = jnp.concatenate([tap_sums, flat])
+    devices = tile_count()
+    bits = [1 << i for i in range(devices.bit_length() - 1)]
+    doubling = devices == 1 << len(bits)
+    small = sum_tiles(small, bits[:1]) if doubling else lax.psum(small, TILE)
     if fast:
         ghi_got = lax.ppermute(ghi_sent, "mb", SWAP)
-        small, ghi_got = together(small, ghi_got)
-    small = sum_everywhere(small)
+        small, ghi_got, *s_w2 = together(small, ghi_got, *s_w2)
+    if doubling:
+        small = sum_tiles(small, bits[1:])
     got = lax.ppermute(small[tap_rows:], "mb", SWAP)
     g_kernel = (small[:tap_rows] + got[:tap_rows])[: cn_kernel.shape[0]]
     flat, got = small[2 * tap_rows :].reshape(-1), got[tap_rows:].reshape(-1)

time: 1530 us -> 1510 us (0.987)
  starting transfers between devices: 192 us -> 128 us
  waiting for transfers between devices: 226 us -> 250 us
  matrix products: 508 us -> 485 us
    ppermute x3, starting transfers between devices: 58.9 us -> 7.22 us  [chip_step(): lax.ppermute(sent, 'chip', [(i, i ^ bit) for i in range(lax.axis_size('ch...]
    ppermute x5, waiting for transfers between devices: 88.3 us -> 112 us  [swap_micro(): return (own, lax.ppermute(sent, 'mb', SWAP))]
    ppermute x4, waiting for transfers between devices: 38.5 us -> 21 us  [pair_sum(): return low.astype(F32) + lax.ppermute(low, axis, pairs).astype(F32)]
    dot_general x22, matrix products: 201 us -> 184 us  [matmul(): return jnp.dot(left, right, preferred_element_type=F32)]
    unnamed x290 -> x304, local copies, waits for them, and re-layouts: 33.2 us -> 45.7 us
  transfers between devices with their start and end apart: 50 -> 50, of which waited for: 12 -> 13; matrix products, arithmetic and copies ran while one was open for 48% -> 48% of each run, Pallas kernels for 21% -> 20%
where the time goes in v6:
time: 1510 us; the launch traced here: 1480 us
  matrix products  485 us (32%)
  Pallas kernels  340 us (23%)
  waiting for transfers between devices  250 us (17%)
  other arithmetic  142 us (9%)
  starting transfers between devices  128 us (8%)
  local copies, waits for them, and re-layouts  122 us (8%)
  between operations  17 us (1%)
    dot_general x22, matrix products, matmul(): return jnp.dot(left, right, preferred_element_type=F32)  184 us
    dot_general x22, matrix products, matmul_nt(): lax.dot_general(left, right, (((1,), (1,)), ((), ())), preferred_element_...  183 us
    pallas_call x2, Pallas kernels, conv_backward(): pl.pallas_call(back_kernel, out_shape=(jax.ShapeDtypeStruct((slots, *x.sh...  120 us
    dot_general x5, matrix products, matmul_tn(): lax.dot_general(left, right, (((0,), (0,)), ((), ())), preferred_element_...  118 us
    ppermute x5, waiting for transfers between devices, swap_micro(): return (own, lax.ppermute(sent, 'mb', SWAP))  112 us
    pallas_call x2, Pallas kernels, conv_forward(): pl.pallas_call(kernel, out_shape=jax.ShapeDtypeStruct((48 * 48, 2 * width...  72.7 us
    all_gather x2, waiting for transfers between devices, gather_all(): full = lax.all_gather(shard, ALL, axis=0)  63.2 us
    unnamed x304, local copies, waits for them, and re-layouts  45.7 us
  transfers between devices with their start and end apart: 50, of which 13 were waited for; matrix products, arithmetic and copies ran while one was open for 48% of the time, Pallas kernels for 20%

profile of v6, /device:TPU:0, one launch (start us, length us, event | category | flops | bytes accessed | tf_op | source)
XLA Modules:
  0.0 1484.3 jit_solution(8521410422201328931)
XLA Ops:
  42.1 36.4 %shard_map.339.into_ref = bf16[2304,1536]{1,0:T(8,128)(2,1)} custom-call(s32[1]{0:T(128)} %bitcast.place_ref, bf16[48,36864]{1,0:T(8,128)(2,1)} %get-tuple-element.258.x_ref.own_ref, bf16[8,36864]{1,0:T(8,128)(2,1)} %get-tuple-element.289.top_ref, bf16[8,36864]{1,0:T(8,128)(2,1)} %get-tuple-element.288.bot_ref, f32[49,768]{1,0:T(8,128)} %convert_element_type.509.taps_ref, ...), custom_call_target="tpu_custom_call" | custom-call | flops 41472000000 | bytes 12000000 | tf_op jit(solution)/shard_map/pallas_call | solution.py:344
  78.4 88.1 %collective-permute-done.3 = bf16[2,8,36864]{2,1,0:T(8,128)(2,1)} collective-permute-done((bf16[2,8,36864]{2,1,0:T(8,128)(2,1)}, bf16[2,8,36864]{2,1,0:T(8,128)(2,1)}, u32[]{:S(2)}, u32[]{:S(2)}) %collective-permute-start.3) | collective-permute-done | bytes 1179680 | tf_op jit(solution)/shard_map/ppermute | solution.py:106
  168.9 36.3 %shard_map.340 = bf16[2304,1536]{1,0:T(8,128)(2,1)} custom-call(s32[1]{0:T(128)S(6)} %sub.45.place_ref, bf16[48,36864]{1,0:T(8,128)(2,1)} %collective-permute-done.x_ref.other_ref, bf16[8,36864]{1,0:T(8,128)(2,1)} %get-tuple-element.291.top_ref, bf16[8,36864]{1,0:T(8,128)(2,1)} %get-tuple-element.290.bot_ref, ...), custom_call_target="tpu_custom_call", output_to_operand_aliasing={{}: (6, {})} | custom-call | flops 41472000000 | bytes 12000000 | tf_op jit(solution)/shard_map/pallas_call | solution.py:344
  217.5 63.2 %all-gather.5.cloned.1.call-done = bf16[3072,7040]{1,0:T(8,128)(2,1)} async-done(((bf16[96,7040]{1,0:T(8,128)(2,1)}), bf16[3072,7040]{1,0:T(8,128)(2,1)}) %all-gather.5.cloned.1.call-update) | async-done | bytes 43253776 | tf_op jit(solution)/shard_map/all_gather | solution.py:201
  286.6 32.6 %multiply_convert_fusion.3 = (bf16[2304,3072]{1,0:T(8,128)(2,1)}, f32[2304,3072]{1,0:T(8,128)}) fusion(bf16[2304,1536]{1,0:T(8,128)(2,1)} %fusion.16, bf16[2,1536,7040]{2,1,0:T(8,128)(2,1)} %bitcast.403), kind=kOutput, calls=%fused_computation.16 | convolution fusion | flops 21778661376 | bytes 58982400 | tf_op jit(solution)/shard_map/dot_general | solution.py:47
  327.2 29.7 %fusion.33 = f32[2304,1536]{1,0:T(8,128)} fusion(bf16[2304,3072]{1,0:T(8,128)(2,1)} %get-tuple-element.86, bf16[2,1536,7040]{2,1,0:T(8,128)(2,1)} %bitcast.404), kind=kOutput, calls=%fused_computation.56 | convolution fusion | flops 21743271936 | bytes 37748736 | tf_op jit(solution)/shard_map/dot_general | solution.py:55
  356.9 31.6 %multiply_convert_fusion.2 = (bf16[2304,3072]{1,0:T(8,128)(2,1)}, f32[2304,3072]{1,0:T(8,128)}) fusion(bf16[2304,1536]{1,0:T(8,128)(2,1)S(1)} %bitcast.378, bf16[2,1536,7040]{2,1,0:T(8,128)(2,1)} %bitcast.405), kind=kOutput, calls=%fused_computation.14 | convolution fusion | flops 21778661376 | bytes 58982400 | tf_op jit(solution)/shard_map/dot_general | solution.py:47
  388.5 30.5 %convolution_add_fusion.1.branch_ref = f32[2304,1536]{1,0:T(8,128)} fusion(f32[2304,1536]{1,0:T(8,128)} %fusion.33, bf16[2304,3072]{1,0:T(8,128)(2,1)} %get-tuple-element.335, bf16[2,1536,7040]{2,1,0:T(8,128)(2,1)} %bitcast.406), kind=kOutput, calls=%fused_computation.30 | convolution fusion | flops 21746810880 | bytes 51904512 | tf_op jit(solution)/shard_map/dot_general | solution.py:55
  514.1 32.5 %shard_map.342 = (bf16[576,1024]{1,0:T(8,128)(2,1)}, f32[8,3,2,192]{3,2,1,0:T(2,128)}) custom-call(s32[3]{0:T(128)} %get-tuple-element.343.first_ref, s32[3]{0:T(128)} %get-tuple-element.342.last_ref, bf16[576,1024]{1,0:T(8,128)(2,1)} %pad_maximum_fusion.8.q_ref, bf16[576,1024]{1,0:T(8,128)(2,1)} %copy-done.119, bf16[576,1024]{1,0:T(8,128)(2,1)} %copy-done.54, ...), custom_call_target="tpu_custom_call" | custom-call | flops 40960000000 | bytes 20000000 | tf_op jit(solution)/shard_map/pallas_call | solution.py:667
  586.1 24.1 %collective-permute-done.17.other_ref.cot_ref = bf16[48,36864]{1,0:T(8,128)(2,1)} collective-permute-done((bf16[48,36864]{1,0:T(8,128)(2,1)}, bf16[48,36864]{1,0:T(8,128)(2,1)}, u32[]{:S(2)}, u32[]{:S(2)}) %collective-permute-start.17) | collective-permute-done | bytes 3538976 | tf_op jit(solution)/shard_map/ppermute | solution.py:106
  615.5 42.4 %shard_map.343 = (bf16[576,1024]{1,0:T(8,128)(2,1)}, f32[576,1024]{1,0:T(8,128)}, f32[576,1024]{1,0:T(8,128)}, bf16[2,576,1024]{2,1,0:T(8,128)(2,1)}, bf16[2,576,1024]{2,1,0:T(8,128)(2,1)}) custom-call(s32[3]{0:T(128)} %get-tuple-element.343.first_ref, s32[3]{0:T(128)} %get-tuple-element.342.last_ref, bf16[576,1024]{1,0:T(8,128)(2,1)} %pad_maximum_fusion.8.q_ref, ...), custom_call_target="tpu_custom_call" | custom-call | flops 56320000000 | bytes 20000000 | tf_op jit(solution)/shard_map/pallas_call | solution.py:755
  671.4 22.3 %shard_map.344 = bf16[1024,8192]{1,0:T(8,128)(2,1)} custom-call(bf16[1024,576]{1,0:T(8,128)(2,1)} %get-tuple-element.275.refs_0_, bf16[1024,576]{1,0:T(8,128)(2,1)} %fusion.210.refs_1_, bf16[576,4096]{1,0:T(8,128)(2,1)} %copy-done.32, bf16[576,4096]{1,0:T(8,128)(2,1)} %get-tuple-element.253.refs_3_), custom_call_target="tpu_custom_call" | custom-call | flops 24159191040 | bytes 16777216 | tf_op jit(solution)/shard_map/pallas_call | solution.py:189
  722.2 28.0 %collective-permute-start.21 = (bf16[1,24,1024]{1,2,0:T(8,128)(2,1)}, bf16[1,24,1024]{1,2,0:T(8,128)(2,1)}, u32[]{:S(2)}, u32[]{:S(2)}) collective-permute-start(bf16[1,24,1024]{1,2,0:T(8,128)(2,1)} %get-tuple-element.276), channel_id=1, source_target_pairs={{0,2},{2,4},{4,6},{6,8},{8,10},{10,12},{12,14},{14,16},{16,18},{18... | collective-permute-start | bytes 147464 | tf_op jit(solution)/shard_map/ppermute | solution.py:41
  823.9 28.5 %collective-permute-start.15 = (bf16[24,24,512]{2,1,0:T(8,128)(2,1)S(1)}, bf16[24,24,512]{2,1,0:T(8,128)(2,1)S(1)}, u32[]{:S(2)}, u32[]{:S(2)}) collective-permute-start(bf16[24,24,512]{2,1,0:T(8,128)(2,1)S(1)} %constant_dynamic-slice_fusion.9), channel_id=1, source_target_pairs={{0,1},{1,0},{2,3},{3,2},{4,5},{5,4},{6,7},{7,6},{8,9},{9,8},{10,11... | collective-permute-start | bytes 1769480 | tf_op jit(solution)/shard_map/ppermute | solution.py:1104
  907.0 28.9 %convolution_convert_fusion.2 = bf16[1536,3072]{1,0:T(8,128)(2,1)} fusion(bf16[2304,1536]{1,0:T(8,128)(2,1)} %get-tuple-element.115, bf16[2304,3072]{1,0:T(8,128)(2,1)} %get-tuple-element.335), kind=kOutput, calls=%fused_computation.40 | convolution fusion | flops 21747990528 | bytes 30670848 | tf_op jit(solution)/shard_map/dot_general | solution.py:51
  935.9 28.9 %convolution_convert_fusion.3 = bf16[1536,3072]{1,0:T(8,128)(2,1)} fusion(bf16[2304,1536]{1,0:T(8,128)(2,1)} %get-tuple-element.115, bf16[2304,3072]{1,0:T(8,128)(2,1)} %get-tuple-element.86), kind=kOutput, calls=%fused_computation.41 | convolution fusion | flops 21747990528 | bytes 30670848 | tf_op jit(solution)/shard_map/dot_general | solution.py:51
  964.7 38.1 %multiply_convert_fusion.1 = bf16[2304,3072]{1,0:T(8,128)(2,1)} fusion(bf16[2304,1536]{1,0:T(8,128)(2,1)} %get-tuple-element.115, f32[2304,3072]{1,0:T(8,128)} %get-tuple-element.334, bf16[2,1536,7040]{2,1,0:T(8,128)(2,1)} %bitcast.415), kind=kOutput, calls=%fused_computation.13 | convolution fusion | flops 21828206592 | bytes 58982400 | tf_op jit(solution)/shard_map/dot_general | solution.py:47
  1002.9 28.7 %convolution_convert_fusion.1 = bf16[1536,3072]{1,0:T(8,128)(2,1)S(1)} fusion(bf16[2304,1536]{1,0:T(8,128)(2,1)} %fusion.16, bf16[2304,3072]{1,0:T(8,128)(2,1)} %multiply_convert_fusion.1), kind=kOutput, calls=%fused_computation.39 | convolution fusion | flops 21747990528 | bytes 30670848 | tf_op jit(solution)/shard_map/dot_general | solution.py:51
  1037.3 36.8 %multiply_convert_fusion = bf16[2304,3072]{1,0:T(8,128)(2,1)S(1)} fusion(bf16[2304,1536]{1,0:T(8,128)(2,1)} %get-tuple-element.115, f32[2304,3072]{1,0:T(8,128)} %get-tuple-element.336, bf16[2,1536,7040]{2,1,0:T(8,128)(2,1)} %bitcast.416), kind=kOutput, calls=%fused_computation.12 | convolution fusion | flops 21828206592 | bytes 58982400 | tf_op jit(solution)/shard_map/dot_general | solution.py:47
  1079.2 25.2 %convolution_convert_fusion = bf16[1536,3072]{1,0:T(8,128)(2,1)} fusion(bf16[2304,1536]{1,0:T(8,128)(2,1)S(1)} %bitcast.380, bf16[2304,3072]{1,0:T(8,128)(2,1)S(1)} %multiply_convert_fusion), kind=kOutput, calls=%fused_computation.38 | convolution fusion | flops 21747990528 | bytes 30670848 | tf_op jit(solution)/shard_map/dot_general | solution.py:51
  1109.7 29.4 %fusion.35 = f32[2304,1536]{1,0:T(8,128)} fusion(bf16[2304,3072]{1,0:T(8,128)(2,1)} %multiply_convert_fusion.1, bf16[2,1536,7040]{2,1,0:T(8,128)(2,1)} %bitcast.417), kind=kOutput, calls=%fused_computation.58 | convolution fusion | flops 21743271936 | bytes 37748736 | tf_op jit(solution)/shard_map/dot_general | solution.py:55
  1158.6 29.8 %fusion.20 = bf16[2304,1536]{1,0:T(8,128)(2,1)} fusion(f32[2304,1536]{1,0:T(8,128)} %fusion.35, bf16[2304,3072]{1,0:T(8,128)(2,1)} %copy-done.122, bf16[2,1536,7040]{2,1,0:T(8,128)(2,1)} %bitcast.418), kind=kOutput, calls=%fused_computation.37 | convolution fusion | flops 21750349824 | bytes 44826624 | tf_op jit(solution)/shard_map/dot_general | solution.py:55
  1238.9 59.9 %shard_map.347 = (bf16[1,48,36864]{2,1,0:T(8,128)(2,1)}, f32[56,768]{1,0:T(8,128)}) custom-call(s32[1]{0:T(128)S(6)} %sub.45.place_ref, bf16[2304,1536]{1,0:T(8,128)(2,1)} %copy-done.22, bf16[48,8,1536]{2,1,0:T(8,128)(2,1)} %collective-permute-done.26.top_ref, bf16[48,8,1536]{2,1,0:T(8,128)(2,1)} %collective-permute-done.27.bot_ref, ...), custom_call_target="tpu_custom_call" | custom-call | flops 69120000000 | bytes 25000000 | tf_op jit(solution)/shard_map/pallas_call | solution.py:450
  1322.8 59.8 %shard_map.348 = (f32[2,48,36864]{2,1,0:T(8,128)}, f32[56,768]{1,0:T(8,128)}) custom-call(s32[1]{0:T(128)} %bitcast.place_ref, bf16[2304,1536]{1,0:T(8,128)(2,1)} %copy-done.22, bf16[48,8,1536]{2,1,0:T(8,128)(2,1)} %collective-permute-done.26.top_ref, bf16[48,8,1536]{2,1,0:T(8,128)(2,1)} %collective-permute-done.27.bot_ref, ...), custom_call_target="tpu_custom_call" | custom-call | flops 69120000000 | bytes 25000000 | tf_op jit(solution)/shard_map/pallas_call | solution.py:450
  (638 shorter events, 575.5 us)
Async XLA Ops:
  7.2 273.4 %all-gather.5.cloned.1.call-start = ((), (), s32[]{:S(2)}) async-start(), calls=%async_computation.10 | async-start | bytes 44605440 | tf_op jit(solution)/shard_map/all_gather | solution.py:201
  9.8 460.8 %all-gather.7.cloned.1.call-start = ((), (), s32[]{:S(2)}) async-start(), calls=%async_computation.11 | async-start | bytes 27574272 | tf_op jit(solution)/shard_map/all_gather | solution.py:201
  27.6 141.3 %collective-permute-start = (bf16[48,36864]{1,0:T(8,128)(2,1)S(1)}, bf16[48,36864]{1,0:T(8,128)(2,1)}, u32[]{:S(2)}, u32[]{:S(2)}) collective-permute-start(bf16[48,36864]{1,0:T(8,128)(2,1)S(1)} %get-tuple-element.259), channel_id=1, source_target_pairs={{0,1},{1,0},{2,3},{3,2},{4,5},{5,4},{6,7},{7,6},{8,9},{9,8},{10,11... | collective-permute-start | bytes 10616840 | tf_op jit(solution)/shard_map/ppermute | solution.py:106
  38.2 128.4 %collective-permute-start.3 = (bf16[2,8,36864]{2,1,0:T(8,128)(2,1)}, bf16[2,8,36864]{2,1,0:T(8,128)(2,1)}, u32[]{:S(2)}, u32[]{:S(2)}) collective-permute-start(bf16[2,8,36864]{2,1,0:T(8,128)(2,1)} %get-tuple-element.268), channel_id=1, source_target_pairs={{0,1},{1,0},{2,3},{3,2},{4,5},{5,4},{6,7},{7,6},{8,9},{9,8},{10,11... | collective-permute-start | bytes 3538952 | tf_op jit(solution)/shard_map/ppermute | solution.py:106
  281.7 822.7 %reduce-scatter.6.cloned.1.call-start = ((), (), s32[]{:S(2)}) async-start(), calls=%async_computation.5 | async-start | bytes 17825792 | tf_op jit(solution)/shard_map/reduce_scatter | solution.py:206
  319.2 99.8 %collective-permute-start.6 = (bf16[768]{0:T(1024)(128)(2,1)}, bf16[768]{0:T(1024)(128)(2,1)}, u32[]{:S(2)}, u32[]{:S(2)}) collective-permute-start(bf16[768]{0:T(1024)(128)(2,1)} %param.27), channel_id=1, source_target_pairs={{0,1},{1,0},{2,3},{3,2},{4,5},{5,4},{6,7},{7,6},{8,9},{9,8},{10,11... | collective-permute-start | bytes 4616 | tf_op jit(solution)/shard_map/ppermute | solution.py:843
  319.6 137.0 %collective-permute-start.7 = (bf16[9,512]{1,0:T(8,128)(2,1)}, bf16[9,512]{1,0:T(8,128)(2,1)}, u32[]{:S(2)}, u32[]{:S(2)}) collective-permute-start(bf16[9,512]{1,0:T(8,128)(2,1)} %param.29), channel_id=1, source_target_pairs={{0,1},{1,0},{2,3},{3,2},{4,5},{5,4},{6,7},{7,6},{8,9},{9,8},{10,11... | collective-permute-start | bytes 27656 | tf_op jit(solution)/shard_map/ppermute | solution.py:843
  323.2 142.4 %collective-permute-start.16 = (bf16[576,512]{1,0:T(8,128)(2,1)}, bf16[576,512]{1,0:T(8,128)(2,1)}, u32[]{:S(2)}, u32[]{:S(2)}) collective-permute-start(bf16[576,512]{1,0:T(8,128)(2,1)} %get-tuple-element.283), channel_id=1, source_target_pairs={{0,1},{1,0},{2,3},{3,2},{4,5},{5,4},{6,7},{7,6},{8,9},{9,8},{10,11... | collective-permute-start | bytes 1769480 | tf_op jit(solution)/shard_map/ppermute | solution.py:106
  325.6 141.5 %collective-permute-start.5 = (bf16[576,512]{1,0:T(8,128)(2,1)}, bf16[576,512]{1,0:T(8,128)(2,1)}, u32[]{:S(2)}, u32[]{:S(2)}) collective-permute-start(bf16[576,512]{1,0:T(8,128)(2,1)} %get-tuple-element.285), channel_id=1, source_target_pairs={{0,1},{1,0},{2,3},{3,2},{4,5},{5,4},{6,7},{7,6},{8,9},{9,8},{10,11... | collective-permute-start | bytes 1769480 | tf_op jit(solution)/shard_map/ppermute | solution.py:106
  456.5 95.1 %collective-permute-start.14 = (bf16[1,48,36864]{2,1,0:T(8,128)(2,1)}, bf16[1,48,36864]{2,1,0:T(8,128)(2,1)}, u32[]{:S(2)}, u32[]{:S(2)}) collective-permute-start(bf16[1,48,36864]{2,1,0:T(8,128)(2,1)} %get-tuple-element.96), channel_id=1, source_target_pairs={{0,1},{1,0},{2,3},{3,2},{4,5},{5,4},{6,7},{7,6},{8,9},{9,8},{10,11... | collective-permute-start | bytes 10616840 | tf_op jit(solution)/shard_map/ppermute | solution.py:952
  509.4 100.9 %collective-permute-start.17 = (bf16[48,36864]{1,0:T(8,128)(2,1)}, bf16[48,36864]{1,0:T(8,128)(2,1)}, u32[]{:S(2)}, u32[]{:S(2)}) collective-permute-start(bf16[48,36864]{1,0:T(8,128)(2,1)} %get-tuple-element.257), channel_id=1, source_target_pairs={{0,1},{1,0},{2,3},{3,2},{4,5},{5,4},{6,7},{7,6},{8,9},{9,8},{10,11... | collective-permute-start | bytes 10616840 | tf_op jit(solution)/shard_map/ppermute | solution.py:106
  693.8 689.8 %reduce-scatter.10.cloned.1.call-start = ((), (), s32[]{:S(2)}) async-start(), calls=%async_computation.7 | async-start | bytes 5849088 | tf_op jit(solution)/shard_map/reduce_scatter | solution.py:206
  722.2 62.3 %collective-permute-start.21 = (bf16[1,24,1024]{1,2,0:T(8,128)(2,1)}, bf16[1,24,1024]{1,2,0:T(8,128)(2,1)}, u32[]{:S(2)}, u32[]{:S(2)}) collective-permute-start(bf16[1,24,1024]{1,2,0:T(8,128)(2,1)} %get-tuple-element.276), channel_id=1, source_target_pairs={{0,2},{2,4},{4,6},{6,8},{8,10},{10,12},{12,14},{14,16},{16,18},{18... | collective-permute-start | bytes 147464 | tf_op jit(solution)/shard_map/ppermute | solution.py:41
  810.5 573.1 %reduce-scatter.8.cloned.1.call-start = ((), (), s32[]{:S(2)}) async-start(), calls=%async_computation.6 | async-start | bytes 10584064 | tf_op jit(solution)/shard_map/reduce_scatter | solution.py:206
  823.9 42.4 %collective-permute-start.15 = (bf16[24,24,512]{2,1,0:T(8,128)(2,1)S(1)}, bf16[24,24,512]{2,1,0:T(8,128)(2,1)S(1)}, u32[]{:S(2)}, u32[]{:S(2)}) collective-permute-start(bf16[24,24,512]{2,1,0:T(8,128)(2,1)S(1)} %constant_dynamic-slice_fusion.9), channel_id=1, source_target_pairs={{0,1},{1,0},{2,3},{3,2},{4,5},{5,4},{6,7},{7,6},{8,9},{9,8},{10,11... | collective-permute-start | bytes 1769480 | tf_op jit(solution)/shard_map/ppermute | solution.py:1104
  852.4 568.7 %reduce-scatter.12.cloned.1.call-start = ((), (), s32[]{:S(2)}) async-start(), calls=%async_computation.8 | async-start | bytes 10027008 | tf_op jit(solution)/shard_map/reduce_scatter | solution.py:206
  883.5 346.5 %collective-permute-start.20 = (bf16[24,24,512]{2,1,0:T(8,128)(2,1)}, bf16[24,24,512]{2,1,0:T(8,128)(2,1)}, u32[]{:S(2)}, u32[]{:S(2)}) collective-permute-start(bf16[24,24,512]{2,1,0:T(8,128)(2,1)} %dynamic-slice_convert_fusion), channel_id=1, source_target_pairs={{0,1},{1,0},{2,3},{3,2},{4,5},{5,4},{6,7},{7,6},{8,9},{9,8},{10,11... | collective-permute-start | bytes 1769480 | tf_op jit(solution)/shard_map/ppermute | solution.py:1104
  1002.9 418.3 %reduce-scatter.14.cloned.1.call-start = ((), (), s32[]{:S(2)}) async-start(), calls=%async_computation.9 | async-start | bytes 10027008 | tf_op jit(solution)/shard_map/reduce_scatter | solution.py:206
  1037.3 102.7 %collective-permute-start.23 = (bf16[1536,1536]{1,0:T(8,128)(2,1)}, bf16[1536,1536]{1,0:T(8,128)(2,1)}, u32[]{:S(2)}, u32[]{:S(2)}) collective-permute-start(bf16[1536,1536]{1,0:T(8,128)(2,1)} %constant_dynamic-slice_fusion.7), channel_id=1, source_target_pairs={{0,2},{2,0},{1,3},{3,1},{4,6},{6,4},{5,7},{7,5},{8,10},{10,8},{9,1... | collective-permute-start | bytes 14155784 | tf_op jit(solution)/shard_map/ppermute | solution.py:214
  1109.2 37.7 %collective-permute-start.24 = (bf16[1536,1536]{1,0:T(8,128)(2,1)}, bf16[1536,1536]{1,0:T(8,128)(2,1)}, u32[]{:S(2)}, u32[]{:S(2)}) collective-permute-start(bf16[1536,1536]{1,0:T(8,128)(2,1)} %constant_dynamic-slice_fusion.6), channel_id=1, source_target_pairs={{0,2},{2,0},{1,3},{3,1},{4,6},{6,4},{5,7},{7,5},{8,10},{10,8},{9,1... | collective-permute-start | bytes 14155784 | tf_op jit(solution)/shard_map/ppermute | solution.py:214
  1146.4 86.8 %collective-permute-start.42 = (bf16[64,4096]{1,0:T(8,128)(2,1)}, bf16[64,4096]{1,0:T(8,128)(2,1)}, u32[]{:S(2)}, u32[]{:S(2)}) collective-permute-start(bf16[64,4096]{1,0:T(8,128)(2,1)} %pad_maximum_fusion.11), channel_id=1, source_target_pairs={{0,1},{1,0},{2,3},{3,2},{4,5},{5,4},{6,7},{7,6},{8,9},{9,8},{10,11... | collective-permute-start | bytes 1572872 | tf_op jit(solution)/shard_map/ppermute | solution.py:248
  1237.6 69.6 %collective-permute-start.28 = (bf16[1536,1024]{1,0:T(8,128)(2,1)}, bf16[1536,1024]{1,0:T(8,128)(2,1)S(1)}, u32[]{:S(2)}, u32[]{:S(2)}) collective-permute-start(bf16[1536,1024]{1,0:T(8,128)(2,1)} %slice.680), channel_id=1, source_target_pairs={{0,1},{1,0},{2,3},{3,2},{4,5},{5,4},{6,7},{7,6},{8,9},{9,8},{10,11... | collective-permute-start | bytes 9437192 | tf_op jit(solution)/shard_map/ppermute | solution.py:1038
  1315.1 68.6 %collective-permute-start.29 = (bf16[4,192,1536]{2,1,0:T(8,128)(2,1)}, bf16[4,192,1536]{2,1,0:T(8,128)(2,1)S(1)}, u32[]{:S(2)}, u32[]{:S(2)}) collective-permute-start(bf16[4,192,1536]{2,1,0:T(8,128)(2,1)} %dynamic-slice_bitcast_fusion.4), channel_id=1, source_target_pairs={{0,4},{4,0},{8,12},{12,8},{16,20},{20,16},{24,28},{28,24},{1,5},{5... | collective-permute-start | bytes 7077896 | tf_op jit(solution)/shard_map/ppermute | solution.py:227
  1322.0 99.1 %collective-permute-start.31 = (bf16[1,48,36864]{2,1,0:T(8,128)(2,1)}, bf16[1,48,36864]{2,1,0:T(8,128)(2,1)}, u32[]{:S(2)}, u32[]{:S(2)}) collective-permute-start(bf16[1,48,36864]{2,1,0:T(8,128)(2,1)} %get-tuple-element.134), channel_id=1, source_target_pairs={{0,1},{1,0},{2,3},{3,2},{4,5},{5,4},{6,7},{7,6},{8,9},{9,8},{10,11... | collective-permute-start | bytes 10616840 | tf_op jit(solution)/shard_map/ppermute | solution.py:1089
  (168 other events, 2257.1 us)
Sparse Core Ops, SparseCore 0:
  11.5 269.0 all-gather.4
  284.1 160.3 all-gather.6
  693.9 208.5 reduce-scatter.5
  906.2 79.0 reduce-scatter.9
  989.9 117.3 reduce-scatter.7
  1111.8 110.8 reduce-scatter.11
  1226.8 121.2 reduce-scatter.13

commit v7 on v6

--- a/solution.py
+++ b/solution.py
@@ -974,7 +974,7 @@
     steps = [(i, i + 1) for i in range(devices - 1)]
     from_before = lax.ppermute(to_after, TILE, steps)
     from_after = lax.ppermute(to_before, TILE, [(j, i) for i, j in steps])
-    p_ff, from_before = together(p_ff, from_before)
+    p_ff, lo_result, from_before, from_after = together(p_ff, lo_result, from_before, from_after)
     s_ff = reduce_tiles(p_ff)
     key_grad, value_grad = [
         (own + from_before[i].astype(F32) + from_after[i].astype(F32)).astype(BF)
@@ -1084,12 +1084,12 @@
     devices = tile_count()
     bits = [1 << i for i in range(devices.bit_length() - 1)]
     doubling = devices == 1 << len(bits)
-    small = sum_tiles(small, bits[:1]) if doubling else lax.psum(small, TILE)
+    small = sum_tiles(small, bits[:-1]) if doubling else lax.psum(small, TILE)
     if fast:
         ghi_got = lax.ppermute(ghi_sent, "mb", SWAP)
         small, ghi_got, *s_w2 = together(small, ghi_got, *s_w2)
     if doubling:
-        small = sum_tiles(small, bits[1:])
+        small = sum_tiles(small, bits[-1:])
     got = lax.ppermute(small[tap_rows:], "mb", SWAP)
     g_kernel = (small[:tap_rows] + got[:tap_rows])[: cn_kernel.shape[0]]
     flat, got = small[2 * tap_rows :].reshape(-1), got[tap_rows:].reshape(-1)

time: 1510 us -> 1500 us (level); the launches traced: 1480 us -> 1500 us
    ppermute x2, starting transfers between devices: 30.8 us -> 2.03 us  [leave(): other = lax.ppermute(sent.astype(BF), 'mb', SWAP)]
    ppermute x3, starting transfers between devices: 7.22 us -> 23.3 us  [chip_step(): lax.ppermute(sent, 'chip', [(i, i ^ bit) for i in range(lax.axis_size('ch...]
    ppermute x4, waiting for transfers between devices: 21 us -> 36.5 us  [pair_sum(): return low.astype(F32) + lax.ppermute(low, axis, pairs).astype(F32)]
    unnamed x304 -> x300, local copies, waits for them, and re-layouts: 45.7 us -> 42.2 us
  transfers between devices with their start and end apart: 50 -> 50, of which waited for: 13 -> 12; matrix products, arithmetic and copies ran while one was open for 48% -> 49% of each run, Pallas kernels for 20% -> 20%
where the time goes in v7:
time: 1500 us
  matrix products  488 us (33%)
  Pallas kernels  339 us (23%)
  waiting for transfers between devices  250 us (17%)
  other arithmetic  151 us (10%)
  local copies, waits for them, and re-layouts  130 us (9%)
  starting transfers between devices  124 us (8%)
  between operations  16.8 us (1%)
    dot_general x22, matrix products, matmul_nt(): lax.dot_general(left, right, (((1,), (1,)), ((), ())), preferred_element_...  186 us
    dot_general x22, matrix products, matmul(): return jnp.dot(left, right, preferred_element_type=F32)  185 us
    pallas_call x2, Pallas kernels, conv_backward(): pl.pallas_call(back_kernel, out_shape=(jax.ShapeDtypeStruct((slots, *x.sh...  119 us
    dot_general x5, matrix products, matmul_tn(): lax.dot_general(left, right, (((0,), (0,)), ((), ())), preferred_element_...  117 us
    ppermute x5, waiting for transfers between devices, swap_micro(): return (own, lax.ppermute(sent, 'mb', SWAP))  111 us
    pallas_call x2, Pallas kernels, conv_forward(): pl.pallas_call(kernel, out_shape=jax.ShapeDtypeStruct((48 * 48, 2 * width...  72.7 us
    all_gather x2, waiting for transfers between devices, gather_all(): full = lax.all_gather(shard, ALL, axis=0)  63.2 us
    pallas_call x1, Pallas kernels, attend_back(): pl.pallas_call(attend_back_kernel, out_shape=(jax.ShapeDtypeStruct(q.shap...  42.8 us
  transfers between devices with their start and end apart: 50, of which 12 were waited for; matrix products, arithmetic and copies ran while one was open for 49% of the time, Pallas kernels for 20%

profile of v7, /device:TPU:0, one launch (start us, length us, event | category | flops | bytes accessed | tf_op | source)
XLA Modules:
  0.0 1498.5 jit_solution(14149195085279649500)
XLA Ops:
  42.0 36.4 %shard_map.339.into_ref = bf16[2304,1536]{1,0:T(8,128)(2,1)} custom-call(s32[1]{0:T(128)} %bitcast.place_ref, bf16[48,36864]{1,0:T(8,128)(2,1)} %get-tuple-element.262.x_ref.own_ref, bf16[8,36864]{1,0:T(8,128)(2,1)} %get-tuple-element.294.top_ref, bf16[8,36864]{1,0:T(8,128)(2,1)} %get-tuple-element.293.bot_ref, f32[49,768]{1,0:T(8,128)} %convert_element_type.509.taps_ref, ...), custom_call_target="tpu_custom_call" | custom-call | flops 41472000000 | bytes 12000000 | tf_op jit(solution)/shard_map/pallas_call | solution.py:344
  78.4 88.2 %collective-permute-done.3 = bf16[2,8,36864]{2,1,0:T(8,128)(2,1)} collective-permute-done((bf16[2,8,36864]{2,1,0:T(8,128)(2,1)}, bf16[2,8,36864]{2,1,0:T(8,128)(2,1)}, u32[]{:S(2)}, u32[]{:S(2)}) %collective-permute-start.3) | collective-permute-done | bytes 1179680 | tf_op jit(solution)/shard_map/ppermute | solution.py:106
  168.9 36.3 %shard_map.340 = bf16[2304,1536]{1,0:T(8,128)(2,1)} custom-call(s32[1]{0:T(128)S(6)} %sub.45.place_ref, bf16[48,36864]{1,0:T(8,128)(2,1)} %collective-permute-done.x_ref.other_ref, bf16[8,36864]{1,0:T(8,128)(2,1)} %get-tuple-element.296.top_ref, bf16[8,36864]{1,0:T(8,128)(2,1)} %get-tuple-element.295.bot_ref, ...), custom_call_target="tpu_custom_call", output_to_operand_aliasing={{}: (6, {})} | custom-call | flops 41472000000 | bytes 12000000 | tf_op jit(solution)/shard_map/pallas_call | solution.py:344
  217.4 63.2 %all-gather.5.cloned.1.call-done = bf16[3072,7040]{1,0:T(8,128)(2,1)} async-done(((bf16[96,7040]{1,0:T(8,128)(2,1)}), bf16[3072,7040]{1,0:T(8,128)(2,1)}) %all-gather.5.cloned.1.call-update) | async-done | bytes 43253776 | tf_op jit(solution)/shard_map/all_gather | solution.py:201
  286.9 32.7 %multiply_convert_fusion.3 = (bf16[2304,3072]{1,0:T(8,128)(2,1)}, f32[2304,3072]{1,0:T(8,128)}) fusion(bf16[2304,1536]{1,0:T(8,128)(2,1)} %fusion.16, bf16[2,1536,7040]{2,1,0:T(8,128)(2,1)} %bitcast.397), kind=kOutput, calls=%fused_computation.16 | convolution fusion | flops 21778661376 | bytes 58982400 | tf_op jit(solution)/shard_map/dot_general | solution.py:47
  327.6 29.6 %fusion.33 = f32[2304,1536]{1,0:T(8,128)} fusion(bf16[2304,3072]{1,0:T(8,128)(2,1)} %get-tuple-element.88, bf16[2,1536,7040]{2,1,0:T(8,128)(2,1)} %bitcast.398), kind=kOutput, calls=%fused_computation.56 | convolution fusion | flops 21743271936 | bytes 37748736 | tf_op jit(solution)/shard_map/dot_general | solution.py:55
  357.2 31.4 %multiply_convert_fusion.2 = (bf16[2304,3072]{1,0:T(8,128)(2,1)}, f32[2304,3072]{1,0:T(8,128)}) fusion(bf16[2304,1536]{1,0:T(8,128)(2,1)S(1)} %bitcast.374, bf16[2,1536,7040]{2,1,0:T(8,128)(2,1)} %bitcast.399), kind=kOutput, calls=%fused_computation.14 | convolution fusion | flops 21778661376 | bytes 58982400 | tf_op jit(solution)/shard_map/dot_general | solution.py:47
  388.7 30.5 %convolution_add_fusion.1.branch_ref = f32[2304,1536]{1,0:T(8,128)} fusion(f32[2304,1536]{1,0:T(8,128)} %fusion.33, bf16[2304,3072]{1,0:T(8,128)(2,1)} %get-tuple-element.340, bf16[2,1536,7040]{2,1,0:T(8,128)(2,1)} %bitcast.400), kind=kOutput, calls=%fused_computation.30 | convolution fusion | flops 21746810880 | bytes 51904512 | tf_op jit(solution)/shard_map/dot_general | solution.py:55
  517.1 32.5 %shard_map.342 = (bf16[576,1024]{1,0:T(8,128)(2,1)}, f32[8,3,2,192]{3,2,1,0:T(2,128)}) custom-call(s32[3]{0:T(128)} %get-tuple-element.348.first_ref, s32[3]{0:T(128)} %get-tuple-element.347.last_ref, bf16[576,1024]{1,0:T(8,128)(2,1)} %pad_maximum_fusion.8.q_ref, bf16[576,1024]{1,0:T(8,128)(2,1)} %copy-done.119, bf16[576,1024]{1,0:T(8,128)(2,1)} %copy-done.56, ...), custom_call_target="tpu_custom_call" | custom-call | flops 40960000000 | bytes 20000000 | tf_op jit(solution)/shard_map/pallas_call | solution.py:667
  588.3 22.6 %collective-permute-done.16.other_ref.cot_ref = bf16[48,36864]{1,0:T(8,128)(2,1)} collective-permute-done((bf16[48,36864]{1,0:T(8,128)(2,1)}, bf16[48,36864]{1,0:T(8,128)(2,1)}, u32[]{:S(2)}, u32[]{:S(2)}) %collective-permute-start.16) | collective-permute-done | bytes 3538976 | tf_op jit(solution)/shard_map/ppermute | solution.py:106
  623.4 42.8 %shard_map.344 = (bf16[576,1024]{1,0:T(8,128)(2,1)}, f32[576,1024]{1,0:T(8,128)}, f32[576,1024]{1,0:T(8,128)}, bf16[2,576,1024]{2,1,0:T(8,128)(2,1)}, bf16[2,576,1024]{2,1,0:T(8,128)(2,1)}) custom-call(s32[3]{0:T(128)} %get-tuple-element.348.first_ref, s32[3]{0:T(128)} %get-tuple-element.347.last_ref, bf16[576,1024]{1,0:T(8,128)(2,1)} %pad_maximum_fusion.8.q_ref, ...), custom_call_target="tpu_custom_call" | custom-call | flops 56320000000 | bytes 20000000 | tf_op jit(solution)/shard_map/pallas_call | solution.py:755
  666.1 26.8 %collective-permute-start.17 = (bf16[2,576,1024]{2,1,0:T(8,128)(2,1)}, bf16[2,576,1024]{2,1,0:T(8,128)(2,1)}, u32[]{:S(2)}, u32[]{:S(2)}) collective-permute-start(bf16[2,576,1024]{2,1,0:T(8,128)(2,1)} %get-tuple-element.104), channel_id=1, source_target_pairs={{0,2},{2,4},{4,6},{6,8},{8,10},{10,12},{12,14},{14,16},{16,18},{18... | collective-permute-start | bytes 7077896 | tf_op jit(solution)/shard_map/ppermute | solution.py:975
  702.5 22.4 %shard_map.343 = bf16[1024,8192]{1,0:T(8,128)(2,1)} custom-call(bf16[1024,576]{1,0:T(8,128)(2,1)} %get-tuple-element.280.refs_0_, bf16[1024,576]{1,0:T(8,128)(2,1)} %fusion.210.refs_1_, bf16[576,4096]{1,0:T(8,128)(2,1)} %copy-done.32, bf16[576,4096]{1,0:T(8,128)(2,1)} %copy-done.31), custom_call_target="tpu_custom_call" | custom-call | flops 24159191040 | bytes 16777216 | tf_op jit(solution)/shard_map/pallas_call | solution.py:189
  878.8 28.7 %convolution_convert_fusion.2 = bf16[1536,3072]{1,0:T(8,128)(2,1)} fusion(bf16[2304,1536]{1,0:T(8,128)(2,1)} %get-tuple-element.119, bf16[2304,3072]{1,0:T(8,128)(2,1)} %get-tuple-element.340), kind=kOutput, calls=%fused_computation.40 | convolution fusion | flops 21747990528 | bytes 30670848 | tf_op jit(solution)/shard_map/dot_general | solution.py:51
  907.5 29.2 %convolution_convert_fusion.3 = bf16[1536,3072]{1,0:T(8,128)(2,1)} fusion(bf16[2304,1536]{1,0:T(8,128)(2,1)} %get-tuple-element.119, bf16[2304,3072]{1,0:T(8,128)(2,1)} %get-tuple-element.88), kind=kOutput, calls=%fused_computation.41 | convolution fusion | flops 21747990528 | bytes 30670848 | tf_op jit(solution)/shard_map/dot_general | solution.py:51
  936.7 38.9 %multiply_convert_fusion.1 = bf16[2304,3072]{1,0:T(8,128)(2,1)} fusion(bf16[2304,1536]{1,0:T(8,128)(2,1)} %get-tuple-element.119, f32[2304,3072]{1,0:T(8,128)} %get-tuple-element.339, bf16[2,1536,7040]{2,1,0:T(8,128)(2,1)} %bitcast.409), kind=kOutput, calls=%fused_computation.13 | convolution fusion | flops 21828206592 | bytes 58982400 | tf_op jit(solution)/shard_map/dot_general | solution.py:47
  975.7 27.7 %convolution_convert_fusion.1 = bf16[1536,3072]{1,0:T(8,128)(2,1)S(1)} fusion(bf16[2304,1536]{1,0:T(8,128)(2,1)} %fusion.16, bf16[2304,3072]{1,0:T(8,128)(2,1)} %multiply_convert_fusion.1), kind=kOutput, calls=%fused_computation.39 | convolution fusion | flops 21747990528 | bytes 30670848 | tf_op jit(solution)/shard_map/dot_general | solution.py:51
  1010.6 36.8 %multiply_convert_fusion = bf16[2304,3072]{1,0:T(8,128)(2,1)S(1)} fusion(bf16[2304,1536]{1,0:T(8,128)(2,1)} %get-tuple-element.119, f32[2304,3072]{1,0:T(8,128)} %get-tuple-element.341, bf16[2,1536,7040]{2,1,0:T(8,128)(2,1)} %bitcast.410), kind=kOutput, calls=%fused_computation.12 | convolution fusion | flops 21828206592 | bytes 58982400 | tf_op jit(solution)/shard_map/dot_general | solution.py:47
  1053.0 25.0 %convolution_convert_fusion = bf16[1536,3072]{1,0:T(8,128)(2,1)} fusion(bf16[2304,1536]{1,0:T(8,128)(2,1)S(1)} %bitcast.376, bf16[2304,3072]{1,0:T(8,128)(2,1)S(1)} %multiply_convert_fusion), kind=kOutput, calls=%fused_computation.38 | convolution fusion | flops 21747990528 | bytes 30670848 | tf_op jit(solution)/shard_map/dot_general | solution.py:51
  1082.9 29.4 %fusion.35 = f32[2304,1536]{1,0:T(8,128)} fusion(bf16[2304,3072]{1,0:T(8,128)(2,1)} %multiply_convert_fusion.1, bf16[2,1536,7040]{2,1,0:T(8,128)(2,1)} %bitcast.411), kind=kOutput, calls=%fused_computation.58 | convolution fusion | flops 21743271936 | bytes 37748736 | tf_op jit(solution)/shard_map/dot_general | solution.py:55
  1135.0 29.8 %fusion.20 = bf16[2304,1536]{1,0:T(8,128)(2,1)} fusion(f32[2304,1536]{1,0:T(8,128)} %fusion.35, bf16[2304,3072]{1,0:T(8,128)(2,1)} %copy-done.122, bf16[2,1536,7040]{2,1,0:T(8,128)(2,1)} %bitcast.412), kind=kOutput, calls=%fused_computation.37 | convolution fusion | flops 21750349824 | bytes 44826624 | tf_op jit(solution)/shard_map/dot_general | solution.py:55
  1212.2 59.0 %shard_map.347 = (bf16[1,48,36864]{2,1,0:T(8,128)(2,1)}, f32[56,768]{1,0:T(8,128)}) custom-call(s32[1]{0:T(128)S(6)} %sub.45.place_ref, bf16[2304,1536]{1,0:T(8,128)(2,1)} %copy-done.23, bf16[48,8,1536]{2,1,0:T(8,128)(2,1)} %collective-permute-done.26.top_ref, bf16[48,8,1536]{2,1,0:T(8,128)(2,1)} %collective-permute-done.27.bot_ref, ...), custom_call_target="tpu_custom_call" | custom-call | flops 69120000000 | bytes 25000000 | tf_op jit(solution)/shard_map/pallas_call | solution.py:450
  1313.0 59.9 %shard_map.348 = (f32[2,48,36864]{2,1,0:T(8,128)}, f32[56,768]{1,0:T(8,128)}) custom-call(s32[1]{0:T(128)} %bitcast.place_ref, bf16[2304,1536]{1,0:T(8,128)(2,1)} %copy-done.23, bf16[48,8,1536]{2,1,0:T(8,128)(2,1)} %collective-permute-done.26.top_ref, bf16[48,8,1536]{2,1,0:T(8,128)(2,1)} %collective-permute-done.27.bot_ref, ...), custom_call_target="tpu_custom_call" | custom-call | flops 69120000000 | bytes 25000000 | tf_op jit(solution)/shard_map/pallas_call | solution.py:450
  1406.4 21.2 %collective-permute-done.32 = bf16[136,768]{1,0:T(8,128)(2,1)S(1)} collective-permute-done((bf16[136,768]{1,0:T(8,128)(2,1)S(1)}, bf16[136,768]{1,0:T(8,128)(2,1)S(1)}, u32[]{:S(2)}, u32[]{:S(2)}) %collective-permute-start.32) | collective-permute-done | bytes 208928 | tf_op jit(solution)/shard_map/ppermute | solution.py:257
  (633 shorter events, 600.9 us)
Async XLA Ops:
  7.2 273.4 %all-gather.5.cloned.1.call-start = ((), (), s32[]{:S(2)}) async-start(), calls=%async_computation.10 | async-start | bytes 44605440 | tf_op jit(solution)/shard_map/all_gather | solution.py:201
  9.8 463.7 %all-gather.7.cloned.1.call-start = ((), (), s32[]{:S(2)}) async-start(), calls=%async_computation.11 | async-start | bytes 27574272 | tf_op jit(solution)/shard_map/all_gather | solution.py:201
  27.6 141.3 %collective-permute-start = (bf16[48,36864]{1,0:T(8,128)(2,1)S(1)}, bf16[48,36864]{1,0:T(8,128)(2,1)}, u32[]{:S(2)}, u32[]{:S(2)}) collective-permute-start(bf16[48,36864]{1,0:T(8,128)(2,1)S(1)} %get-tuple-element.263), channel_id=1, source_target_pairs={{0,1},{1,0},{2,3},{3,2},{4,5},{5,4},{6,7},{7,6},{8,9},{9,8},{10,11... | collective-permute-start | bytes 10616840 | tf_op jit(solution)/shard_map/ppermute | solution.py:106
  38.2 128.4 %collective-permute-start.3 = (bf16[2,8,36864]{2,1,0:T(8,128)(2,1)}, bf16[2,8,36864]{2,1,0:T(8,128)(2,1)}, u32[]{:S(2)}, u32[]{:S(2)}) collective-permute-start(bf16[2,8,36864]{2,1,0:T(8,128)(2,1)} %get-tuple-element.272), channel_id=1, source_target_pairs={{0,1},{1,0},{2,3},{3,2},{4,5},{5,4},{6,7},{7,6},{8,9},{9,8},{10,11... | collective-permute-start | bytes 3538952 | tf_op jit(solution)/shard_map/ppermute | solution.py:106
  281.7 796.3 %reduce-scatter.6.cloned.1.call-start = ((), (), s32[]{:S(2)}) async-start(), calls=%async_computation.5 | async-start | bytes 17825792 | tf_op jit(solution)/shard_map/reduce_scatter | solution.py:206
  319.6 99.5 %collective-permute-start.6 = (bf16[768]{0:T(1024)(128)(2,1)}, bf16[768]{0:T(1024)(128)(2,1)}, u32[]{:S(2)}, u32[]{:S(2)}) collective-permute-start(bf16[768]{0:T(1024)(128)(2,1)} %param.27), channel_id=1, source_target_pairs={{0,1},{1,0},{2,3},{3,2},{4,5},{5,4},{6,7},{7,6},{8,9},{9,8},{10,11... | collective-permute-start | bytes 4616 | tf_op jit(solution)/shard_map/ppermute | solution.py:843
  319.9 136.8 %collective-permute-start.7 = (bf16[9,512]{1,0:T(8,128)(2,1)}, bf16[9,512]{1,0:T(8,128)(2,1)}, u32[]{:S(2)}, u32[]{:S(2)}) collective-permute-start(bf16[9,512]{1,0:T(8,128)(2,1)} %param.29), channel_id=1, source_target_pairs={{0,1},{1,0},{2,3},{3,2},{4,5},{5,4},{6,7},{7,6},{8,9},{9,8},{10,11... | collective-permute-start | bytes 27656 | tf_op jit(solution)/shard_map/ppermute | solution.py:843
  323.6 141.6 %collective-permute-start.15 = (bf16[576,512]{1,0:T(8,128)(2,1)}, bf16[576,512]{1,0:T(8,128)(2,1)}, u32[]{:S(2)}, u32[]{:S(2)}) collective-permute-start(bf16[576,512]{1,0:T(8,128)(2,1)} %get-tuple-element.288), channel_id=1, source_target_pairs={{0,1},{1,0},{2,3},{3,2},{4,5},{5,4},{6,7},{7,6},{8,9},{9,8},{10,11... | collective-permute-start | bytes 1769480 | tf_op jit(solution)/shard_map/ppermute | solution.py:106
  325.9 141.6 %collective-permute-start.5 = (bf16[576,512]{1,0:T(8,128)(2,1)}, bf16[576,512]{1,0:T(8,128)(2,1)}, u32[]{:S(2)}, u32[]{:S(2)}) collective-permute-start(bf16[576,512]{1,0:T(8,128)(2,1)} %get-tuple-element.290), channel_id=1, source_target_pairs={{0,1},{1,0},{2,3},{3,2},{4,5},{5,4},{6,7},{7,6},{8,9},{9,8},{10,11... | collective-permute-start | bytes 1769480 | tf_op jit(solution)/shard_map/ppermute | solution.py:106
  456.7 98.2 %collective-permute-start.14 = (bf16[1,48,36864]{2,1,0:T(8,128)(2,1)}, bf16[1,48,36864]{2,1,0:T(8,128)(2,1)}, u32[]{:S(2)}, u32[]{:S(2)}) collective-permute-start(bf16[1,48,36864]{2,1,0:T(8,128)(2,1)} %get-tuple-element.98), channel_id=1, source_target_pairs={{0,1},{1,0},{2,3},{3,2},{4,5},{5,4},{6,7},{7,6},{8,9},{9,8},{10,11... | collective-permute-start | bytes 10616840 | tf_op jit(solution)/shard_map/ppermute | solution.py:952
  512.4 98.5 %collective-permute-start.16 = (bf16[48,36864]{1,0:T(8,128)(2,1)}, bf16[48,36864]{1,0:T(8,128)(2,1)}, u32[]{:S(2)}, u32[]{:S(2)}) collective-permute-start(bf16[48,36864]{1,0:T(8,128)(2,1)} %get-tuple-element.261), channel_id=1, source_target_pairs={{0,1},{1,0},{2,3},{3,2},{4,5},{5,4},{6,7},{7,6},{8,9},{9,8},{10,11... | collective-permute-start | bytes 10616840 | tf_op jit(solution)/shard_map/ppermute | solution.py:106
  666.1 58.8 %collective-permute-start.17 = (bf16[2,576,1024]{2,1,0:T(8,128)(2,1)}, bf16[2,576,1024]{2,1,0:T(8,128)(2,1)}, u32[]{:S(2)}, u32[]{:S(2)}) collective-permute-start(bf16[2,576,1024]{2,1,0:T(8,128)(2,1)} %get-tuple-element.104), channel_id=1, source_target_pairs={{0,2},{2,4},{4,6},{6,8},{8,10},{10,12},{12,14},{14,16},{16,18},{18... | collective-permute-start | bytes 7077896 | tf_op jit(solution)/shard_map/ppermute | solution.py:975
  725.0 648.8 %reduce-scatter.10.cloned.1.call-start = ((), (), s32[]{:S(2)}) async-start(), calls=%async_computation.7 | async-start | bytes 5849088 | tf_op jit(solution)/shard_map/reduce_scatter | solution.py:206
  831.4 542.5 %reduce-scatter.8.cloned.1.call-start = ((), (), s32[]{:S(2)}) async-start(), calls=%async_computation.6 | async-start | bytes 10584064 | tf_op jit(solution)/shard_map/reduce_scatter | solution.py:206
  832.0 598.8 %reduce-scatter.12.cloned.1.call-start = ((), (), s32[]{:S(2)}) async-start(), calls=%async_computation.8 | async-start | bytes 10027008 | tf_op jit(solution)/shard_map/reduce_scatter | solution.py:206
  842.8 272.0 %collective-permute-start.19 = (bf16[24,24,512]{2,1,0:T(8,128)(2,1)}, bf16[24,24,512]{2,1,0:T(8,128)(2,1)}, u32[]{:S(2)}, u32[]{:S(2)}) collective-permute-start(bf16[24,24,512]{2,1,0:T(8,128)(2,1)} %constant_dynamic-slice_fusion.8), channel_id=1, source_target_pairs={{0,1},{1,0},{2,3},{3,2},{4,5},{5,4},{6,7},{7,6},{8,9},{9,8},{10,11... | collective-permute-start | bytes 1769480 | tf_op jit(solution)/shard_map/ppermute | solution.py:1104
  855.4 349.7 %collective-permute-start.20 = (bf16[24,24,512]{2,1,0:T(8,128)(2,1)}, bf16[24,24,512]{2,1,0:T(8,128)(2,1)}, u32[]{:S(2)}, u32[]{:S(2)}) collective-permute-start(bf16[24,24,512]{2,1,0:T(8,128)(2,1)} %dynamic-slice_convert_fusion), channel_id=1, source_target_pairs={{0,1},{1,0},{2,3},{3,2},{4,5},{5,4},{6,7},{7,6},{8,9},{9,8},{10,11... | collective-permute-start | bytes 1769480 | tf_op jit(solution)/shard_map/ppermute | solution.py:1104
  975.7 455.1 %reduce-scatter.14.cloned.1.call-start = ((), (), s32[]{:S(2)}) async-start(), calls=%async_computation.9 | async-start | bytes 10027008 | tf_op jit(solution)/shard_map/reduce_scatter | solution.py:206
  1009.1 108.8 %collective-permute-start.23 = (bf16[1536,1536]{1,0:T(8,128)(2,1)}, bf16[1536,1536]{1,0:T(8,128)(2,1)}, u32[]{:S(2)}, u32[]{:S(2)}) collective-permute-start(bf16[1536,1536]{1,0:T(8,128)(2,1)} %constant_dynamic-slice_fusion.7), channel_id=1, source_target_pairs={{0,2},{2,0},{1,3},{3,1},{4,6},{6,4},{5,7},{7,5},{8,10},{10,8},{9,1... | collective-permute-start | bytes 14155784 | tf_op jit(solution)/shard_map/ppermute | solution.py:214
  1124.4 83.9 %collective-permute-start.42 = (bf16[64,4096]{1,0:T(8,128)(2,1)}, bf16[64,4096]{1,0:T(8,128)(2,1)}, u32[]{:S(2)}, u32[]{:S(2)}) collective-permute-start(bf16[64,4096]{1,0:T(8,128)(2,1)} %pad_maximum_fusion.11), channel_id=1, source_target_pairs={{0,1},{1,0},{2,3},{3,2},{4,5},{5,4},{6,7},{7,6},{8,9},{9,8},{10,11... | collective-permute-start | bytes 1572872 | tf_op jit(solution)/shard_map/ppermute | solution.py:248
  1210.9 71.1 %collective-permute-start.28 = (bf16[1536,1024]{1,0:T(8,128)(2,1)S(1)}, bf16[1536,1024]{1,0:T(8,128)(2,1)}, u32[]{:S(2)}, u32[]{:S(2)}) collective-permute-start(bf16[1536,1024]{1,0:T(8,128)(2,1)S(1)} %slice.678), channel_id=1, source_target_pairs={{0,1},{1,0},{2,3},{3,2},{4,5},{5,4},{6,7},{7,6},{8,9},{9,8},{10,11... | collective-permute-start | bytes 9437192 | tf_op jit(solution)/shard_map/ppermute | solution.py:1038
  1291.5 94.6 %collective-permute-start.29 = (bf16[4,192,1536]{2,1,0:T(8,128)(2,1)}, bf16[4,192,1536]{2,1,0:T(8,128)(2,1)S(1)}, u32[]{:S(2)}, u32[]{:S(2)}) collective-permute-start(bf16[4,192,1536]{2,1,0:T(8,128)(2,1)} %dynamic-slice_bitcast_fusion.4), channel_id=1, source_target_pairs={{0,4},{4,0},{8,12},{12,8},{16,20},{20,16},{24,28},{28,24},{1,5},{5... | collective-permute-start | bytes 7077896 | tf_op jit(solution)/shard_map/ppermute | solution.py:227
  1311.6 119.2 %collective-permute-start.33 = (bf16[1,48,36864]{2,1,0:T(8,128)(2,1)}, bf16[1,48,36864]{2,1,0:T(8,128)(2,1)}, u32[]{:S(2)}, u32[]{:S(2)}) collective-permute-start(bf16[1,48,36864]{2,1,0:T(8,128)(2,1)} %get-tuple-element.138), channel_id=1, source_target_pairs={{0,1},{1,0},{2,3},{3,2},{4,5},{5,4},{6,7},{7,6},{8,9},{9,8},{10,11... | collective-permute-start | bytes 10616840 | tf_op jit(solution)/shard_map/ppermute | solution.py:1089
  1428.9 58.4 %collective-permute-start.35 = (bf16[1,192,1536]{2,1,0:T(8,128)(2,1)}, bf16[1,192,1536]{2,1,0:T(8,128)(2,1)}, u32[]{:S(2)}, u32[]{:S(2)}) collective-permute-start(bf16[1,192,1536]{2,1,0:T(8,128)(2,1)} %constant_dynamic-slice_fusion.5), channel_id=1, source_target_pairs={{0,16},{4,20},{8,24},{12,28},{16,0},{20,4},{24,8},{28,12},{1,17},{... | collective-permute-start | bytes 1769480 | tf_op jit(solution)/shard_map/ppermute | solution.py:227
  (166 other events, 2401.3 us)
Sparse Core Ops, SparseCore 0:
  11.5 269.0 all-gather.4
  284.1 160.3 all-gather.6
  725.1 201.3 reduce-scatter.5
  930.3 79.0 reduce-scatter.9
  1014.0 119.0 reduce-scatter.7
  1137.5 128.2 reduce-scatter.11
  1270.0 128.6 reduce-scatter.13
